TPU v7x, 128 devices: a whole 4x4x4 slice. The times are simulated.
128 devices in a mesh: dp: 16 (over x, y), tensor: 8 (over z, core).
Axes of the slice: x: 4, y: 4, z: 4, core: 2. Of those that a mesh axis runs over, the one named last changes fastest.
Arguments:
- queries: bfloat16 [16384, 8192], P('dp', 'tensor'), may hold values from -6 to 6
- key_rows: bfloat16 [16384, 1024], P('dp', 'tensor'), may hold values from -6 to 6
- value_rows: bfloat16 [16384, 1024], P('dp', 'tensor'), may hold values from -6 to 6
- out_grad: bfloat16 [16384, 8192], P('dp', 'tensor'), may hold values from -24 to 24
- prefix: float32 [2, 64, 1024], P(None, None, 'tensor'), may hold values from -6 to 6
- lengths: int32 [32], P('dp'), may hold values from 1 to 512, as said below
- qkv_weight: bfloat16 [8192, 10240], P('dp', 'tensor'), may hold values from -0.0625 to 0.0625
Outputs:
- input_grad: bfloat16 [16384, 8192], P('dp', 'tensor')
- new_prefix: float32 [2, 64, 1024], P(None, None, 'tensor')
Inputs may be any that keep to these rules, and one draw needn't show every extreme that they name: `lengths`: the longest prompt has exactly 512 live tokens.
All inputs are finite; a program needn't handle non-finite values.
Results may differ from a plain program's by a relative error of at most 0.019.
Values may be sent and summed in bfloat16 or wider, within the bound.
No kernel may reach another device: no remote copies, remote signals or barrier semaphores. Data moves between devices by JAX's collectives and lax.ppermute only.
A program may use at most 192 MiB of HBM per device.

v0:
```python
import math

import jax
import jax.numpy as jnp
from jax import lax
from jax.sharding import PartitionSpec as P

HD = 128
KVH = 8
QH = 64
PREFIX = 64
SEQ = 512


rope_base = 500000.0
learning_rate = 0.1


def unrotate(gradient, positions):
    half_dim = gradient.shape[-1] // 2
    frequency = jnp.power(
        rope_base, -(2.0 * jnp.arange(half_dim).astype(jnp.float32)) / gradient.shape[-1]
    )
    angles = positions.astype(jnp.float32)[:, None] * frequency[None, :]
    broadcast_shape = (gradient.shape[0],) + (1,) * (gradient.ndim - 2) + (half_dim,)
    cosine = jnp.cos(angles).reshape(broadcast_shape)
    sine_part = jnp.sin(angles).reshape(broadcast_shape)
    lower_half = gradient[..., :half_dim]
    upper_half = gradient[..., half_dim:]
    return jnp.concatenate(
        [
            lower_half * cosine + upper_half * sine_part,
            upper_half * cosine - lower_half * sine_part,
        ],
        -1,
    )


def attend_block(query_block, key_block, value_block, grad_block, prefix_keys, prefix_values):
    block_len = query_block.shape[0]
    prefix_len = prefix_keys.shape[0]
    inverse = 1.0 / math.sqrt(query_block.shape[-1])
    joined_keys = jnp.concatenate([prefix_keys, key_block], 0)
    joined_values = jnp.concatenate([prefix_values, value_block], 0)
    scores = (
        jnp.einsum("igrd,jgd->grij", query_block, joined_keys, preferred_element_type=jnp.float32)
        * inverse
    )
    row_index = lax.broadcasted_iota(jnp.int32, (block_len, prefix_len + block_len), 0)
    col_index = lax.broadcasted_iota(jnp.int32, (block_len, prefix_len + block_len), 1)
    visible = col_index <= row_index + prefix_len
    scores = jnp.where(visible, scores, -1e30)
    largest = jnp.max(scores, -1, keepdims=True)
    powers = jnp.exp(scores - largest)
    attn_probs = powers / jnp.sum(powers, -1, keepdims=True)
    dprobs = jnp.einsum(
        "igrd,jgd->grij", grad_block, joined_values, preferred_element_type=jnp.float32
    )
    row_term = jnp.sum(attn_probs * dprobs, -1, keepdims=True)
    dscores = (attn_probs * (dprobs - row_term)).astype(jnp.bfloat16)
    rounded = attn_probs.astype(jnp.bfloat16)
    query_grad = (
        jnp.einsum("grij,jgd->igrd", dscores, joined_keys, preferred_element_type=jnp.float32)
        * inverse
    )
    key_grad = (
        jnp.einsum("grij,igrd->jgd", dscores, query_block, preferred_element_type=jnp.float32)
        * inverse
    )
    value_grad = jnp.einsum(
        "grij,igrd->jgd", rounded, grad_block, preferred_element_type=jnp.float32
    )
    return (
        query_grad,
        key_grad[prefix_len:],
        value_grad[prefix_len:],
        key_grad[:prefix_len],
        value_grad[:prefix_len],
    )


def body(queries, key_rows, value_rows, out_grad, prefix, lengths, qkv_weight):
    live_count = lax.psum(jnp.sum(lengths), "dp")
    tok_rows = queries.shape[0]
    prompt_count = lengths.shape[0]
    group_size = QH // KVH
    kv_width = key_rows.shape[1]
    kv_heads = kv_width // HD
    prefix_keys = prefix[0].reshape(PREFIX, kv_heads, HD).astype(jnp.bfloat16)
    prefix_values = prefix[1].reshape(PREFIX, kv_heads, HD).astype(jnp.bfloat16)
    positions = jnp.arange(SEQ)

    def prompt_grads(prompt_data):
        query_part, key_part, value_part, grad_part, prompt_len = prompt_data
        live_rows = (positions < prompt_len)[:, None]
        grad_part = jnp.where(live_rows, grad_part, jnp.zeros_like(grad_part))
        operands = (
            query_part.reshape(SEQ, kv_heads, group_size, HD),
            key_part.reshape(SEQ, kv_heads, HD),
            value_part.reshape(SEQ, kv_heads, HD),
            grad_part.reshape(SEQ, kv_heads, group_size, HD),
        )
        result = attend_block(
            operands[0], operands[1], operands[2], operands[3], prefix_keys, prefix_values
        )
        query_grad, key_grad, value_grad, prefix_kgrad, prefix_vgrad = result
        query_grad = unrotate(query_grad, positions)
        key_grad = unrotate(key_grad, positions)
        grads = jnp.concatenate([query_grad, key_grad[:, :, None], value_grad[:, :, None]], 2)
        grads = grads.astype(jnp.bfloat16).reshape(SEQ, kv_heads * (group_size + 2) * HD)
        prefix_terms = jnp.stack(
            [prefix_kgrad.reshape(PREFIX, kv_width), prefix_vgrad.reshape(PREFIX, kv_width)], 0
        )
        return (grads, prefix_terms)

    local_grads, prefix_terms = lax.map(
        prompt_grads,
        (
            queries.reshape(prompt_count, SEQ, -1),
            key_rows.reshape(prompt_count, SEQ, -1),
            value_rows.reshape(prompt_count, SEQ, -1),
            out_grad.reshape(prompt_count, SEQ, -1),
            lengths,
        ),
    )
    local_grads = local_grads.reshape(tok_rows, -1)
    prefix_grad = jnp.sum(prefix_terms, 0)
    loss_scale = jnp.float32(tok_rows * lax.axis_size("dp")) / live_count.astype(jnp.float32)
    head_terms = lax.dot_general(
        local_grads,
        lax.all_gather(qkv_weight, "dp", axis=0, tiled=True),
        (((1,), (1,)), ((), ())),
        preferred_element_type=jnp.float32,
    )
    summed = lax.psum_scatter(
        head_terms.astype(jnp.bfloat16), "tensor", scatter_dimension=1, tiled=True
    ).astype(jnp.float32)
    input_grad = (summed * loss_scale).astype(jnp.bfloat16)
    owned_grad = lax.psum_scatter(
        prefix_grad.astype(jnp.bfloat16), "dp", scatter_dimension=1, tiled=True
    ).astype(jnp.float32)
    share_rows = owned_grad.shape[1]
    own_rows = lax.dynamic_slice_in_dim(prefix, lax.axis_index("dp") * share_rows, share_rows, 1)
    updated = own_rows - learning_rate * loss_scale * owned_grad
    new_prefix = lax.all_gather(updated, "dp", axis=1, tiled=True)
    return (input_grad, new_prefix)


def solution(mesh):
    placed = (
        P("dp", "tensor"),
        P("dp", "tensor"),
        P("dp", "tensor"),
        P("dp", "tensor"),
        P(None, None, "tensor"),
        P("dp"),
        P("dp", "tensor"),
    )
    return jax.shard_map(
        body,
        mesh=mesh,
        in_specs=placed,
        out_specs=(P("dp", "tensor"), P(None, None, "tensor")),
        check_vma=False,
    )
```

profile of v0, /device:TPU:2, one launch (start us, length us, event | category | flops | bytes accessed | tf_op | source)
XLA Modules:
  0.0 296.5 jit_solution(3340721724111906847)
XLA Ops:
  7.2 0.7 all-gather.2.cloned.1.call-update
  8.0 0.8 convert.24
  8.8 67.8 %while.15 = (s32[]{:T(128)}, bf16[2,512,1280]{2,1,0:T(8,128)(2,1)}, f32[2,2,64,128]{2,3,1,0:T(8,128)}, bf16[2,512,128]{2,1,0:T(8,128)(2,1)}, bf16[64,1,128]{2,0,...) while((s32[]{:T(128)}, bf16[2,512,1280]{2,1,0:T(8,128)(2,1)}, ...), condition=%wide.region_4.5_spmd.clone.clone, body=%wide.region_0.4_spmd.clone.clone.sunk | while | flops 3089643264 | bytes 181515440 | solution.py:116
  8.8 1.7 constant_dynamic-slice_fusion.3
  10.5 0.5 copy.69
  11.1 1.6 dynamic-slice_bitcast_fusion.3
  12.7 0.2 iota_compare_fusion.4
  12.9 1.7 fusion.73
  14.6 3.6 %copy-done = f32[576,512,8]{1,0,2:T(8,128)} copy-done((f32[576,512,8]{1,0,2:T(8,128)}, f32[576,512,8]{1,0,2:T(8,128)S(1)}, u32[]{:S(2)}) %copy-start) | copy-done | bytes 9437208 | tf_op jit(solution)/shard_map/while
  18.2 2.0 fusion.74
  20.2 0.5 copy.70
  20.8 0.6 dynamic_slice.47
  21.4 0.6 iota_compare_fusion.5
  22.0 6.5 %fusion.77 = (f32[8,512]{1,0:T(8,128)S(1)}, f32[576,512,8]{1,0,2:T(8,128)S(1)}) fusion(f32[8,512]{1,0:T(8,128)S(1)} %fusion.74, f32[8,512]{1,0:T(8,128)S(1)} %get-tuple-element.337, f32[576,512,8]{1,0,2:T(8,128)} %copy-done, pred[512,576]{0,1:T(8,128)(4,1)S(1)} %iota_compare_fusion.4, bf16[512,8,128]{0,2,1:T(8,128)(2,1)S(1)} %bitcast.184, ...), kind=kOutput, calls=%fused_computation.5.clone.1 | convolution fusion | flops 618426368 | bytes 20414464 | tf_op jit(solution)/shard_map/while/body/eval_jaxpr/igrd,jgd->grij/dot_general | solution.py:56
  28.6 0.7 slice-done.1
  29.2 0.2 slice-done.2
  29.5 3.0 %fusion.78 = bf16[8,512,576]{1,2,0:T(8,128)(2,1)S(1)} fusion(f32[576,512,8]{1,0,2:T(8,128)S(1)} %get-tuple-element.340, f32[8,512]{1,0:T(8,128)S(1)} %get-tuple-element.341, f32[8,512]{1,0:T(8,128)S(1)} %fusion.74, f32[8,512]{1,0:T(8,128)S(1)} %get-tuple-element.337, f32[576,512,8]{1,0,2:T(8,128)S(1)} %bitcast.179, ...), kind=kLoop, calls=%fused_computation.12.clone.1 | loop fusion | flops 16515072 | bytes 23937024 | tf_op jit(solution)/shard_map/reshape.156
  32.5 1.7 fusion.79
  34.2 2.8 fusion.75
  37.1 0.7 copy-done.4
  37.8 1.0 multiply_bitcast_fusion.2
  38.9 0.5 multiply_cosine_fusion.3
  39.4 0.4 add_convert_fusion.2
  39.8 0.6 fusion.80
  40.4 0.1 fusion.76
  40.5 0.1 pad_maximum_fusion.2
  40.6 0.6 copy.71
  41.2 1.2 constant_dynamic-update-slice_fusion.2
  42.3 1.8 constant_dynamic-slice_fusion.3
  44.1 0.5 copy.69
  44.7 1.6 dynamic-slice_bitcast_fusion.3
  46.3 0.2 iota_compare_fusion.4
  46.5 1.7 fusion.73
  48.2 3.6 %copy-done = f32[576,512,8]{1,0,2:T(8,128)} copy-done((f32[576,512,8]{1,0,2:T(8,128)}, f32[576,512,8]{1,0,2:T(8,128)S(1)}, u32[]{:S(2)}) %copy-start) | copy-done | bytes 9437208 | tf_op jit(solution)/shard_map/while
  51.8 2.0 fusion.74
  53.8 0.5 copy.70
  54.3 0.6 dynamic_slice.47
  54.9 0.6 iota_compare_fusion.5
  55.6 7.3 %fusion.77 = (f32[8,512]{1,0:T(8,128)S(1)}, f32[576,512,8]{1,0,2:T(8,128)S(1)}) fusion(f32[8,512]{1,0:T(8,128)S(1)} %fusion.74, f32[8,512]{1,0:T(8,128)S(1)} %get-tuple-element.337, f32[576,512,8]{1,0,2:T(8,128)} %copy-done, pred[512,576]{0,1:T(8,128)(4,1)S(1)} %iota_compare_fusion.4, bf16[512,8,128]{0,2,1:T(8,128)(2,1)S(1)} %bitcast.184, ...), kind=kOutput, calls=%fused_computation.5.clone.1 | convolution fusion | flops 618426368 | bytes 20414464 | tf_op jit(solution)/shard_map/while/body/eval_jaxpr/igrd,jgd->grij/dot_general | solution.py:56
  62.9 0.6 slice-done.1
  63.5 0.2 slice-done.2
  63.8 3.0 %fusion.78 = bf16[8,512,576]{1,2,0:T(8,128)(2,1)S(1)} fusion(f32[576,512,8]{1,0,2:T(8,128)S(1)} %get-tuple-element.340, f32[8,512]{1,0:T(8,128)S(1)} %get-tuple-element.341, f32[8,512]{1,0:T(8,128)S(1)} %fusion.74, f32[8,512]{1,0:T(8,128)S(1)} %get-tuple-element.337, f32[576,512,8]{1,0,2:T(8,128)S(1)} %bitcast.179, ...), kind=kLoop, calls=%fused_computation.12.clone.1 | loop fusion | flops 16515072 | bytes 23937024 | tf_op jit(solution)/shard_map/reshape.156
  66.7 1.7 fusion.79
  68.5 2.8 fusion.75
  71.4 0.7 copy-done.4
  72.1 1.0 multiply_bitcast_fusion.2
  73.1 0.5 multiply_cosine_fusion.3
  73.7 0.4 add_convert_fusion.2
  74.0 0.6 fusion.80
  74.6 0.1 fusion.76
  74.8 0.6 copy.71
  75.5 1.1 constant_dynamic-update-slice_fusion.2
  76.6 68.6 %all-gather.2.cloned.1.call-done = bf16[8192,1280]{1,0:T(8,128)(2,1)} async-done(((bf16[512,1280]{1,0:T(8,128)(2,1)}), bf16[8192,1280]{1,0:T(8,128)(2,1)}) %all-gather.2.cloned.1.call-update) | async-done | bytes 20971536 | tf_op jit(solution)/shard_map/all_gather | solution.py:131
  145.2 27.9 %convolution_convert_fusion = bf16[1024,8192]{1,0:T(8,128)(2,1)} fusion(bf16[1024,1280]{1,0:T(8,128)(2,1)} %bitcast.191, bf16[8192,1280]{1,0:T(8,128)(2,1)} %all-gather.2.cloned.1.call-done), kind=kOutput, calls=%fused_computation.69 | convolution fusion | flops 21483225088 | bytes 40370176 | tf_op jit(solution)/shard_map/dot_general | solution.py:129
  173.1 0.6 copy-done.7
  173.7 0.6 reduce_sum.36
  174.3 14.1 %psum.7 = s32[]{:T(128)} all-reduce(s32[]{:T(128)} %reduce_sum.36), channel_id=1, replica_groups=mesh['dp'=16,'tensor'=8] {'dp'}, use_global_device_ids=true, to_apply=%region_7.8 | all-reduce | flops 1 | bytes 8 | tf_op jit(solution)/shard_map/psum | solution.py:83
  188.5 0.1 copy.49
  189.3 0.6 dynamic-slice
  190.5 67.2 %all-reduce = bf16[2,64,128]{2,1,0:T(8,128)(2,1)S(1)} all-reduce(bf16[2,64,128]{2,1,0:T(8,128)(2,1)S(1)} %copy.49), channel_id=3, replica_groups=mesh['dp'=16,'tensor'=8] {'dp'}, use_global_device_ids=true, to_apply=%region_9.10.clone | all-reduce | flops 16384 | bytes 65536
  257.8 0.7 multiply_subtract_fusion
  258.5 27.2 %all_gather.7 = f32[2,64,128]{2,0,1:T(2,128)S(1)} all-gather(f32[2,4,128]{2,0,1:T(2,128)S(1)} %copy.50), channel_id=1, replica_groups=mesh['dp'=16,'tensor'=8] {'dp'}, dimensions={1}, use_global_device_ids=true | all-gather | bytes 69632 | tf_op jit(solution)/shard_map/all_gather | solution.py:145
  285.6 0.6 copy.51
  286.3 3.4 %multiply_convert_fusion = bf16[1024,1024]{1,0:T(8,128)(2,1)} fusion(bf16[1024,1024]{1,0:T(8,128)(2,1)} %reduce-scatter.3.cloned.1.call-done, f32[]{:T(128)S(6)} %div.31), kind=kLoop, calls=%fused_computation.70 | loop fusion | flops 3145728 | bytes 4194308 | tf_op jit(solution)/shard_map/convert_element_type | solution.py:138
  (61 shorter events, 0.6 us)
Async XLA Ops:
  7.2 138.0 %all-gather.2.cloned.1.call-start = ((), (), s32[]{:S(2)}) async-start(), calls=%async_computation.1 | async-start | bytes 22282240 | tf_op jit(solution)/shard_map/all_gather | solution.py:131
  7.9 278.4 %reduce-scatter.3.cloned.1.call-start = ((), (), s32[]{:S(2)}) async-start(), calls=%async_computation.2 | async-start | bytes 18874368 | tf_op jit(solution)/shard_map/reduce_scatter | solution.py:135
  12.7 7.5 %copy-start.1 = (bf16[512,1,128]{2,0,1:T(8,128)(2,1)}, bf16[512,1,128]{2,0,1:T(8,128)(2,1)S(1)}, u32[]{:S(2)}) copy-start(bf16[512,1,128]{2,0,1:T(8,128)(2,1)S(1)} %get-tuple-element.335) | copy-start | bytes 393220 | tf_op jit(solution)/shard_map/while
  12.9 7.8 %copy-start.6 = (s32[2]{0:T(128)S(1)}, s32[2]{0:T(128)}, u32[]{:S(2)}) copy-start(s32[2]{0:T(128)} %get-tuple-element.378) | copy-start | bytes 28 | tf_op jit(solution)/shard_map/while
  14.6 3.6 %copy-start = (f32[576,512,8]{1,0,2:T(8,128)}, f32[576,512,8]{1,0,2:T(8,128)S(1)}, u32[]{:S(2)}) copy-start(f32[576,512,8]{1,0,2:T(8,128)S(1)} %get-tuple-element.336) | copy-start | bytes 28311556 | tf_op jit(solution)/shard_map/while
  21.9 6.6 %slice-start = ((s8[9437184]{0:T(1024)(128)(4,1)}), s8[4194304]{0:T(1024)(128)(4,1)S(1)}, s32[]{:S(2)}) async-start(s8[9437184]{0:T(1024)(128)(4,1)} %bitcast.178), calls=%async_computation.3 | async-start | bytes 8388608 | tf_op jit(solution)/shard_map/while
  22.0 7.2 %slice-start.1 = ((s8[9437184]{0:T(1024)(128)(4,1)}), s8[4194304]{0:T(1024)(128)(4,1)S(1)}, s32[]{:S(2)}) async-start(s8[9437184]{0:T(1024)(128)(4,1)} %bitcast.178), calls=%async_computation.4 | async-start | bytes 8388608 | tf_op jit(solution)/shard_map/while
  22.0 7.4 %slice-start.2 = ((s8[9437184]{0:T(1024)(128)(4,1)}), s8[1048576]{0:T(1024)(128)(4,1)S(1)}, s32[]{:S(2)}) async-start(s8[9437184]{0:T(1024)(128)(4,1)} %bitcast.178), calls=%async_computation.5 | async-start | bytes 2097152 | tf_op jit(solution)/shard_map/while
  34.2 2.9 copy-start.3
  34.2 3.6 %copy-start.2 = (bf16[512,1,128]{2,0,1:T(8,128)(2,1)S(1)}, bf16[512,1,128]{2,0,1:T(8,128)(2,1)}, u32[]{:S(2)}) copy-start(bf16[512,1,128]{2,0,1:T(8,128)(2,1)} %copy-done.1) | copy-start | bytes 393220 | tf_op jit(solution)/shard_map/while
  37.1 0.7 copy-start.4
  46.3 7.5 %copy-start.1 = (bf16[512,1,128]{2,0,1:T(8,128)(2,1)}, bf16[512,1,128]{2,0,1:T(8,128)(2,1)S(1)}, u32[]{:S(2)}) copy-start(bf16[512,1,128]{2,0,1:T(8,128)(2,1)S(1)} %get-tuple-element.335) | copy-start | bytes 393220 | tf_op jit(solution)/shard_map/while
  46.5 7.8 %copy-start.6 = (s32[2]{0:T(128)S(1)}, s32[2]{0:T(128)}, u32[]{:S(2)}) copy-start(s32[2]{0:T(128)} %get-tuple-element.378) | copy-start | bytes 28 | tf_op jit(solution)/shard_map/while
  48.2 3.6 %copy-start = (f32[576,512,8]{1,0,2:T(8,128)}, f32[576,512,8]{1,0,2:T(8,128)S(1)}, u32[]{:S(2)}) copy-start(f32[576,512,8]{1,0,2:T(8,128)S(1)} %get-tuple-element.336) | copy-start | bytes 28311556 | tf_op jit(solution)/shard_map/while
  55.5 7.4 %slice-start = ((s8[9437184]{0:T(1024)(128)(4,1)}), s8[4194304]{0:T(1024)(128)(4,1)S(1)}, s32[]{:S(2)}) async-start(s8[9437184]{0:T(1024)(128)(4,1)} %bitcast.178), calls=%async_computation.3 | async-start | bytes 8388608 | tf_op jit(solution)/shard_map/while
  55.6 8.0 %slice-start.1 = ((s8[9437184]{0:T(1024)(128)(4,1)}), s8[4194304]{0:T(1024)(128)(4,1)S(1)}, s32[]{:S(2)}) async-start(s8[9437184]{0:T(1024)(128)(4,1)} %bitcast.178), calls=%async_computation.4 | async-start | bytes 8388608 | tf_op jit(solution)/shard_map/while
  55.6 8.2 %slice-start.2 = ((s8[9437184]{0:T(1024)(128)(4,1)}), s8[1048576]{0:T(1024)(128)(4,1)S(1)}, s32[]{:S(2)}) async-start(s8[9437184]{0:T(1024)(128)(4,1)} %bitcast.178), calls=%async_computation.5 | async-start | bytes 2097152 | tf_op jit(solution)/shard_map/while
  68.5 2.9 copy-start.3
  68.5 3.6 %copy-start.2 = (bf16[512,1,128]{2,0,1:T(8,128)(2,1)S(1)}, bf16[512,1,128]{2,0,1:T(8,128)(2,1)}, u32[]{:S(2)}) copy-start(bf16[512,1,128]{2,0,1:T(8,128)(2,1)} %copy-done.1) | copy-start | bytes 393220 | tf_op jit(solution)/shard_map/while
  71.4 0.7 copy-start.4
  173.0 0.7 copy-start.7
  173.0 15.4 %copy-start.5 = (f32[2,2,64,128]{2,3,1,0:T(8,128)S(1)}, f32[2,2,64,128]{2,3,1,0:T(8,128)}, u32[]{:S(2)}) copy-start(f32[2,2,64,128]{2,3,1,0:T(8,128)} %get-tuple-element.131) | copy-start | bytes 393220
  173.0 16.2 %copy-start.8 = (u32[128]{0:T(128)S(1)}, u32[128]{0:T(128)}, u32[]{:S(2)}) copy-start(u32[128]{0:T(128)} %constant.73) | copy-start | bytes 1540
Sparse Core Ops, SparseCore 0:
  10.2 134.9 all-gather.1
  173.2 91.7 reduce-scatter.2
where the time goes:
time: 297 us
  blocking collectives  108 us (36%)
  waiting for transfers between devices  69.3 us (23%)
  matrix products  56.1 us (19%)
  local copies, waits for them, and re-layouts  26.2 us (9%)
  other arithmetic  20.4 us (7%)
  between operations  15.4 us (5%)
    all_gather x1, waiting for transfers between devices, body(): lax.all_gather(qkv_weight, 'dp', axis=0, tiled=True)  68.6 us
    unnamed x1, blocking collectives  67.2 us
    dot_general x1, matrix products, body(): lax.dot_general(local_grads, lax.all_gather(qkv_weight, 'dp', axis=0, til...  27.9 us
    all_gather x1, blocking collectives, body(): new_prefix = lax.all_gather(updated, 'dp', axis=1, tiled=True)  27.2 us
    psum x1, blocking collectives, body(): live_count = lax.psum(jnp.sum(lengths), 'dp')  14.1 us
    dot_general x2, matrix products, attend_block(): jnp.einsum('igrd,jgd->grij', grad_block, joined_values, preferred_element...  13.8 us
    while x36, local copies, waits for them, and re-layouts  10.4 us
    another operation x7, other arithmetic  8.68 us
  transfers between devices with their start and end apart: 2, of which 1 were waited for; matrix products, arithmetic and copies ran while one was open for 20% of the time, Pallas kernels for 0%

commit v1 on v0

v1 whole, which is shorter than its diff:
```python
import functools
import math

import jax
import jax.numpy as jnp
import numpy as np
from jax import lax
from jax.experimental import pallas as pl
from jax.experimental.pallas import tpu as pltpu
from jax.sharding import Mesh
from jax.sharding import PartitionSpec as P

learning_rate = 0.1

HD=128; GROUP=8; PREFIX=64; SEQ=512; QB=256
rope_base=500000.0

def rope_tables():
    half=HD//2
    freq=np.power(rope_base,-(2.0*np.arange(half))/HD).astype(np.float32)
    ang=(np.arange(SEQ,dtype=np.float32)[:,None]*freq[None,:]).astype(np.float64)
    cos,sin=np.cos(ang).astype(np.float32),np.sin(ang).astype(np.float32)
    wide_cos=np.concatenate([cos,cos],1)
    wide_sin=np.concatenate([sin,-sin],1)
    return cos.T.copy(),sin.T.copy(),wide_cos,wide_sin

NT=(((1,),(1,)),((),()))
NN=(((1,),(0,)),((),()))
def dot(a,b,dims): return lax.dot_general(a,b,dims,preferred_element_type=jnp.float32)

def attn_kernel(len_ref,q_ref,g_ref,k_ref,v_ref,pre_ref,cosT_ref,sinT_ref,cos_ref,sin_ref,out_ref,pg_ref,kj,vj,kT,dk_acc,dv_acc,*,prompt):
    h=pl.program_id(0)
    inverse=1.0/math.sqrt(HD)
    @pl.when(h==0)
    def _():
        kj[0:PREFIX,:]=pre_ref[0].astype(jnp.bfloat16)
        vj[0:PREFIX,:]=pre_ref[1].astype(jnp.bfloat16)
        kj[PREFIX:,:]=k_ref[...]
        vj[PREFIX:,:]=v_ref[...]
        kT[...]=jnp.transpose(kj[...].astype(jnp.float32)).astype(jnp.bfloat16)
        dk_acc[...]=jnp.zeros_like(dk_acc)
        dv_acc[...]=jnp.zeros_like(dv_acc)
    live=len_ref[prompt]
    col=pl.multiple_of(h*HD,HD)
    for b in range(SEQ//QB):
        r0=b*QB; nk=PREFIX+r0+QB
        q=q_ref[r0:r0+QB,:]
        rows=lax.broadcasted_iota(jnp.int32,(QB,HD),0)+r0
        g=jnp.where(rows<live,g_ref[r0:r0+QB,:].astype(jnp.float32),0.0).astype(jnp.bfloat16)
        s=dot(kj[0:nk,:],q,NT)
        dp=dot(vj[0:nk,:],g,NT)
        key=lax.broadcasted_iota(jnp.int32,(QB,QB),0)
        row=lax.broadcasted_iota(jnp.int32,(QB,QB),1)
        s=jnp.concatenate([s[:nk-QB],jnp.where(key<=row,s[nk-QB:],-1e30)],0)
        top=jnp.max(s,0,keepdims=True)
        e=jnp.exp((s-top)*inverse)
        p=e*(1.0/jnp.sum(e,0,keepdims=True))
        rt=jnp.sum(p*dp,0,keepdims=True)
        ds=(p*(dp-rt)).astype(jnp.bfloat16)
        pb=p.astype(jnp.bfloat16)
        dk_acc[0:nk,:]+=dot(ds,q,NN)
        dv_acc[0:nk,:]+=dot(pb,g,NN)
        dqT=dot(kT[:,0:nk],ds,NN)*inverse
        a=dqT[:HD//2]; c=dqT[HD//2:]
        co=cosT_ref[:,r0:r0+QB]; si=sinT_ref[:,r0:r0+QB]
        rot=jnp.concatenate([a*co+c*si,c*co-a*si],0)
        out_ref[r0:r0+QB,pl.ds(col,HD)]=jnp.transpose(rot).astype(jnp.bfloat16)
    @pl.when(h==GROUP-1)
    def _():
        dk=dk_acc[...]*inverse
        pg_ref[0]=dk[0:PREFIX]
        pg_ref[1]=dv_acc[0:PREFIX,:]
        d=dk[PREFIX:]
        out_ref[:,GROUP*HD:(GROUP+1)*HD]=(d*cos_ref[...]+pltpu.roll(d,HD//2,1)*sin_ref[...]).astype(jnp.bfloat16)
        out_ref[:,(GROUP+1)*HD:]=dv_acc[PREFIX:,:].astype(jnp.bfloat16)

def attention(prompt,lengths,queries,out_grad,key_rows,value_rows,prefix,tables):
    whole=lambda shape: pl.BlockSpec(shape,lambda h:(0,)*len(shape))
    return pl.pallas_call(
        functools.partial(attn_kernel,prompt=prompt),
        grid=(GROUP,),
        in_specs=[pl.BlockSpec(memory_space=pltpu.SMEM),
            pl.BlockSpec((SEQ,HD),lambda h:(prompt,h)),
            pl.BlockSpec((SEQ,HD),lambda h:(prompt,h)),
            pl.BlockSpec((SEQ,HD),lambda h:(prompt,0)),
            pl.BlockSpec((SEQ,HD),lambda h:(prompt,0)),
            whole((2,PREFIX,HD)),whole((HD//2,SEQ)),whole((HD//2,SEQ)),whole((SEQ,HD)),whole((SEQ,HD))],
        out_specs=[whole((SEQ,(GROUP+2)*HD)),whole((2,PREFIX,HD))],
        out_shape=[jax.ShapeDtypeStruct((SEQ,(GROUP+2)*HD),jnp.bfloat16),jax.ShapeDtypeStruct((2,PREFIX,HD),jnp.float32)],
        scratch_shapes=[pltpu.VMEM((PREFIX+SEQ,HD),jnp.bfloat16),pltpu.VMEM((PREFIX+SEQ,HD),jnp.bfloat16),pltpu.VMEM((HD,PREFIX+SEQ),jnp.bfloat16),
            pltpu.VMEM((PREFIX+SEQ,HD),jnp.float32),pltpu.VMEM((PREFIX+SEQ,HD),jnp.float32)],
        compiler_params=pltpu.CompilerParams(vmem_limit_bytes=40*2**20),
        cost_estimate=pl.CostEstimate(flops=5*2*8*512*576*128,bytes_accessed=4*2**20,transcendentals=8*512*576),
        name="attention_backward",
    )(lengths,queries,out_grad,key_rows,value_rows,prefix,*tables)


def multiply_kernel(place_ref, own_ref, other_ref, *refs):
    blocks, out_ref = refs[:-1], refs[-1]
    width = own_ref.shape[1]
    for at, block in enumerate(blocks):
        total = dot(own_ref[...], block[:, :width], NT) + dot(other_ref[...], block[:, width:], NT)
        out_ref[place_ref[at]] = total.astype(jnp.bfloat16)


def multiply(own, other, blocks, places):
    rows, width = own.shape
    cols = blocks[0].shape[0]
    step = min(rows, 512)
    count = len(blocks)
    return pl.pallas_call(
        multiply_kernel,
        grid=(rows // step,),
        in_specs=[
            pl.BlockSpec(memory_space=pltpu.SMEM),
            pl.BlockSpec((step, width), lambda r: (r, 0)),
            pl.BlockSpec((step, width), lambda r: (r, 0)),
        ]
        + [pl.BlockSpec((cols, 2 * width), lambda r: (0, 0))] * count,
        out_specs=pl.BlockSpec((count, step, cols), lambda r: (0, r, 0)),
        out_shape=jax.ShapeDtypeStruct((count, rows, cols), jnp.bfloat16),
        compiler_params=pltpu.CompilerParams(vmem_limit_bytes=32 * 2**20),
        cost_estimate=pl.CostEstimate(
            flops=4 * count * rows * cols * width,
            bytes_accessed=4 * rows * width + 2 * count * cols * (2 * width + rows),
            transcendentals=0,
        ),
        name="project",
    )(places, own, other, *blocks)


AXES = ("x", "y", "z", "c")


def pairs_of(move):
    def flat(x, y, z, c):
        return ((x * 4 + y) * 4 + z) * 2 + c

    found = []
    for x in range(4):
        for y in range(4):
            for z in range(4):
                for c in range(2):
                    target = move(x, y, z, c)
                    if target is not None:
                        found.append((flat(x, y, z, c), flat(*target)))
    return found


def send(array, move):
    return lax.ppermute(array, AXES, pairs_of(move))


def x_up(x, y, z, c):
    return ((x + 1) % 4, y, z, c)


def x_down(x, y, z, c):
    return ((x - 1) % 4, y, z, c)


def y_mate(x, y, z, c):
    return (x, y ^ 1, z, c)


def y_partner(x, y, z, c):
    return (x, 3 - y, z, c)


def sibling(x, y, z, c):
    return (x, y, z, 1 - c)


def home(x, y, z, c):
    half = y // 2
    return (x, 3 - y, z, c) if c == half else (x, y, z, 1 - c)


def home_rest(x, y, z, c):
    half = y // 2
    return (x, 3 - y, z, 1 - c) if c != half else None


def gather_blocks(mine):
    rows = mine.shape[0]
    from_down = send(mine, x_up)
    from_up = send(mine, x_down)
    mate = send(mine, y_mate)
    far_a = send(from_down[: rows // 2], x_up)
    far_b = send(from_up[rows // 2 :], x_down)
    far = jnp.concatenate([far_a, far_b], 0)
    mate_down = send(mate, x_up)
    mate_up = send(mate, x_down)
    mate_far = send(far, y_mate)
    return (mine, from_down, from_up, far), (mate, mate_down, mate_up, mate_far)


def body(queries, key_rows, value_rows, out_grad, prefix, lengths, qkv_weight):
    x_at, y_at, core = lax.axis_index("x"), lax.axis_index("y"), lax.axis_index("c")
    half = y_at // 2
    rows = qkv_weight.shape[0] // 2
    kept = lax.dynamic_slice_in_dim(qkv_weight, core * rows, rows, 0)
    given = lax.dynamic_slice_in_dim(qkv_weight, (1 - core) * rows, rows, 0)
    mine = jnp.concatenate([kept, send(given, sibling)], 1)
    near_blocks, mate_blocks = gather_blocks(mine)
    places = jnp.stack([x_at, (x_at + 3) % 4, (x_at + 1) % 4, (x_at + 2) % 4]).astype(jnp.int32)

    tables = tuple(jnp.asarray(t) for t in rope_tables())
    grads, prefix_terms = [], []
    for prompt in range(2):
        g, t = attention(prompt, lengths, queries, out_grad, key_rows, value_rows, prefix, tables)
        grads.append(g)
        prefix_terms.append(t)
    others = [send(g, sibling) for g in grads]
    theirs = [send(g, y_partner) for g in grads]
    their_others = [send(g, sibling) for g in theirs]

    count_row = jnp.full((8, HD), jnp.sum(lengths).astype(jnp.float32))
    terms = jnp.concatenate([(prefix_terms[0] + prefix_terms[1]).reshape(2 * PREFIX, HD), count_row], 0)
    for move in (
        lambda x, y, z, c: (x ^ 1, y, z, c),
        lambda x, y, z, c: (3 - x, y, z, c),
        lambda x, y, z, c: (x, y ^ 1, z, c),
        lambda x, y, z, c: (x, 3 - y, z, c),
    ):
        terms = terms + send(terms, move)
    loss_scale = 16384.0 / terms[2 * PREFIX, 0]
    new_prefix = prefix - learning_rate * loss_scale * terms[: 2 * PREFIX].reshape(2, PREFIX, HD)

    def reduced(own, other, blocks):
        partial = multiply(own, other, blocks, places)
        summed = lax.psum_scatter(partial, "z", scatter_dimension=0, tiled=True)[0]
        return (summed.astype(jnp.float32) * loss_scale).astype(jnp.bfloat16)

    self_own, self_other = jnp.concatenate(grads, 0), jnp.concatenate(others, 0)
    self_near = reduced(self_own, self_other, near_blocks)
    q0_near = reduced(theirs[0], their_others[0], near_blocks)
    q0_mate = reduced(theirs[0], their_others[0], mate_blocks)
    q1_near = reduced(theirs[1], their_others[1], near_blocks)
    q1_mate = reduced(theirs[1], their_others[1], mate_blocks)
    self_mate = reduced(self_own, self_other, mate_blocks)

    odd = y_at % 2 == 1

    def ordered(near, mate):
        return jnp.concatenate([jnp.where(odd, mate, near), jnp.where(odd, near, mate)], 1)

    self_part = ordered(self_near, self_mate)
    pair_part = ordered(jnp.concatenate([q0_near, q1_near], 0), jnp.concatenate([q0_mate, q1_mate], 0))
    at_home = core == half
    first = send(jnp.where(at_home, pair_part, self_part), home)
    second = send(pair_part, home_rest)
    same = jnp.where(at_home, self_part, first)
    swapped = jnp.where(at_home, first, second)
    zero, one = jnp.where(core == 0, same, swapped), jnp.where(core == 0, swapped, same)
    input_grad = jnp.stack([zero.reshape(1024, 2, 256), one.reshape(1024, 2, 256)], 2).reshape(1024, 1024)
    return (input_grad, new_prefix)


def solution(mesh):
    fine = Mesh(mesh.devices.reshape(4, 4, 4, 2), AXES)
    dp, tensor = ("x", "y"), ("z", "c")
    both = P(dp, tensor)
    return jax.shard_map(
        body,
        mesh=fine,
        in_specs=(both, both, both, both, P(None, None, tensor), P(dp), both),
        out_specs=(both, P(None, None, tensor)),
        check_vma=False,
    )
```

time: 297 us -> 348 us (1.17)
  waiting for transfers between devices: 69.3 us -> 185 us
  blocking collectives: 108 us -> 0 us
  Pallas kernels: 0 us -> 59.7 us
  matrix products: 56.1 us -> 0 us
  starting transfers between devices: 0.08 us -> 24.4 us
  local copies, waits for them, and re-layouts: 26.2 us -> 45.7 us
  other arithmetic: 20.4 us -> 13.6 us
    ppermute x0 -> x21, waiting for transfers between devices: none -> 135 us  [send(): return lax.ppermute(array, AXES, pairs_of(move))]
    all_gather x1 -> x0, waiting for transfers between devices: 68.6 us -> none  [body(): lax.all_gather(qkv_weight, 'dp', axis=0, tiled=True)]
    unnamed x1 -> x0, blocking collectives: 67.2 us -> none
    pallas_call x0 -> x8, Pallas kernels: none -> 59.7 us  [the longest x6 34.3 us: multiply(): pl.pallas_call(multiply_kernel, grid=(rows // step,), in_specs=[pl.BlockS...]
    dot_general x11 -> x0, matrix products: 56.1 us -> none  [the longest x1 27.9 us: body(): lax.dot_general(local_grads, lax.all_gather(qkv_weight, 'dp', axis=0, til...]
    reduce_scatter x1 -> x6, waiting for transfers between devices: 0.01 us -> 50.4 us  [reduced(): summed = lax.psum_scatter(partial, 'z', scatter_dimension=0, tiled=True)[0]]
    unnamed x8 -> x89, local copies, waits for them, and re-layouts: 1.85 us -> 33.7 us
    all_gather x1 -> x0, blocking collectives: 27.2 us -> none  [body(): new_prefix = lax.all_gather(updated, 'dp', axis=1, tiled=True)]
  transfers between devices with their start and end apart: 2 -> 27, of which waited for: 1 -> 17; matrix products, arithmetic and copies ran while one was open for 20% -> 4% of each run, Pallas kernels for 0% -> 17%
where the time goes in v1:
time: 348 us; the launch traced here: 345 us
  waiting for transfers between devices  185 us (53%)
  Pallas kernels  59.7 us (17%)
  local copies, waits for them, and re-layouts  45.7 us (13%)
  starting transfers between devices  24.4 us (7%)
  between operations  16 us (5%)
  other arithmetic  13.6 us (4%)
    ppermute x21, waiting for transfers between devices, send(): return lax.ppermute(array, AXES, pairs_of(move))  135 us
    reduce_scatter x6, waiting for transfers between devices, reduced(): summed = lax.psum_scatter(partial, 'z', scatter_dimension=0, tiled=True)[0]  50.4 us
    pallas_call x6, Pallas kernels, multiply(): pl.pallas_call(multiply_kernel, grid=(rows // step,), in_specs=[pl.BlockS...  34.3 us
    unnamed x89, local copies, waits for them, and re-layouts  33.7 us
    pallas_call x2, Pallas kernels, attention(): pl.pallas_call(functools.partial(attn_kernel, prompt=prompt), grid=(GROUP...  25.5 us
    ppermute x21, starting transfers between devices, send(): return lax.ppermute(array, AXES, pairs_of(move))  24.2 us
  transfers between devices with their start and end apart: 27, of which 17 were waited for; matrix products, arithmetic and copies ran while one was open for 4% of the time, Pallas kernels for 17%

profile of v1, /device:TPU:2, one launch (start us, length us, event | category | flops | bytes accessed | tf_op | source)
XLA Modules:
  0.0 344.8 jit_solution(541920622073164070)
XLA Ops:
  7.3 1.5 constant_dynamic-slice_fusion.1
  8.9 2.1 collective-permute-done.2
  11.1 1.6 collective-permute-start.6
  14.6 12.2 %attention_backward.3 = (bf16[512,1280]{1,0:T(8,128)(2,1)S(1)}, f32[2,64,128]{2,1,0:T(8,128)S(1)}) custom-call(s32[2]{0:T(128)S(1)} %copy-done.35, bf16[1024,1024]{1,0:T(8,128)(2,1)S(1)} %copy-done.20, bf16[1024,1024]{1,0:T(8,128)(2,1)S(1)} %copy-done.21, bf16[1024,128]{1,0:T(8,128)(2,1)S(1)} %copy-done.33, bf16[1024,128]{1,0:T(8,128)(2,1)S(1)} %copy-done.34, ...), custom_call_target="tpu_custom_call" | custom-call | flops 3019898880 | bytes 4194304 | tf_op jit(solution)/shard_map/attention_backward/pallas_call | solution.py:79
  26.8 3.1 collective-permute-start.17
  30.4 11.6 %collective-permute-done.6.refs_1_ = bf16[256,2560]{1,0:T(8,128)(2,1)S(1)} collective-permute-done((bf16[256,2560]{1,0:T(8,128)(2,1)S(1)}, bf16[256,2560]{1,0:T(8,128)(2,1)S(1)}, u32[]{:S(2)}, u32[]{:S(2)}) %collective-permute-start.6) | collective-permute-done | bytes 1310752 | tf_op jit(solution)/shard_map/ppermute | solution.py:151
  43.0 1.5 collective-permute-start.7
  44.5 14.3 %collective-permute-done.17.own_ref = bf16[512,1280]{1,0:T(8,128)(2,1)} collective-permute-done((bf16[512,1280]{1,0:T(8,128)(2,1)S(1)}, bf16[512,1280]{1,0:T(8,128)(2,1)}, u32[]{:S(2)}, u32[]{:S(2)}) %collective-permute-start.17) | collective-permute-done | bytes 1310752 | tf_op jit(solution)/shard_map/ppermute | solution.py:151
  58.8 1.4 collective-permute-done.8.refs_2_
  61.7 13.3 %attention_backward.2 = (bf16[512,1280]{1,0:T(8,128)(2,1)}, f32[2,64,128]{2,1,0:T(8,128)S(1)}) custom-call(s32[2]{0:T(128)S(1)} %copy-done.35, bf16[1024,1024]{1,0:T(8,128)(2,1)S(1)} %copy-done.20, bf16[1024,1024]{1,0:T(8,128)(2,1)S(1)} %copy-done.21, bf16[1024,128]{1,0:T(8,128)(2,1)S(1)} %copy-done.33, bf16[1024,128]{1,0:T(8,128)(2,1)S(1)} %copy-done.34, ...), custom_call_target="tpu_custom_call" | custom-call | flops 3019898880 | bytes 4194304 | tf_op jit(solution)/shard_map/attention_backward/pallas_call | solution.py:79
  74.9 1.6 collective-permute-start.15
  77.2 1.2 constant_dynamic-update-slice_fusion.4.refs_3_
  78.5 4.7 %project.11 = bf16[4,512,256]{2,1,0:T(8,128)(2,1)S(1)} custom-call(s32[4]{0:T(128)S(1)} %pad_add_fusion.place_ref, bf16[512,1280]{1,0:T(8,128)(2,1)} %collective-permute-done.17.own_ref, bf16[512,1280]{1,0:T(8,128)(2,1)} %collective-permute-done.18.other_ref, bf16[256,2560]{1,0:T(8,128)(2,1)S(1)} %pad_maximum_fusion.1.refs_0_, ...), custom_call_target="tpu_custom_call" | custom-call | flops 2684354560 | bytes 8912896 | tf_op jit(solution)/shard_map/project/pallas_call | solution.py:111
  84.2 1.1 copy-done.16
  85.3 20.7 %collective-permute-done.15.own_ref = bf16[512,1280]{1,0:T(8,128)(2,1)} collective-permute-done((bf16[512,1280]{1,0:T(8,128)(2,1)}, bf16[512,1280]{1,0:T(8,128)(2,1)}, u32[]{:S(2)}, u32[]{:S(2)}) %collective-permute-start.15) | collective-permute-done | bytes 1310752 | tf_op jit(solution)/shard_map/ppermute | solution.py:151
  106.0 3.2 collective-permute-done.16.other_ref
  109.3 1.3 copy-done.10
  110.6 1.3 copy-done.14
  111.9 1.3 copy-done.17
  113.3 4.3 %project.10 = bf16[4,512,256]{2,1,0:T(8,128)(2,1)S(1)} custom-call(s32[4]{0:T(128)S(1)} %pad_add_fusion.place_ref, bf16[512,1280]{1,0:T(8,128)(2,1)} %collective-permute-done.15.own_ref, bf16[512,1280]{1,0:T(8,128)(2,1)S(1)} %collective-permute-done.16.other_ref, bf16[256,2560]{1,0:T(8,128)(2,1)S(1)} %pad_maximum_fusion.1.refs_0_, ...), custom_call_target="tpu_custom_call" | custom-call | flops 2684354560 | bytes 8912896 | tf_op jit(solution)/shard_map/project/pallas_call | solution.py:111
  118.5 1.1 copy-done.31
  119.7 17.7 %collective-permute-done.3.refs_0_ = bf16[256,2560]{1,0:T(8,128)(2,1)} collective-permute-done((bf16[256,2560]{1,0:T(8,128)(2,1)S(1)}, bf16[256,2560]{1,0:T(8,128)(2,1)}, u32[]{:S(2)}, u32[]{:S(2)}) %collective-permute-start.3) | collective-permute-done | bytes 1310752 | tf_op jit(solution)/shard_map/ppermute | solution.py:151
  137.3 2.5 collective-permute-start.5
  140.1 28.0 %collective-permute-done.5.refs_2_ = bf16[256,2560]{1,0:T(8,128)(2,1)S(1)} collective-permute-done((bf16[256,2560]{1,0:T(8,128)(2,1)}, bf16[256,2560]{1,0:T(8,128)(2,1)S(1)}, u32[]{:S(2)}, u32[]{:S(2)}) %collective-permute-start.5) | collective-permute-done | bytes 1310752 | tf_op jit(solution)/shard_map/ppermute | solution.py:151
  168.0 2.1 collective-permute-done.4.refs_1_
  170.1 5.0 %project.9 = bf16[4,512,256]{2,1,0:T(8,128)(2,1)S(1)} custom-call(s32[4]{0:T(128)S(1)} %pad_add_fusion.place_ref, bf16[512,1280]{1,0:T(8,128)(2,1)} %collective-permute-done.17.own_ref, bf16[512,1280]{1,0:T(8,128)(2,1)} %collective-permute-done.18.other_ref, bf16[256,2560]{1,0:T(8,128)(2,1)} %collective-permute-done.3.refs_0_, ...), custom_call_target="tpu_custom_call" | custom-call | flops 2684354560 | bytes 8912896 | tf_op jit(solution)/shard_map/project/pallas_call | solution.py:111
  176.2 1.1 copy-done.22
  177.3 1.1 copy-done.25
  178.4 1.0 copy-done.28
  179.6 1.3 copy-done.23
  180.9 1.3 copy-done.26
  182.2 1.3 copy-done.29
  183.5 1.3 copy-done.32
  184.8 4.7 %project.8 = bf16[4,512,256]{2,1,0:T(8,128)(2,1)S(1)} custom-call(s32[4]{0:T(128)S(1)} %pad_add_fusion.place_ref, bf16[512,1280]{1,0:T(8,128)(2,1)} %collective-permute-done.15.own_ref, bf16[512,1280]{1,0:T(8,128)(2,1)S(1)} %copy-done.32, bf16[256,2560]{1,0:T(8,128)(2,1)} %collective-permute-done.3.refs_0_, bf16[256,2560]{1,0:T(8,128)(2,1)S(1)} %copy-done.26, ...), custom_call_target="tpu_custom_call" | custom-call | flops 2684354560 | bytes 8912896 | tf_op jit(solution)/shard_map/project/pallas_call | solution.py:111
  191.1 1.4 constant_dynamic-update-slice_fusion.1
  192.7 2.4 constant_dynamic-update-slice_fusion.3
  196.1 7.5 %project.7 = bf16[4,1024,256]{2,1,0:T(8,128)(2,1)} custom-call(s32[4]{0:T(128)S(1)} %pad_add_fusion.place_ref, bf16[1024,1280]{1,0:T(8,128)(2,1)S(1)} %constant_dynamic-update-slice_fusion.own_ref, bf16[1024,1280]{1,0:T(8,128)(2,1)S(1)} %constant_dynamic-update-slice_fusion.2.other_ref, bf16[256,2560]{1,0:T(8,128)(2,1)S(1)} %pad_maximum_fusion.1.refs_0_, ...), custom_call_target="tpu_custom_call" | custom-call | flops 5368709120 | bytes 12582912 | tf_op jit(solution)/shard_map/project/pallas_call | solution.py:111
  203.6 1.5 copy-done.4
  205.2 1.3 copy-done.24
  206.4 1.7 copy-done.5
  208.1 1.7 copy-done.7
  209.9 1.3 copy-done.30
  211.2 8.2 %project.6 = bf16[4,1024,256]{2,1,0:T(8,128)(2,1)} custom-call(s32[4]{0:T(128)S(1)} %pad_add_fusion.place_ref, bf16[1024,1280]{1,0:T(8,128)(2,1)S(1)} %copy-done.7, bf16[1024,1280]{1,0:T(8,128)(2,1)S(1)} %copy-done.5, bf16[256,2560]{1,0:T(8,128)(2,1)} %collective-permute-done.3.refs_0_, bf16[256,2560]{1,0:T(8,128)(2,1)S(1)} %copy-done.27, ...), custom_call_target="tpu_custom_call" | custom-call | flops 5368709120 | bytes 12582912 | tf_op jit(solution)/shard_map/project/pallas_call | solution.py:111
  220.7 2.2 collective-permute-start.11
  222.9 2.4 collective-permute-done.11
  225.3 1.2 collective-permute-start.12
  226.5 3.2 collective-permute-done.12
  230.2 3.9 %collective-permute-done.13 = f32[136,128]{1,0:T(8,128)S(1)} collective-permute-done((f32[136,128]{1,0:T(8,128)S(1)}, f32[136,128]{1,0:T(8,128)S(1)}, u32[]{:S(2)}, u32[]{:S(2)}) %collective-permute-start.13) | collective-permute-done | bytes 69664 | tf_op jit(solution)/shard_map/ppermute | solution.py:151
  234.1 3.0 collective-permute-start.14
  237.1 2.6 collective-permute-done.14
  240.9 1.0 fusion.3
  242.0 1.0 fusion.2
  243.0 1.0 fusion.1
  244.0 1.0 fusion
  245.2 17.9 %reduce-scatter.9.cloned.1.call-done = bf16[1,1024,256]{2,1,0:T(8,128)(2,1)} async-done(((bf16[4,1024,256]{2,1,0:T(8,128)(2,1)}), bf16[1,1024,256]{2,1,0:T(8,128)(2,1)}) %reduce-scatter.9.cloned.1.call-update) | async-done | bytes 524304 | tf_op jit(solution)/shard_map/reduce_scatter | solution.py:232
  263.1 32.5 %reduce-scatter.7.cloned.1.call-done = bf16[1,1024,256]{2,1,0:T(8,128)(2,1)} async-done(((bf16[4,1024,256]{2,1,0:T(8,128)(2,1)}), bf16[1,1024,256]{2,1,0:T(8,128)(2,1)}) %reduce-scatter.7.cloned.1.call-update) | async-done | bytes 524304 | tf_op jit(solution)/shard_map/reduce_scatter | solution.py:232
  295.6 1.5 select_bitcast_fusion.1
  297.1 1.7 pad_maximum_fusion.3
  299.4 4.2 %collective-permute-start.19 = (bf16[1024,512]{1,0:T(8,128)(2,1)}, bf16[1024,512]{1,0:T(8,128)(2,1)}, u32[]{:S(2)}, u32[]{:S(2)}) collective-permute-start(bf16[1024,512]{1,0:T(8,128)(2,1)} %get-tuple-element.15), channel_id=1, source_target_pairs={{0,24},{1,0},{2,26},{3,2},{4,28},{5,4},{6,30},{7,6},{8,16},{9,8},{... | collective-permute-start | bytes 3145736 | tf_op jit(solution)/shard_map/ppermute | solution.py:151
  305.3 21.3 %collective-permute-done.19 = bf16[1024,512]{1,0:T(8,128)(2,1)} collective-permute-done((bf16[1024,512]{1,0:T(8,128)(2,1)}, bf16[1024,512]{1,0:T(8,128)(2,1)}, u32[]{:S(2)}, u32[]{:S(2)}) %collective-permute-start.19) | collective-permute-done | bytes 1048608 | tf_op jit(solution)/shard_map/ppermute | solution.py:151
  326.6 1.8 broadcast_select_fusion.4
  329.0 3.0 pad_maximum_fusion
  332.0 3.2 copy.13
  335.2 2.7 reshape.44
  (124 shorter events, 17.1 us)
Async XLA Ops:
  7.2 233.8 %reduce-scatter.17.cloned.1.call-start = ((), (), s32[]{:S(2)}) async-start(), calls=%async_computation.11 | async-start | bytes 1310720 | tf_op jit(solution)/shard_map/reduce_scatter | solution.py:232
  7.2 5.4 %copy-start.19 = (f32[2,64,128]{2,1,0:T(8,128)S(1)}, f32[2,64,128]{2,1,0:T(8,128)}, u32[]{:S(2)}) copy-start(f32[2,64,128]{2,1,0:T(8,128)} %pre_ref.3) | copy-start | bytes 196612
  7.2 5.4 %copy-start.20 = (bf16[1024,1024]{1,0:T(8,128)(2,1)S(1)}, bf16[1024,1024]{1,0:T(8,128)(2,1)}, u32[]{:S(2)}) copy-start(bf16[1024,1024]{1,0:T(8,128)(2,1)} %q_ref.3) | copy-start | bytes 6291460
  7.2 5.4 %copy-start.21 = (bf16[1024,1024]{1,0:T(8,128)(2,1)S(1)}, bf16[1024,1024]{1,0:T(8,128)(2,1)}, u32[]{:S(2)}) copy-start(bf16[1024,1024]{1,0:T(8,128)(2,1)} %g_ref.3) | copy-start | bytes 6291460
  7.2 5.4 %copy-start.33 = (bf16[1024,128]{1,0:T(8,128)(2,1)S(1)}, bf16[1024,128]{1,0:T(8,128)(2,1)}, u32[]{:S(2)}) copy-start(bf16[1024,128]{1,0:T(8,128)(2,1)} %k_ref.3) | copy-start | bytes 786436
  7.3 5.4 %copy-start.34 = (bf16[1024,128]{1,0:T(8,128)(2,1)S(1)}, bf16[1024,128]{1,0:T(8,128)(2,1)}, u32[]{:S(2)}) copy-start(bf16[1024,128]{1,0:T(8,128)(2,1)} %v_ref.3) | copy-start | bytes 786436
  7.3 5.4 %copy-start.35 = (s32[2]{0:T(128)S(1)}, s32[2]{0:T(128)}, u32[]{:S(2)}) copy-start(s32[2]{0:T(128)} %len_ref.3) | copy-start | bytes 28
  7.3 5.4 %copy-start.36 = (f32[512,128]{1,0:T(8,128)S(1)}, f32[512,128]{1,0:T(8,128)}, u32[]{:S(2)}) copy-start(f32[512,128]{1,0:T(8,128)} %constant.78.clone.sin_ref) | copy-start | bytes 786436
  7.3 5.4 %copy-start.39 = (f32[64,512]{1,0:T(8,128)S(1)}, f32[64,512]{1,0:T(8,128)}, u32[]{:S(2)}) copy-start(f32[64,512]{1,0:T(8,128)} %constant.76.clone.sinT_ref) | copy-start | bytes 393220
  8.8 2.2 collective-permute-start.2
  11.1 30.9 %collective-permute-start.6 = (bf16[256,2560]{1,0:T(8,128)(2,1)S(1)}, bf16[256,2560]{1,0:T(8,128)(2,1)S(1)}, u32[]{:S(2)}, u32[]{:S(2)}) collective-permute-start(bf16[256,2560]{1,0:T(8,128)(2,1)S(1)} %pad_maximum_fusion.1.refs_0_), channel_id=1, source_target_pairs={{0,32},{1,33},{2,34},{3,35},{4,36},{5,37},{6,38},{7,39},{8,40},{9,... | collective-permute-start | bytes 3932168 | tf_op jit(solution)/shard_map/ppermute | solution.py:151
  26.8 34.9 %copy-start.38 = (f32[512,128]{1,0:T(8,128)S(1)}, f32[512,128]{1,0:T(8,128)}, u32[]{:S(2)}) copy-start(f32[512,128]{1,0:T(8,128)} %constant.77.clone.cos_ref) | copy-start | bytes 786436
  26.8 34.9 %copy-start.41 = (f32[64,512]{1,0:T(8,128)S(1)}, f32[64,512]{1,0:T(8,128)}, u32[]{:S(2)}) copy-start(f32[64,512]{1,0:T(8,128)} %constant.75.clone.cosT_ref) | copy-start | bytes 393220
  26.8 32.0 %collective-permute-start.17 = (bf16[512,1280]{1,0:T(8,128)(2,1)S(1)}, bf16[512,1280]{1,0:T(8,128)(2,1)}, u32[]{:S(2)}, u32[]{:S(2)}) collective-permute-start(bf16[512,1280]{1,0:T(8,128)(2,1)S(1)} %get-tuple-element.7), channel_id=1, source_target_pairs={{0,24},{1,25},{2,26},{3,27},{4,28},{5,29},{6,30},{7,31},{8,16},{9,... | collective-permute-start | bytes 3932168 | tf_op jit(solution)/shard_map/ppermute | solution.py:151
  29.9 30.3 %collective-permute-start.8 = (bf16[256,2560]{1,0:T(8,128)(2,1)S(1)}, bf16[256,2560]{1,0:T(8,128)(2,1)S(1)}, u32[]{:S(2)}, u32[]{:S(2)}) collective-permute-start(bf16[256,2560]{1,0:T(8,128)(2,1)S(1)} %pad_maximum_fusion.1.refs_0_), channel_id=1, source_target_pairs={{0,96},{1,97},{2,98},{3,99},{4,100},{5,101},{6,102},{7,103},{8,104... | collective-permute-start | bytes 3932168 | tf_op jit(solution)/shard_map/ppermute | solution.py:151
  42.0 18.2 %copy-start.8 = (bf16[256,2560]{1,0:T(8,128)(2,1)}, bf16[256,2560]{1,0:T(8,128)(2,1)S(1)}, u32[]{:S(2)}) copy-start(bf16[256,2560]{1,0:T(8,128)(2,1)S(1)} %collective-permute-done.6.refs_1_) | copy-start | bytes 3932164
  43.0 33.7 %collective-permute-start.7 = (bf16[128,2560]{1,0:T(8,128)(2,1)}, bf16[128,2560]{1,0:T(8,128)(2,1)S(1)}, u32[]{:S(2)}, u32[]{:S(2)}) collective-permute-start(bf16[128,2560]{1,0:T(8,128)(2,1)} %slice.16), channel_id=1, source_target_pairs={{0,32},{1,33},{2,34},{3,35},{4,36},{5,37},{6,38},{7,39},{8,40},{9,... | collective-permute-start | bytes 1966088 | tf_op jit(solution)/shard_map/ppermute | solution.py:151
  58.8 19.7 %collective-permute-start.18 = (bf16[512,1280]{1,0:T(8,128)(2,1)}, bf16[512,1280]{1,0:T(8,128)(2,1)}, u32[]{:S(2)}, u32[]{:S(2)}) collective-permute-start(bf16[512,1280]{1,0:T(8,128)(2,1)} %collective-permute-done.17.own_ref), channel_id=1, source_target_pairs={{0,1},{1,0},{2,3},{3,2},{4,5},{5,4},{6,7},{7,6},{8,9},{9,8},{10,11... | collective-permute-start | bytes 3932168 | tf_op jit(solution)/shard_map/ppermute | solution.py:151
  60.1 14.8 %copy-start.12 = (bf16[256,2560]{1,0:T(8,128)(2,1)}, bf16[256,2560]{1,0:T(8,128)(2,1)S(1)}, u32[]{:S(2)}) copy-start(bf16[256,2560]{1,0:T(8,128)(2,1)S(1)} %collective-permute-done.8.refs_2_) | copy-start | bytes 3932164
  61.1 16.1 %collective-permute-start.9 = (bf16[128,2560]{1,0:T(8,128)(2,1)}, bf16[128,2560]{1,0:T(8,128)(2,1)}, u32[]{:S(2)}, u32[]{:S(2)}) collective-permute-start(bf16[128,2560]{1,0:T(8,128)(2,1)} %slice.17), channel_id=1, source_target_pairs={{0,96},{1,97},{2,98},{3,99},{4,100},{5,101},{6,102},{7,103},{8,104... | collective-permute-start | bytes 1966088 | tf_op jit(solution)/shard_map/ppermute | solution.py:151
  74.9 31.1 %collective-permute-start.15 = (bf16[512,1280]{1,0:T(8,128)(2,1)}, bf16[512,1280]{1,0:T(8,128)(2,1)}, u32[]{:S(2)}, u32[]{:S(2)}) collective-permute-start(bf16[512,1280]{1,0:T(8,128)(2,1)} %get-tuple-element.6), channel_id=1, source_target_pairs={{0,24},{1,25},{2,26},{3,27},{4,28},{5,29},{6,30},{7,31},{8,16},{9,... | collective-permute-start | bytes 3932168 | tf_op jit(solution)/shard_map/ppermute | solution.py:151
  76.6 1.9 copy-start.9
  76.6 1.9 copy-start.13
  84.2 1.1 copy-start.16
  85.3 156.7 %reduce-scatter.15.cloned.1.call-start = ((), (), s32[]{:S(2)}) async-start(), calls=%async_computation.10 | async-start | bytes 1310720 | tf_op jit(solution)/shard_map/reduce_scatter | solution.py:232
  106.0 3.2 collective-permute-start.16
  106.0 31.3 %collective-permute-start.3 = (bf16[256,2560]{1,0:T(8,128)(2,1)S(1)}, bf16[256,2560]{1,0:T(8,128)(2,1)}, u32[]{:S(2)}, u32[]{:S(2)}) collective-permute-start(bf16[256,2560]{1,0:T(8,128)(2,1)S(1)} %pad_maximum_fusion.1.refs_0_), channel_id=1, source_target_pairs={{0,8},{1,9},{2,10},{3,11},{4,12},{5,13},{6,14},{7,15},{8,0},{9,1},... | collective-permute-start | bytes 3932168 | tf_op jit(solution)/shard_map/ppermute | solution.py:151
  109.3 1.3 copy-start.10
  110.6 1.3 copy-start.14
  111.9 1.3 copy-start.17
  118.5 1.1 copy-start.31
  119.6 123.4 %reduce-scatter.13.cloned.1.call-start = ((), (), s32[]{:S(2)}) async-start(), calls=%async_computation.9 | async-start | bytes 1310720 | tf_op jit(solution)/shard_map/reduce_scatter | solution.py:232
  137.3 30.7 %collective-permute-start.5 = (bf16[256,2560]{1,0:T(8,128)(2,1)}, bf16[256,2560]{1,0:T(8,128)(2,1)S(1)}, u32[]{:S(2)}, u32[]{:S(2)}) collective-permute-start(bf16[256,2560]{1,0:T(8,128)(2,1)} %collective-permute-done.3.refs_0_), channel_id=1, source_target_pairs={{0,96},{1,97},{2,98},{3,99},{4,100},{5,101},{6,102},{7,103},{8,104... | collective-permute-start | bytes 3932168 | tf_op jit(solution)/shard_map/ppermute | solution.py:151
  139.8 30.3 %collective-permute-start.4 = (bf16[256,2560]{1,0:T(8,128)(2,1)}, bf16[256,2560]{1,0:T(8,128)(2,1)S(1)}, u32[]{:S(2)}, u32[]{:S(2)}) collective-permute-start(bf16[256,2560]{1,0:T(8,128)(2,1)} %collective-permute-done.3.refs_0_), channel_id=1, source_target_pairs={{0,32},{1,33},{2,34},{3,35},{4,36},{5,37},{6,38},{7,39},{8,40},{9,... | collective-permute-start | bytes 3932168 | tf_op jit(solution)/shard_map/ppermute | solution.py:151
  139.8 30.3 %collective-permute-start.10 = (bf16[256,2560]{1,0:T(8,128)(2,1)}, bf16[256,2560]{1,0:T(8,128)(2,1)S(1)}, u32[]{:S(2)}, u32[]{:S(2)}) collective-permute-start(bf16[256,2560]{1,0:T(8,128)(2,1)} %copy-done.16), channel_id=1, source_target_pairs={{0,8},{1,9},{2,10},{3,11},{4,12},{5,13},{6,14},{7,15},{8,0},{9,1},... | collective-permute-start | bytes 3932168 | tf_op jit(solution)/shard_map/ppermute | solution.py:151
  176.2 1.1 copy-start.22
  177.3 1.1 copy-start.25
  178.4 1.0 copy-start.28
  179.4 64.6 %reduce-scatter.11.cloned.1.call-start = ((), (), s32[]{:S(2)}) async-start(), calls=%async_computation.8 | async-start | bytes 1310720 | tf_op jit(solution)/shard_map/reduce_scatter | solution.py:232
  179.5 13.2 %collective-permute-start = (bf16[512,1280]{1,0:T(8,128)(2,1)}, bf16[512,1280]{1,0:T(8,128)(2,1)}, u32[]{:S(2)}, u32[]{:S(2)}) collective-permute-start(bf16[512,1280]{1,0:T(8,128)(2,1)} %get-tuple-element.6), channel_id=1, source_target_pairs={{0,1},{1,0},{2,3},{3,2},{4,5},{5,4},{6,7},{7,6},{8,9},{9,8},{10,11... | collective-permute-start | bytes 3932168 | tf_op jit(solution)/shard_map/ppermute | solution.py:151
  179.6 1.3 copy-start.23
  180.9 1.3 copy-start.26
  182.2 1.3 copy-start.29
  183.5 1.3 copy-start.32
  189.5 1.0 copy-start.3
  190.5 72.6 %reduce-scatter.9.cloned.1.call-start = ((), (), s32[]{:S(2)}) async-start(), calls=%async_computation.7 | async-start | bytes 2621440 | tf_op jit(solution)/shard_map/reduce_scatter | solution.py:232
  190.6 4.5 %collective-permute-start.1 = (bf16[512,1280]{1,0:T(8,128)(2,1)S(1)}, bf16[512,1280]{1,0:T(8,128)(2,1)S(1)}, u32[]{:S(2)}, u32[]{:S(2)}) collective-permute-start(bf16[512,1280]{1,0:T(8,128)(2,1)S(1)} %get-tuple-element.7), channel_id=1, source_target_pairs={{0,1},{1,0},{2,3},{3,2},{4,5},{5,4},{6,7},{7,6},{8,9},{9,8},{10,11... | collective-permute-start | bytes 3932168 | tf_op jit(solution)/shard_map/ppermute | solution.py:151
  192.6 2.5 copy-start.6
  192.7 2.7 copy-start.11
  192.7 3.0 copy-start.15
  192.7 3.4 copy-start.18
  196.1 9.0 %copy-start.27 = (bf16[256,2560]{1,0:T(8,128)(2,1)S(1)}, bf16[256,2560]{1,0:T(8,128)(2,1)}, u32[]{:S(2)}) copy-start(bf16[256,2560]{1,0:T(8,128)(2,1)} %copy-done.25) | copy-start | bytes 3932164
  203.6 1.5 copy-start.4
  205.1 1.3 copy-start.24
  205.1 90.5 %reduce-scatter.7.cloned.1.call-start = ((), (), s32[]{:S(2)}) async-start(), calls=%async_computation.6 | async-start | bytes 2621440 | tf_op jit(solution)/shard_map/reduce_scatter | solution.py:232
  206.4 1.7 copy-start.5
  208.1 1.7 copy-start.7
  209.9 1.3 copy-start.30
  220.7 4.5 %collective-permute-start.11 = (f32[136,128]{1,0:T(8,128)S(1)}, f32[136,128]{1,0:T(8,128)S(1)}, u32[]{:S(2)}, u32[]{:S(2)}) collective-permute-start(f32[136,128]{1,0:T(8,128)S(1)} %concatenate.31), channel_id=1, source_target_pairs={{0,32},{1,33},{2,34},{3,35},{4,36},{5,37},{6,38},{7,39},{8,40},{9,... | collective-permute-start | bytes 208904 | tf_op jit(solution)/shard_map/ppermute | solution.py:151
  225.3 4.4 %collective-permute-start.12 = (f32[136,128]{1,0:T(8,128)S(1)}, f32[136,128]{1,0:T(8,128)S(1)}, u32[]{:S(2)}, u32[]{:S(2)}) collective-permute-start(f32[136,128]{1,0:T(8,128)S(1)} %pad_add_fusion.1), channel_id=1, source_target_pairs={{0,96},{1,97},{2,98},{3,99},{4,100},{5,101},{6,102},{7,103},{8,104... | collective-permute-start | bytes 208904 | tf_op jit(solution)/shard_map/ppermute | solution.py:151
  229.7 4.4 %collective-permute-start.13 = (f32[136,128]{1,0:T(8,128)S(1)}, f32[136,128]{1,0:T(8,128)S(1)}, u32[]{:S(2)}, u32[]{:S(2)}) collective-permute-start(f32[136,128]{1,0:T(8,128)S(1)} %add.69), channel_id=1, source_target_pairs={{0,8},{1,9},{2,10},{3,11},{4,12},{5,13},{6,14},{7,15},{8,0},{9,1},... | collective-permute-start | bytes 208904 | tf_op jit(solution)/shard_map/ppermute | solution.py:151
  234.1 5.6 %collective-permute-start.14 = (f32[136,128]{1,0:T(8,128)S(1)}, f32[136,128]{1,0:T(8,128)S(1)}, u32[]{:S(2)}, u32[]{:S(2)}) collective-permute-start(f32[136,128]{1,0:T(8,128)S(1)} %add.70), channel_id=1, source_target_pairs={{0,24},{1,25},{2,26},{3,27},{4,28},{5,29},{6,30},{7,31},{8,16},{9,... | collective-permute-start | bytes 208904 | tf_op jit(solution)/shard_map/ppermute | solution.py:151
  298.7 5.6 %collective-permute-start.20 = (bf16[1024,512]{1,0:T(8,128)(2,1)}, bf16[1024,512]{1,0:T(8,128)(2,1)S(1)}, u32[]{:S(2)}, u32[]{:S(2)}) collective-permute-start(bf16[1024,512]{1,0:T(8,128)(2,1)} %get-tuple-element.14), channel_id=1, source_target_pairs={{1,24},{3,26},{5,28},{7,30},{9,16},{11,18},{13,20},{15,22},{16,9},... | collective-permute-start | bytes 3145736 | tf_op jit(solution)/shard_map/ppermute | solution.py:151
  299.4 27.2 %collective-permute-start.19 = (bf16[1024,512]{1,0:T(8,128)(2,1)}, bf16[1024,512]{1,0:T(8,128)(2,1)}, u32[]{:S(2)}, u32[]{:S(2)}) collective-permute-start(bf16[1024,512]{1,0:T(8,128)(2,1)} %get-tuple-element.15), channel_id=1, source_target_pairs={{0,24},{1,0},{2,26},{3,2},{4,28},{5,4},{6,30},{7,6},{8,16},{9,8},{... | collective-permute-start | bytes 3145736 | tf_op jit(solution)/shard_map/ppermute | solution.py:151
  (6 other events, 5.8 us)
Sparse Core Ops, SparseCore 0:
  85.4 25.6 reduce-scatter.16
  119.7 25.8 reduce-scatter.14
  179.5 26.0 reduce-scatter.12
  208.0 23.3 reduce-scatter.10
  233.7 29.3 reduce-scatter.8
  266.1 29.4 reduce-scatter.6

commit v2 on v1

v2 whole, which is shorter than its diff:
```python
import functools
import math

import jax
import jax.numpy as jnp
import numpy as np
from jax import lax
from jax.experimental import pallas as pl
from jax.experimental.pallas import tpu as pltpu
from jax.sharding import Mesh
from jax.sharding import PartitionSpec as P

learning_rate = 0.1

HD=128; GROUP=8; PREFIX=64; SEQ=512; QB=256
rope_base=500000.0

def rope_tables():
    half=HD//2
    freq=np.power(rope_base,-(2.0*np.arange(half))/HD).astype(np.float32)
    ang=(np.arange(SEQ,dtype=np.float32)[:,None]*freq[None,:]).astype(np.float64)
    cos,sin=np.cos(ang).astype(np.float32),np.sin(ang).astype(np.float32)
    wide_cos=np.concatenate([cos,cos],1)
    wide_sin=np.concatenate([sin,-sin],1)
    return cos.T.copy(),sin.T.copy(),wide_cos,wide_sin

NT=(((1,),(1,)),((),()))
NN=(((1,),(0,)),((),()))
def dot(a,b,dims): return lax.dot_general(a,b,dims,preferred_element_type=jnp.float32)

def attn_kernel(len_ref,q_ref,g_ref,k_ref,v_ref,pre_ref,cosT_ref,sinT_ref,cos_ref,sin_ref,out_ref,pg_ref,kj,vj,kT,dk_acc,dv_acc,*,prompt):
    h=pl.program_id(0)
    inverse=1.0/math.sqrt(HD)
    @pl.when(h==0)
    def _():
        kj[0:PREFIX,:]=pre_ref[0].astype(jnp.bfloat16)
        vj[0:PREFIX,:]=pre_ref[1].astype(jnp.bfloat16)
        kj[PREFIX:,:]=k_ref[...]
        vj[PREFIX:,:]=v_ref[...]
        kT[...]=jnp.transpose(kj[...].astype(jnp.float32)).astype(jnp.bfloat16)
        dk_acc[...]=jnp.zeros_like(dk_acc)
        dv_acc[...]=jnp.zeros_like(dv_acc)
    live=len_ref[prompt]
    col=pl.multiple_of(h*HD,HD)
    for b in range(SEQ//QB):
        r0=b*QB; nk=PREFIX+r0+QB
        q=q_ref[r0:r0+QB,:]
        rows=lax.broadcasted_iota(jnp.int32,(QB,HD),0)+r0
        g=jnp.where(rows<live,g_ref[r0:r0+QB,:].astype(jnp.float32),0.0).astype(jnp.bfloat16)
        s=dot(kj[0:nk,:],q,NT)
        dp=dot(vj[0:nk,:],g,NT)
        key=lax.broadcasted_iota(jnp.int32,(QB,QB),0)
        row=lax.broadcasted_iota(jnp.int32,(QB,QB),1)
        s=jnp.concatenate([s[:nk-QB],jnp.where(key<=row,s[nk-QB:],-1e30)],0)
        top=jnp.max(s,0,keepdims=True)
        e=jnp.exp((s-top)*inverse)
        p=e*(1.0/jnp.sum(e,0,keepdims=True))
        rt=jnp.sum(p*dp,0,keepdims=True)
        ds=(p*(dp-rt)).astype(jnp.bfloat16)
        pb=p.astype(jnp.bfloat16)
        dk_acc[0:nk,:]+=dot(ds,q,NN)
        dv_acc[0:nk,:]+=dot(pb,g,NN)
        dqT=dot(kT[:,0:nk],ds,NN)*inverse
        a=dqT[:HD//2]; c=dqT[HD//2:]
        co=cosT_ref[:,r0:r0+QB]; si=sinT_ref[:,r0:r0+QB]
        rot=jnp.concatenate([a*co+c*si,c*co-a*si],0)
        out_ref[r0:r0+QB,pl.ds(col,HD)]=jnp.transpose(rot).astype(jnp.bfloat16)
    @pl.when(h==GROUP-1)
    def _():
        dk=dk_acc[...]*inverse
        pg_ref[0]=dk[0:PREFIX]
        pg_ref[1]=dv_acc[0:PREFIX,:]
        d=dk[PREFIX:]
        out_ref[:,GROUP*HD:(GROUP+1)*HD]=(d*cos_ref[...]+pltpu.roll(d,HD//2,1)*sin_ref[...]).astype(jnp.bfloat16)
        out_ref[:,(GROUP+1)*HD:]=dv_acc[PREFIX:,:].astype(jnp.bfloat16)

def attention(prompt,lengths,queries,out_grad,key_rows,value_rows,prefix,tables):
    whole=lambda shape: pl.BlockSpec(shape,lambda h:(0,)*len(shape))
    return pl.pallas_call(
        functools.partial(attn_kernel,prompt=prompt),
        grid=(GROUP,),
        in_specs=[pl.BlockSpec(memory_space=pltpu.SMEM),
            pl.BlockSpec((SEQ,HD),lambda h:(prompt,h)),
            pl.BlockSpec((SEQ,HD),lambda h:(prompt,h)),
            pl.BlockSpec((SEQ,HD),lambda h:(prompt,0)),
            pl.BlockSpec((SEQ,HD),lambda h:(prompt,0)),
            whole((2,PREFIX,HD)),whole((HD//2,SEQ)),whole((HD//2,SEQ)),whole((SEQ,HD)),whole((SEQ,HD))],
        out_specs=[whole((SEQ,(GROUP+2)*HD)),whole((2,PREFIX,HD))],
        out_shape=[jax.ShapeDtypeStruct((SEQ,(GROUP+2)*HD),jnp.bfloat16),jax.ShapeDtypeStruct((2,PREFIX,HD),jnp.float32)],
        scratch_shapes=[pltpu.VMEM((PREFIX+SEQ,HD),jnp.bfloat16),pltpu.VMEM((PREFIX+SEQ,HD),jnp.bfloat16),pltpu.VMEM((HD,PREFIX+SEQ),jnp.bfloat16),
            pltpu.VMEM((PREFIX+SEQ,HD),jnp.float32),pltpu.VMEM((PREFIX+SEQ,HD),jnp.float32)],
        compiler_params=pltpu.CompilerParams(vmem_limit_bytes=58*2**20),
        cost_estimate=pl.CostEstimate(flops=5*2*8*512*576*128,bytes_accessed=4*2**20,transcendentals=8*512*576),
        name="attention_backward",
    )(lengths,queries,out_grad,key_rows,value_rows,prefix,*tables)

AXES = ("x", "y", "z", "c")


def pairs_of(move):
    def flat(x, y, z, c):
        return ((x * 4 + y) * 4 + z) * 2 + c

    found = []
    for x in range(4):
        for y in range(4):
            for z in range(4):
                for c in range(2):
                    target = move(x, y, z, c)
                    if target is not None:
                        found.append((flat(x, y, z, c), flat(*target)))
    return found


def send(array, move):
    return lax.ppermute(array, AXES, pairs_of(move))


def x_mate(x, y, z, c):
    return (x ^ 1, y, z, c)


def x_cross(x, y, z, c):
    return (3 - x, y, z, c)


def x_side(x, y, z, c):
    return (x ^ 1 if c == 0 else 3 - x, y, z, c)


def x_side_other(x, y, z, c):
    return (x ^ 1 if c == 1 else 3 - x, y, z, 1 - c)


def x_turn(x, y, z, c):
    return (3 - x if c == 0 else x ^ 1, y, z, c)


def y_mate(x, y, z, c):
    return (x, y ^ 1, z, c)


def y_partner(x, y, z, c):
    return (x, 3 - y, z, c)


def z_side(x, y, z, c):
    return (x, y, z ^ 1 if c == 0 else 3 - z, c)


def z_turn(x, y, z, c):
    return (x, y, 3 - z if c == 0 else z ^ 1, c)


def sibling(x, y, z, c):
    return (x, y, z, 1 - c)


def home_same(x, y, z, c):
    return (x, 3 - y, z, c) if c == y // 2 else None


def home_other(x, y, z, c):
    return (x, 3 - y, z, 1 - c) if c != y // 2 else None


def project_kernel(plan, n_arrays, *refs):
    sides, groups, outs_of = plan
    arrays, rest = refs[:n_arrays], refs[n_arrays:]
    outs, left, right, made, sems = rest[:outs_of], *rest[outs_of:]
    width = right.shape[-1]
    sem = iter(range(sems.shape[0]))

    def begin(source, target):
        copy = pltpu.make_async_copy(source, target, sems.at[next(sem)])
        copy.start()
        return copy

    side_loads = [
        [begin(arrays[at], left.at[n, :, part * width : (part + 1) * width]) for part, at in enumerate(side)]
        for n, side in enumerate(sides)
    ]
    block_loads = []
    for blocks, _ in groups:
        for pair in blocks:
            slot = len(block_loads)
            block_loads.append(
                [begin(arrays[at].at[row : row + right.shape[2]], right.at[slot, part]) for part, (at, row) in enumerate(pair)]
            )
    ready, stores, slot = set(), [], 0
    for blocks, units in groups:
        for index in range(len(blocks)):
            for copy in block_loads[slot]:
                copy.wait()
            for side, places, out, row in units:
                if side not in ready:
                    ready.add(side)
                    for copy in side_loads[side]:
                        copy.wait()
                total = dot(left[side, :, :width], right[slot, 0], NT) + dot(left[side, :, width:], right[slot, 1], NT)
                at = len(stores)
                made[at] = total.astype(jnp.bfloat16)
                place = arrays[places][index]
                stores.append(begin(made.at[at], outs[out].at[place, row : row + total.shape[0]]))
            slot += 1
    for copy in stores:
        copy.wait()


def project(groups, cols=256):
    arrays, kinds = [], []

    def slot_of(array, kind):
        for at, known in enumerate(arrays):
            if known is array:
                return at
        arrays.append(array)
        kinds.append(kind)
        return len(arrays) - 1

    sides, plan, out_rows = [], [], {}
    for blocks, units in groups:
        pairs = [tuple((slot_of(array, pl.ANY), row) for array, row in pair) for pair in blocks]
        done = []
        for (own, other), places, out, row in units:
            side = (slot_of(own, pl.ANY), slot_of(other, pl.ANY))
            if side not in sides:
                sides.append(side)
            out_rows[out] = max(out_rows.get(out, 0), row + own.shape[0])
            done.append((sides.index(side), slot_of(places, pltpu.SMEM), out, row))
        plan.append((pairs, done))
    rows, width = arrays[sides[0][0]].shape
    n_blocks = sum(len(blocks) for blocks, _ in plan)
    n_out = sum(len(blocks) * len(units) for blocks, units in plan)
    return pl.pallas_call(
        functools.partial(project_kernel, (sides, plan, len(out_rows)), len(arrays)),
        in_specs=[pl.BlockSpec(memory_space=kind) for kind in kinds],
        out_specs=[pl.BlockSpec(memory_space=pl.ANY)] * len(out_rows),
        out_shape=[jax.ShapeDtypeStruct((4, out_rows[at], cols), jnp.bfloat16) for at in sorted(out_rows)],
        scratch_shapes=[
            pltpu.VMEM((len(sides), rows, 2 * width), jnp.bfloat16),
            pltpu.VMEM((n_blocks, 2, cols, width), jnp.bfloat16),
            pltpu.VMEM((n_out, rows, cols), jnp.bfloat16),
            pltpu.SemaphoreType.DMA((2 * len(sides) + 2 * n_blocks + n_out,)),
        ],
        compiler_params=pltpu.CompilerParams(vmem_limit_bytes=58 * 2**20),
        name="project",
    )(*arrays)


def arrange_kernel(info, near, mate, near_in, mate_in, same0, same1, other0, other1, out_ref):
    at_home, near_at, own_at = info[0], info[1], info[2]
    size = near.shape[1]

    def put(value, row, base, core_at):
        col = pl.multiple_of(base * 512 + core_at * 256, 256)
        out_ref[row * size : (row + 1) * size, pl.ds(col, 256)] = value

    @pl.when(at_home == 1)
    def _():
        for row in range(2):
            put(near[row], row, near_at, own_at)
            put(mate[row], row, 1 - near_at, own_at)
            put(near_in[row], row, near_at, 1 - own_at)
            put(mate_in[row], row, 1 - near_at, 1 - own_at)

    @pl.when(at_home == 0)
    def _():
        for row, (same, other) in enumerate(((same0, other0), (same1, other1))):
            put(same[0], row, near_at, own_at)
            put(same[1], row, 1 - near_at, own_at)
            put(other[0], row, near_at, 1 - own_at)
            put(other[1], row, 1 - near_at, 1 - own_at)


def arrange(info, *parts):
    vmem = pl.BlockSpec(memory_space=pltpu.VMEM)
    return pl.pallas_call(
        arrange_kernel,
        in_specs=[pl.BlockSpec(memory_space=pltpu.SMEM)] + [vmem] * 8,
        out_specs=vmem,
        out_shape=jax.ShapeDtypeStruct((1024, 1024), jnp.bfloat16),
        compiler_params=pltpu.CompilerParams(vmem_limit_bytes=58 * 2**20),
        name="arrange",
    )(info, *parts)


def wide(array):
    return array.astype(jnp.float32)


def body(queries, key_rows, value_rows, out_grad, prefix, lengths, qkv_weight):
    gate = lax.optimization_barrier
    x_at, y_at, z_at, core = (lax.axis_index(a) for a in AXES)
    half = y_at // 2
    rows = qkv_weight.shape[0] // 2
    tables = tuple(jnp.asarray(t) for t in rope_tables())
    x_first, x_second = jnp.where(core == 0, x_at ^ 1, 3 - x_at), jnp.where(core == 0, 3 - x_at, x_at ^ 1)
    z_first, z_second = jnp.where(core == 0, z_at ^ 1, 3 - z_at), jnp.where(core == 0, 3 - z_at, z_at ^ 1)
    targets = jnp.stack([x_at, x_first, x_second, x_at ^ 2]).astype(jnp.int32)
    places = jnp.where(
        targets == z_at, 0, jnp.where(targets == z_second, 1, jnp.where(targets == z_first, 2, 3))
    ).astype(jnp.int32)

    kept = lax.dynamic_slice_in_dim(qkv_weight, core * rows, rows, 0)
    given = lax.dynamic_slice_in_dim(qkv_weight, (1 - core) * rows, rows, 0)
    kept, given, places = gate((kept, given, places))

    side_a = send(kept, x_side)
    side_b = send(given, x_side_other)
    taken = send(given, sibling)
    self0, terms0 = attention(0, lengths, queries, out_grad, key_rows, value_rows, prefix, tables)
    side_a, side_b, taken, self0, terms0, key_rows, kept = gate((side_a, side_b, taken, self0, terms0, key_rows, kept))
    mine = jnp.concatenate([kept, taken], 0)
    turned = send(jnp.concatenate([kept, taken, side_a, side_b], 0), x_turn)
    mate = send(mine, y_mate)
    pair0 = send(self0, y_partner)
    self0_other = send(self0, sibling)
    self1, terms1 = attention(1, lengths, queries, out_grad, key_rows, value_rows, prefix, tables)
    count_row = jnp.full((8, HD), jnp.sum(lengths).astype(jnp.float32))
    turned, mate, pair0, self0_other, self1, terms1, terms0, mine, self0 = gate(
        (turned, mate, pair0, self0_other, self1, terms1, terms0, mine, self0)
    )
    terms = jnp.concatenate([(terms0 + terms1).reshape(2 * PREFIX, HD), count_row], 0)
    near_blocks = [
        ((mine, 0), (mine, rows)),
        ((side_a, 0), (side_b, 0)),
        ((turned, 0), (turned, rows)),
        ((turned, 2 * rows), (turned, 3 * rows)),
    ]

    def start_unit(partial):
        return partial, send(partial[2:], z_side)

    def pass_on(held):
        partial, arrived = held
        total = (wide(partial[1]) + wide(arrived[1])).astype(jnp.bfloat16)
        return partial, arrived, send(total, z_turn)

    def finish(held):
        partial, arrived, last = held
        return ((wide(partial[0]) + wide(arrived[0]) + wide(last)) * loss_scale).astype(jnp.bfloat16)

    self1_other = send(self1, sibling)
    pair0_other = send(pair0, sibling)
    mate_side = send(mate, x_side)
    mate_turn = send(mate, x_turn)
    mate_far = send(turned[2 * rows :], y_mate)
    pair1 = send(self1, y_partner)
    both0, both1, there0 = (self0, self0_other), (self1, self1_other), (pair0, pair0_other)
    sn, p0n = project([(near_blocks, [(both0, places, 0, 0), (both1, places, 0, SEQ), (there0, places, 1, 0)])])
    mate_side, mate_turn, mate_far, pair1, there0, both0, both1, sn, p0n, mate, terms = gate(
        (mate_side, mate_turn, mate_far, pair1, there0, both0, both1, sn, p0n, mate, terms)
    )
    mate_blocks = [((array, 0), (array, rows)) for array in (mate, mate_side, mate_turn, mate_far)]
    pair1_other = send(pair1, sibling)
    sn, p0n = start_unit(sn), start_unit(p0n)
    terms = terms + send(terms, x_mate)
    p0m, sm = project([(mate_blocks, [(there0, places, 0, 0), (both0, places, 1, 0), (both1, places, 1, SEQ)])])
    pair1_other, sn, p0n, p0m, pair1, terms, sm = gate((pair1_other, sn, p0n, p0m, pair1, terms, sm))
    sn, p0n, p0m = pass_on(sn), pass_on(p0n), start_unit(p0m)
    there1 = (pair1, pair1_other)
    terms = terms + send(terms, x_cross)
    p1 = project([(near_blocks, [(there1, places, 0, 0)]), (mate_blocks, [(there1, places, 0, SEQ)])])[0]
    sn, p0n, p0m, p1, terms, sm = gate((sn, p0n, p0m, p1, terms, sm))
    p0m, p1 = pass_on(p0m), start_unit(p1)
    terms = terms + send(terms, y_mate)
    terms = terms + send(terms, y_partner)
    p0m, p1, terms, p0n, sn, sm = gate((p0m, p1, terms, p0n, sn, sm))
    loss_scale = 16384.0 / terms[2 * PREFIX, 0]
    p1, sm = pass_on(p1), start_unit(sm)
    near = finish(sn).reshape(2, SEQ, 256)
    pair0 = jnp.stack([finish(p0n), finish(p0m)])
    same0, other0 = send(pair0, home_same), send(pair0, home_other)
    near_in = send(near, sibling)
    near_in, same0, other0, p1, sm, loss_scale, near = gate((near_in, same0, other0, p1, sm, loss_scale, near))
    pair1 = finish(p1).reshape(2, SEQ, 256)
    same1, other1 = send(pair1, home_same), send(pair1, home_other)
    sm = pass_on(sm)
    mate = finish(sm).reshape(2, SEQ, 256)
    mate_in = send(mate, sibling)
    at_home = core == half
    near_at = jnp.where(at_home, y_at % 2, 1 - y_at % 2)
    info = jnp.stack([at_home.astype(jnp.int32), near_at, core]).astype(jnp.int32)
    input_grad = arrange(info, near, mate, near_in, mate_in, same0, same1, other0, other1)
    new_prefix = prefix - learning_rate * loss_scale * terms[: 2 * PREFIX].reshape(2, PREFIX, HD)
    return (input_grad, new_prefix)


def solution(mesh):
    fine = Mesh(mesh.devices.reshape(4, 4, 4, 2), AXES)
    dp, tensor = ("x", "y"), ("z", "c")
    both = P(dp, tensor)
    return jax.shard_map(
        body,
        mesh=fine,
        in_specs=(both, both, both, both, P(None, None, tensor), P(dp), both),
        out_specs=(both, P(None, None, tensor)),
        check_vma=False,
    )
```

time: 348 us -> 222 us (0.64)
  waiting for transfers between devices: 185 us -> 62.5 us
  local copies, waits for them, and re-layouts: 45.7 us -> 11.7 us
  Pallas kernels: 59.7 us -> 84.2 us
  starting transfers between devices: 24.4 us -> 43.5 us
  between operations: 16 us -> 2.54 us
    ppermute x21 -> x34, waiting for transfers between devices: 135 us -> 62.5 us  [send(): return lax.ppermute(array, AXES, pairs_of(move))]
    reduce_scatter x6 -> x0, waiting for transfers between devices: 50.4 us -> none  [reduced(): summed = lax.psum_scatter(partial, 'z', scatter_dimension=0, tiled=True)[0]]
    unnamed x89 -> x47, local copies, waits for them, and re-layouts: 33.7 us -> 1.72 us
    pallas_call x6 -> x4, Pallas kernels: 34.3 us -> 56.7 us  [the longest x3 53 us: project(): pl.pallas_call(functools.partial(project_kernel, (sides, plan, len(out_ro...]
    ppermute x21 -> x34, starting transfers between devices: 24.2 us -> 43.5 us  [send(): return lax.ppermute(array, AXES, pairs_of(move))]
    slice x2 -> x6, local copies, waits for them, and re-layouts: 1.95 us -> 8.06 us  [the longest x5 6.77 us: start_unit(): return (partial, send(partial[2:], z_side))]
    another operation x3 -> x0, local copies, waits for them, and re-layouts: 3.81 us -> none  [body(): jnp.stack([zero.reshape(1024, 2, 256), one.reshape(1024, 2, 256)], 2)]
  transfers between devices with their start and end apart: 27 -> 34, of which waited for: 17 -> 15; matrix products, arithmetic and copies ran while one was open for 4% -> 6% of each run, Pallas kernels for 17% -> 37%
where the time goes in v2:
time: 222 us; the launch traced here: 218 us
  Pallas kernels  84.2 us (38%)
  waiting for transfers between devices  62.5 us (28%)
  starting transfers between devices  43.5 us (20%)
  other arithmetic  13.2 us (6%)
  local copies, waits for them, and re-layouts  11.7 us (5%)
  between operations  2.54 us (1%)
    ppermute x34, waiting for transfers between devices, send(): return lax.ppermute(array, AXES, pairs_of(move))  62.5 us
    pallas_call x3, Pallas kernels, project(): pl.pallas_call(functools.partial(project_kernel, (sides, plan, len(out_ro...  53 us
    ppermute x34, starting transfers between devices, send(): return lax.ppermute(array, AXES, pairs_of(move))  43.5 us
    pallas_call x2, Pallas kernels, attention(): pl.pallas_call(functools.partial(attn_kernel, prompt=prompt), grid=(GROUP...  27.5 us
    slice x5, local copies, waits for them, and re-layouts, start_unit(): return (partial, send(partial[2:], z_side))  6.77 us
  transfers between devices with their start and end apart: 34, of which 15 were waited for; matrix products, arithmetic and copies ran while one was open for 6% of the time, Pallas kernels for 37%

profile of v2, /device:TPU:2, one launch (start us, length us, event | category | flops | bytes accessed | tf_op | source)
XLA Modules:
  0.0 217.7 jit_solution(12446963225786227785)
XLA Ops:
  0.7 1.4 constant_dynamic-slice_fusion
  2.0 0.6 compare_select_fusion.2.refs_6_
  3.1 0.6 collective-permute-start.2
  3.7 1.8 collective-permute-start.1
  5.4 13.8 %attention_backward.2 = (bf16[512,1280]{1,0:T(8,128)(2,1)}, f32[2,64,128]{2,1,0:T(8,128)}) custom-call(s32[2]{0:T(128)} %len_ref.3, bf16[1024,1024]{1,0:T(8,128)(2,1)} %q_ref.3, bf16[1024,1024]{1,0:T(8,128)(2,1)} %g_ref.3, bf16[1024,128]{1,0:T(8,128)(2,1)} %k_ref.2, bf16[1024,128]{1,0:T(8,128)(2,1)} %v_ref.3, f32[2,64,128]{2,1,0:T(8,128)} %pre_ref.3, ...), custom_call_target="tpu_custom_call" | custom-call | flops 3019898880 | bytes 4194304 | tf_op jit(solution)/shard_map/attention_backward/pallas_call | solution.py:79
  19.2 0.6 collective-permute-done.refs_1_
  20.2 1.7 pad_maximum_fusion
  22.0 1.5 collective-permute-start.3
  23.6 1.7 collective-permute-start.4
  25.2 2.2 %collective-permute-start.5 = (bf16[512,1280]{1,0:T(8,128)(2,1)}, bf16[512,1280]{1,0:T(8,128)(2,1)}, u32[]{:S(2)}, u32[]{:S(2)}) collective-permute-start(bf16[512,1280]{1,0:T(8,128)(2,1)} %get-tuple-element.120.refs_4_.refs_7_), channel_id=1, source_target_pairs={{0,24},{1,25},{2,26},{3,27},{4,28},{5,29},{6,30},{7,31},{8,16},{9,... | collective-permute-start | bytes 3932168 | tf_op jit(solution)/shard_map/ppermute | solution.py:116
  27.4 13.8 %attention_backward.3 = (bf16[512,1280]{1,0:T(8,128)(2,1)}, f32[2,64,128]{2,1,0:T(8,128)}) custom-call(s32[2]{0:T(128)} %len_ref.3, bf16[1024,1024]{1,0:T(8,128)(2,1)} %q_ref.3, bf16[1024,1024]{1,0:T(8,128)(2,1)} %g_ref.3, bf16[1024,128]{1,0:T(8,128)(2,1)} %k_ref.2, bf16[1024,128]{1,0:T(8,128)(2,1)} %v_ref.3, f32[2,64,128]{2,1,0:T(8,128)} %pre_ref.3, ...), custom_call_target="tpu_custom_call" | custom-call | flops 3019898880 | bytes 4194304 | tf_op jit(solution)/shard_map/attention_backward/pallas_call | solution.py:79
  41.2 11.7 %collective-permute-done.4.refs_0_.refs_7_ = bf16[512,1280]{1,0:T(8,128)(2,1)} collective-permute-done((bf16[512,1280]{1,0:T(8,128)(2,1)S(1)}, bf16[512,1280]{1,0:T(8,128)(2,1)}, u32[]{:S(2)}, u32[]{:S(2)}) %collective-permute-start.4) | collective-permute-done | bytes 1310752 | tf_op jit(solution)/shard_map/ppermute | solution.py:116
  52.9 5.0 %collective-permute-done.5.refs_9_.refs_4_ = bf16[512,1280]{1,0:T(8,128)(2,1)} collective-permute-done((bf16[512,1280]{1,0:T(8,128)(2,1)}, bf16[512,1280]{1,0:T(8,128)(2,1)}, u32[]{:S(2)}, u32[]{:S(2)}) %collective-permute-start.5) | collective-permute-done | bytes 1310752 | tf_op jit(solution)/shard_map/ppermute | solution.py:116
  58.5 1.3 slice.84
  59.8 0.5 collective-permute-start.8
  60.4 1.8 collective-permute-start.7
  62.2 2.2 %collective-permute-start.10 = (bf16[512,1280]{1,0:T(8,128)(2,1)}, bf16[512,1280]{1,0:T(8,128)(2,1)}, u32[]{:S(2)}, u32[]{:S(2)}) collective-permute-start(bf16[512,1280]{1,0:T(8,128)(2,1)} %get-tuple-element.122.refs_7_.refs_9_), channel_id=1, source_target_pairs={{0,24},{1,25},{2,26},{3,27},{4,28},{5,29},{6,30},{7,31},{8,16},{9,... | collective-permute-start | bytes 3932168 | tf_op jit(solution)/shard_map/ppermute | solution.py:116
  64.4 0.7 reduce_sum.9
  65.9 18.5 %project.3 = (bf16[4,1024,256]{2,1,0:T(8,128)(2,1)}, bf16[4,512,256]{2,1,0:T(8,128)(2,1)}) custom-call(bf16[512,1280]{1,0:T(8,128)(2,1)} %copy-done.2, bf16[256,1280]{1,0:T(8,128)(2,1)} %copy-done.3, bf16[256,1280]{1,0:T(8,128)(2,1)} %copy-done.4, bf16[1024,1280]{1,0:T(8,128)(2,1)} %copy-done, bf16[512,1280]{1,0:T(8,128)(2,1)} %get-tuple-element.120.refs_4_.refs_7_, ...), custom_call_target="tpu_custom_call" | custom-call | tf_op jit(solution)/shard_map/project/pallas_call | solution.py:235
  84.4 6.3 %collective-permute-done.9.refs_3_.refs_10_ = bf16[512,1280]{1,0:T(8,128)(2,1)} collective-permute-done((bf16[512,1280]{1,0:T(8,128)(2,1)}, bf16[512,1280]{1,0:T(8,128)(2,1)}, u32[]{:S(2)}, u32[]{:S(2)}) %collective-permute-start.9) | collective-permute-done | bytes 1310752 | tf_op jit(solution)/shard_map/ppermute | solution.py:116
  90.8 0.6 collective-permute-done.8.refs_2_.refs_9_
  91.4 2.4 %collective-permute-done.10.refs_4_ = bf16[512,1280]{1,0:T(8,128)(2,1)} collective-permute-done((bf16[512,1280]{1,0:T(8,128)(2,1)}, bf16[512,1280]{1,0:T(8,128)(2,1)}, u32[]{:S(2)}, u32[]{:S(2)}) %collective-permute-start.10) | collective-permute-done | bytes 1310752 | tf_op jit(solution)/shard_map/ppermute | solution.py:116
  93.8 2.3 %slice.85 = bf16[2,1024,256]{2,1,0:T(8,128)(2,1)} slice(bf16[4,1024,256]{2,1,0:T(8,128)(2,1)} %get-tuple-element.147), slice={[2:4], [0:1024], [0:256]} | slice | bytes 2097152 | tf_op jit(solution)/shard_map/slice | solution.py:333
  96.0 1.9 collective-permute-start.14
  97.9 0.9 slice.86
  98.9 1.8 collective-permute-start.16
  100.7 18.5 %project.4 = (bf16[4,512,256]{2,1,0:T(8,128)(2,1)}, bf16[4,1024,256]{2,1,0:T(8,128)(2,1)}) custom-call(bf16[512,1280]{1,0:T(8,128)(2,1)} %collective-permute-done.4.refs_0_.refs_7_, bf16[512,1280]{1,0:T(8,128)(2,1)} %collective-permute-done.7.refs_1_.refs_8_, bf16[512,1280]{1,0:T(8,128)(2,1)} %collective-permute-done.8.refs_2_.refs_9_, ...), custom_call_target="tpu_custom_call" | custom-call | tf_op jit(solution)/shard_map/project/pallas_call | solution.py:235
  119.3 0.9 add.98
  120.2 2.2 %slice.91 = bf16[2,512,256]{2,1,0:T(8,128)(2,1)} slice(bf16[4,512,256]{2,1,0:T(8,128)(2,1)} %get-tuple-element.154), slice={[2:4], [0:512], [0:256]} | slice | bytes 1048576 | tf_op jit(solution)/shard_map/slice | solution.py:333
  122.4 1.9 collective-permute-start.19
  124.4 0.9 fusion.6
  125.3 2.5 %collective-permute-start.17 = (bf16[1024,256]{1,0:T(8,128)(2,1)}, bf16[1024,256]{1,0:T(8,128)(2,1)}, u32[]{:S(2)}, u32[]{:S(2)}) collective-permute-start(bf16[1024,256]{1,0:T(8,128)(2,1)} %fusion.6), channel_id=1, source_target_pairs={{0,6},{1,3},{2,4},{3,1},{4,2},{5,7},{6,0},{7,5},{8,14},{9,11},{10,... | collective-permute-start | bytes 1572872 | tf_op jit(solution)/shard_map/ppermute | solution.py:116
  127.9 0.8 fusion.13
  128.7 0.7 collective-permute-start.18
  129.4 0.6 collective-permute-start.20
  130.0 15.9 %project.5 = bf16[4,1024,256]{2,1,0:T(8,128)(2,1)} custom-call(bf16[512,1280]{1,0:T(8,128)(2,1)} %copy-done.2, bf16[256,1280]{1,0:T(8,128)(2,1)} %copy-done.3, bf16[256,1280]{1,0:T(8,128)(2,1)} %copy-done.4, bf16[1024,1280]{1,0:T(8,128)(2,1)} %copy-done, bf16[512,1280]{1,0:T(8,128)(2,1)} %collective-permute-done.10.refs_4_, bf16[512,1280]{1,0:T(8,128)(2,1)} %copy-done.10, ...), custom_call_target="tpu_custom_call" | custom-call | tf_op jit(solution)/shard_map/project/pallas_call | solution.py:235
  145.9 1.0 add.101
  147.0 1.3 slice.94
  148.6 1.2 fusion.14
  149.8 2.7 %collective-permute-start.21 = (bf16[512,256]{1,0:T(8,128)(2,1)S(1)}, bf16[512,256]{1,0:T(8,128)(2,1)S(1)}, u32[]{:S(2)}, u32[]{:S(2)}) collective-permute-start(bf16[512,256]{1,0:T(8,128)(2,1)S(1)} %fusion.14), channel_id=1, source_target_pairs={{0,6},{1,3},{2,4},{3,1},{4,2},{5,7},{6,0},{7,5},{8,14},{9,11},{10,... | collective-permute-start | bytes 786440 | tf_op jit(solution)/shard_map/ppermute | solution.py:116
  152.5 0.5 collective-permute-start.23
  153.0 3.8 %collective-permute-done.23 = f32[136,128]{1,0:T(8,128)S(1)} collective-permute-done((f32[136,128]{1,0:T(8,128)S(1)}, f32[136,128]{1,0:T(8,128)S(1)}, u32[]{:S(2)}, u32[]{:S(2)}) %collective-permute-start.23) | collective-permute-done | bytes 69664 | tf_op jit(solution)/shard_map/ppermute | solution.py:116
  156.8 2.3 %collective-permute-start.24 = (f32[136,128]{1,0:T(8,128)S(1)}, f32[136,128]{1,0:T(8,128)S(1)}, u32[]{:S(2)}, u32[]{:S(2)}) collective-permute-start(f32[136,128]{1,0:T(8,128)S(1)} %add.103), channel_id=1, source_target_pairs={{0,24},{1,25},{2,26},{3,27},{4,28},{5,29},{6,30},{7,31},{8,16},{9,... | collective-permute-start | bytes 208904 | tf_op jit(solution)/shard_map/ppermute | solution.py:116
  159.1 3.3 %collective-permute-done.24 = f32[136,128]{1,0:T(8,128)S(1)} collective-permute-done((f32[136,128]{1,0:T(8,128)S(1)}, f32[136,128]{1,0:T(8,128)S(1)}, u32[]{:S(2)}, u32[]{:S(2)}) %collective-permute-start.24) | collective-permute-done | bytes 69664 | tf_op jit(solution)/shard_map/ppermute | solution.py:116
  162.4 3.5 %collective-permute-done.22 = bf16[2,1024,256]{2,1,0:T(8,128)(2,1)S(1)} collective-permute-done((bf16[2,1024,256]{2,1,0:T(8,128)(2,1)S(1)}, bf16[2,1024,256]{2,1,0:T(8,128)(2,1)S(1)}, u32[]{:S(2)}, u32[]{:S(2)}) %collective-permute-start.22) | collective-permute-done | bytes 1048608 | tf_op jit(solution)/shard_map/ppermute | solution.py:116
  167.2 1.3 fusion.15
  168.5 0.8 collective-permute-start.27
  169.3 6.7 %collective-permute-start.26 = (bf16[2,512,256]{2,1,0:T(8,128)(2,1)S(1)}, bf16[2,512,256]{2,1,0:T(8,128)(2,1)S(1)}, u32[]{:S(2)}, u32[]{:S(2)}) collective-permute-start(bf16[2,512,256]{2,1,0:T(8,128)(2,1)S(1)} %pad_maximum_fusion.1), channel_id=1, source_target_pairs={{0,24},{2,26},{4,28},{6,30},{8,16},{10,18},{12,20},{14,22},{17,9},... | collective-permute-start | bytes 1572872 | tf_op jit(solution)/shard_map/ppermute | solution.py:116
  176.4 1.6 collective-permute-start.28
  178.0 1.3 fusion.5
  179.4 5.1 %collective-permute-done.26.same0 = bf16[2,512,256]{2,1,0:T(8,128)(2,1)S(1)} collective-permute-done((bf16[2,512,256]{2,1,0:T(8,128)(2,1)S(1)}, bf16[2,512,256]{2,1,0:T(8,128)(2,1)S(1)}, u32[]{:S(2)}, u32[]{:S(2)}) %collective-permute-start.26) | collective-permute-done | bytes 524320 | tf_op jit(solution)/shard_map/ppermute | solution.py:116
  184.4 8.1 %collective-permute-done.28 = bf16[1024,256]{1,0:T(8,128)(2,1)S(1)} collective-permute-done((bf16[1024,256]{1,0:T(8,128)(2,1)S(1)}, bf16[1024,256]{1,0:T(8,128)(2,1)S(1)}, u32[]{:S(2)}, u32[]{:S(2)}) %collective-permute-start.28) | collective-permute-done | bytes 524320 | tf_op jit(solution)/shard_map/ppermute | solution.py:116
  192.5 3.6 %collective-permute-done.29 = bf16[2,1024,256]{2,1,0:T(8,128)(2,1)S(1)} collective-permute-done((bf16[2,1024,256]{2,1,0:T(8,128)(2,1)S(1)}, bf16[2,1024,256]{2,1,0:T(8,128)(2,1)S(1)}, u32[]{:S(2)}, u32[]{:S(2)}) %collective-permute-start.29) | collective-permute-done | bytes 1048608 | tf_op jit(solution)/shard_map/ppermute | solution.py:116
  196.3 0.8 collective-permute-start.30
  197.1 1.0 fusion.1
  198.2 0.7 collective-permute-start.33
  198.9 3.9 %collective-permute-start.32 = (bf16[2,512,256]{2,1,0:T(8,128)(2,1)}, bf16[2,512,256]{2,1,0:T(8,128)(2,1)S(1)}, u32[]{:S(2)}, u32[]{:S(2)}) collective-permute-start(bf16[2,512,256]{2,1,0:T(8,128)(2,1)} %bitcast.23), channel_id=1, source_target_pairs={{0,24},{2,26},{4,28},{6,30},{8,16},{10,18},{12,20},{14,22},{17,9},... | collective-permute-start | bytes 1572872 | tf_op jit(solution)/shard_map/ppermute | solution.py:116
  202.7 4.1 %collective-permute-done.30 = bf16[1024,256]{1,0:T(8,128)(2,1)S(1)} collective-permute-done((bf16[1024,256]{1,0:T(8,128)(2,1)S(1)}, bf16[1024,256]{1,0:T(8,128)(2,1)S(1)}, u32[]{:S(2)}, u32[]{:S(2)}) %collective-permute-start.30) | collective-permute-done | bytes 524320 | tf_op jit(solution)/shard_map/ppermute | solution.py:116
  207.2 0.6 pad_add_fusion.info
  207.8 0.6 sub.26
  208.5 3.8 %collective-permute-done.32.same1 = bf16[2,512,256]{2,1,0:T(8,128)(2,1)S(1)} collective-permute-done((bf16[2,512,256]{2,1,0:T(8,128)(2,1)}, bf16[2,512,256]{2,1,0:T(8,128)(2,1)S(1)}, u32[]{:S(2)}, u32[]{:S(2)}) %collective-permute-start.32) | collective-permute-done | bytes 524320 | tf_op jit(solution)/shard_map/ppermute | solution.py:116
  212.3 0.8 copy-done.17
  213.1 0.8 copy-done.18
  213.9 3.8 %arrange.1 = bf16[1024,1024]{1,0:T(8,128)(2,1)} custom-call(s32[3]{0:T(128)} %pad_add_fusion.info, bf16[2,512,256]{2,1,0:T(8,128)(2,1)} %bitcast.62, bf16[2,512,256]{2,1,0:T(8,128)(2,1)} %bitcast.64, bf16[2,512,256]{2,1,0:T(8,128)(2,1)} %copy-done.15, bf16[2,512,256]{2,1,0:T(8,128)(2,1)} %copy-done.18, bf16[2,512,256]{2,1,0:T(8,128)(2,1)} %copy-done.14, ...), custom_call_target="tpu_custom_call" | custom-call | tf_op jit(solution)/shard_map/arrange/pallas_call | solution.py:278
  (88 shorter events, 3.6 us)
Async XLA Ops:
  2.6 17.2 %collective-permute-start = (bf16[256,1280]{1,0:T(8,128)(2,1)S(1)}, bf16[256,1280]{1,0:T(8,128)(2,1)S(1)}, u32[]{:S(2)}, u32[]{:S(2)}) collective-permute-start(bf16[256,1280]{1,0:T(8,128)(2,1)S(1)} %get-tuple-element.90), channel_id=1, source_target_pairs={{0,32},{1,97},{2,34},{3,99},{4,36},{5,101},{6,38},{7,103},{8,40},{... | collective-permute-start | bytes 1966088 | tf_op jit(solution)/shard_map/ppermute | solution.py:116
  3.1 16.8 %collective-permute-start.2 = (bf16[256,1280]{1,0:T(8,128)(2,1)S(1)}, bf16[256,1280]{1,0:T(8,128)(2,1)S(1)}, u32[]{:S(2)}, u32[]{:S(2)}) collective-permute-start(bf16[256,1280]{1,0:T(8,128)(2,1)S(1)} %get-tuple-element.87), channel_id=1, source_target_pairs={{0,1},{1,0},{2,3},{3,2},{4,5},{5,4},{6,7},{7,6},{8,9},{9,8},{10,11... | collective-permute-start | bytes 1966088 | tf_op jit(solution)/shard_map/ppermute | solution.py:116
  3.7 16.6 %collective-permute-start.1 = (bf16[256,1280]{1,0:T(8,128)(2,1)S(1)}, bf16[256,1280]{1,0:T(8,128)(2,1)S(1)}, u32[]{:S(2)}, u32[]{:S(2)}) collective-permute-start(bf16[256,1280]{1,0:T(8,128)(2,1)S(1)} %get-tuple-element.87), channel_id=1, source_target_pairs={{0,97},{1,32},{2,99},{3,34},{4,101},{5,36},{6,103},{7,38},{8,105},... | collective-permute-start | bytes 1966088 | tf_op jit(solution)/shard_map/ppermute | solution.py:116
  19.8 2.1 copy-start.3
  20.2 1.7 copy-start.4
  22.0 36.0 %collective-permute-start.3 = (bf16[1024,1280]{1,0:T(8,128)(2,1)}, bf16[1024,1280]{1,0:T(8,128)(2,1)S(1)}, u32[]{:S(2)}, u32[]{:S(2)}) collective-permute-start(bf16[1024,1280]{1,0:T(8,128)(2,1)} %pad_maximum_fusion), channel_id=1, source_target_pairs={{0,96},{1,33},{2,98},{3,35},{4,100},{5,37},{6,102},{7,39},{8,104},... | collective-permute-start | bytes 7864328 | tf_op jit(solution)/shard_map/ppermute | solution.py:116
  23.5 17.6 %copy-start.2 = (bf16[512,1280]{1,0:T(8,128)(2,1)}, bf16[512,1280]{1,0:T(8,128)(2,1)S(1)}, u32[]{:S(2)}) copy-start(bf16[512,1280]{1,0:T(8,128)(2,1)S(1)} %constant_dynamic-update-slice_fusion.refs_0_) | copy-start | bytes 3932164
  23.6 29.4 %collective-permute-start.4 = (bf16[512,1280]{1,0:T(8,128)(2,1)S(1)}, bf16[512,1280]{1,0:T(8,128)(2,1)}, u32[]{:S(2)}, u32[]{:S(2)}) collective-permute-start(bf16[512,1280]{1,0:T(8,128)(2,1)S(1)} %constant_dynamic-update-slice_fusion.refs_0_), channel_id=1, source_target_pairs={{0,8},{1,9},{2,10},{3,11},{4,12},{5,13},{6,14},{7,15},{8,0},{9,1},... | collective-permute-start | bytes 3932168 | tf_op jit(solution)/shard_map/ppermute | solution.py:116
  25.2 27.7 %collective-permute-start.6 = (bf16[512,1280]{1,0:T(8,128)(2,1)}, bf16[512,1280]{1,0:T(8,128)(2,1)S(1)}, u32[]{:S(2)}, u32[]{:S(2)}) collective-permute-start(bf16[512,1280]{1,0:T(8,128)(2,1)} %get-tuple-element.120.refs_4_.refs_7_), channel_id=1, source_target_pairs={{0,1},{1,0},{2,3},{3,2},{4,5},{5,4},{6,7},{7,6},{8,9},{9,8},{10,11... | collective-permute-start | bytes 3932168 | tf_op jit(solution)/shard_map/ppermute | solution.py:116
  25.2 32.7 %collective-permute-start.5 = (bf16[512,1280]{1,0:T(8,128)(2,1)}, bf16[512,1280]{1,0:T(8,128)(2,1)}, u32[]{:S(2)}, u32[]{:S(2)}) collective-permute-start(bf16[512,1280]{1,0:T(8,128)(2,1)} %get-tuple-element.120.refs_4_.refs_7_), channel_id=1, source_target_pairs={{0,24},{1,25},{2,26},{3,27},{4,28},{5,29},{6,30},{7,31},{8,16},{9,... | collective-permute-start | bytes 3932168 | tf_op jit(solution)/shard_map/ppermute | solution.py:116
  41.2 23.3 %copy-start.22 = (s32[2]{0:T(128)S(1)}, s32[2]{0:T(128)}, u32[]{:S(2)}) copy-start(s32[2]{0:T(128)} %len_ref.3) | copy-start | bytes 28
  41.2 24.6 %copy-start.20 = (f32[2,64,128]{2,1,0:T(8,128)S(1)}, f32[2,64,128]{2,1,0:T(8,128)}, u32[]{:S(2)}) copy-start(f32[2,64,128]{2,1,0:T(8,128)} %get-tuple-element.109) | copy-start | bytes 196612
  41.2 24.6 %copy-start.21 = (f32[2,64,128]{2,1,0:T(8,128)S(1)}, f32[2,64,128]{2,1,0:T(8,128)}, u32[]{:S(2)}) copy-start(f32[2,64,128]{2,1,0:T(8,128)} %get-tuple-element.110) | copy-start | bytes 196612
  52.9 5.0 %copy-start.5 = (bf16[512,1280]{1,0:T(8,128)(2,1)}, bf16[512,1280]{1,0:T(8,128)(2,1)S(1)}, u32[]{:S(2)}) copy-start(bf16[512,1280]{1,0:T(8,128)(2,1)S(1)} %collective-permute-done.6.refs_5_.refs_8_) | copy-start | bytes 3932164
  57.9 7.9 %copy-start = (bf16[1024,1280]{1,0:T(8,128)(2,1)}, bf16[1024,1280]{1,0:T(8,128)(2,1)S(1)}, u32[]{:S(2)}) copy-start(bf16[1024,1280]{1,0:T(8,128)(2,1)S(1)} %collective-permute-done.3.refs_3_) | copy-start | bytes 7864324
  57.9 4.2 %collective-permute-start.11 = (bf16[512,1280]{1,0:T(8,128)(2,1)}, bf16[512,1280]{1,0:T(8,128)(2,1)}, u32[]{:S(2)}, u32[]{:S(2)}) collective-permute-start(bf16[512,1280]{1,0:T(8,128)(2,1)} %collective-permute-done.5.refs_9_.refs_4_), channel_id=1, source_target_pairs={{0,1},{1,0},{2,3},{3,2},{4,5},{5,4},{6,7},{7,6},{8,9},{9,8},{10,11... | collective-permute-start | bytes 3932168 | tf_op jit(solution)/shard_map/ppermute | solution.py:116
  58.0 7.8 %collective-permute-start.12 = (bf16[512,1280]{1,0:T(8,128)(2,1)}, bf16[512,1280]{1,0:T(8,128)(2,1)}, u32[]{:S(2)}, u32[]{:S(2)}) collective-permute-start(bf16[512,1280]{1,0:T(8,128)(2,1)} %get-tuple-element.122.refs_7_.refs_9_), channel_id=1, source_target_pairs={{0,1},{1,0},{2,3},{3,2},{4,5},{5,4},{6,7},{7,6},{8,9},{9,8},{10,11... | collective-permute-start | bytes 3932168 | tf_op jit(solution)/shard_map/ppermute | solution.py:116
  59.8 31.0 %collective-permute-start.9 = (bf16[512,1280]{1,0:T(8,128)(2,1)}, bf16[512,1280]{1,0:T(8,128)(2,1)}, u32[]{:S(2)}, u32[]{:S(2)}) collective-permute-start(bf16[512,1280]{1,0:T(8,128)(2,1)} %slice.84), channel_id=1, source_target_pairs={{0,8},{1,9},{2,10},{3,11},{4,12},{5,13},{6,14},{7,15},{8,0},{9,1},... | collective-permute-start | bytes 3932168 | tf_op jit(solution)/shard_map/ppermute | solution.py:116
  59.8 31.5 %collective-permute-start.8 = (bf16[512,1280]{1,0:T(8,128)(2,1)}, bf16[512,1280]{1,0:T(8,128)(2,1)}, u32[]{:S(2)}, u32[]{:S(2)}) collective-permute-start(bf16[512,1280]{1,0:T(8,128)(2,1)} %collective-permute-done.4.refs_0_.refs_7_), channel_id=1, source_target_pairs={{0,96},{1,33},{2,98},{3,35},{4,100},{5,37},{6,102},{7,39},{8,104},... | collective-permute-start | bytes 3932168 | tf_op jit(solution)/shard_map/ppermute | solution.py:116
  60.4 31.0 %collective-permute-start.7 = (bf16[512,1280]{1,0:T(8,128)(2,1)}, bf16[512,1280]{1,0:T(8,128)(2,1)}, u32[]{:S(2)}, u32[]{:S(2)}) collective-permute-start(bf16[512,1280]{1,0:T(8,128)(2,1)} %collective-permute-done.4.refs_0_.refs_7_), channel_id=1, source_target_pairs={{0,32},{1,97},{2,34},{3,99},{4,36},{5,101},{6,38},{7,103},{8,40},{... | collective-permute-start | bytes 3932168 | tf_op jit(solution)/shard_map/ppermute | solution.py:116
  62.2 31.6 %collective-permute-start.10 = (bf16[512,1280]{1,0:T(8,128)(2,1)}, bf16[512,1280]{1,0:T(8,128)(2,1)}, u32[]{:S(2)}, u32[]{:S(2)}) collective-permute-start(bf16[512,1280]{1,0:T(8,128)(2,1)} %get-tuple-element.122.refs_7_.refs_9_), channel_id=1, source_target_pairs={{0,24},{1,25},{2,26},{3,27},{4,28},{5,29},{6,30},{7,31},{8,16},{9,... | collective-permute-start | bytes 3932168 | tf_op jit(solution)/shard_map/ppermute | solution.py:116
  84.4 13.5 %copy-start.11 = (bf16[4,512,256]{2,1,0:T(8,128)(2,1)S(1)}, bf16[4,512,256]{2,1,0:T(8,128)(2,1)}, u32[]{:S(2)}) copy-start(bf16[4,512,256]{2,1,0:T(8,128)(2,1)} %get-tuple-element.151) | copy-start | bytes 3145732
  93.7 26.4 %collective-permute-start.13 = (bf16[512,1280]{1,0:T(8,128)(2,1)}, bf16[512,1280]{1,0:T(8,128)(2,1)S(1)}, u32[]{:S(2)}, u32[]{:S(2)}) collective-permute-start(bf16[512,1280]{1,0:T(8,128)(2,1)} %collective-permute-done.10.refs_4_), channel_id=1, source_target_pairs={{0,1},{1,0},{2,3},{3,2},{4,5},{5,4},{6,7},{7,6},{8,9},{9,8},{10,11... | collective-permute-start | bytes 3932168 | tf_op jit(solution)/shard_map/ppermute | solution.py:116
  96.0 24.2 %collective-permute-start.14 = (bf16[2,1024,256]{2,1,0:T(8,128)(2,1)}, bf16[2,1024,256]{2,1,0:T(8,128)(2,1)S(1)}, u32[]{:S(2)}, u32[]{:S(2)}) collective-permute-start(bf16[2,1024,256]{2,1,0:T(8,128)(2,1)} %slice.85), channel_id=1, source_target_pairs={{0,2},{1,7},{2,0},{3,5},{4,6},{5,3},{6,4},{7,1},{8,10},{9,15},{10,... | collective-permute-start | bytes 3145736 | tf_op jit(solution)/shard_map/ppermute | solution.py:116
  98.8 25.5 %copy-start.9 = (bf16[4,1024,256]{2,1,0:T(8,128)(2,1)S(1)}, bf16[4,1024,256]{2,1,0:T(8,128)(2,1)}, u32[]{:S(2)}) copy-start(bf16[4,1024,256]{2,1,0:T(8,128)(2,1)} %get-tuple-element.147) | copy-start | bytes 6291460
  98.8 21.3 %collective-permute-start.15 = (bf16[2,512,256]{2,1,0:T(8,128)(2,1)}, bf16[2,512,256]{2,1,0:T(8,128)(2,1)S(1)}, u32[]{:S(2)}, u32[]{:S(2)}) collective-permute-start(bf16[2,512,256]{2,1,0:T(8,128)(2,1)} %slice.86), channel_id=1, source_target_pairs={{0,2},{1,7},{2,0},{3,5},{4,6},{5,3},{6,4},{7,1},{8,10},{9,15},{10,... | collective-permute-start | bytes 1572872 | tf_op jit(solution)/shard_map/ppermute | solution.py:116
  98.9 20.3 %collective-permute-start.16 = (f32[136,128]{1,0:T(8,128)S(1)}, f32[136,128]{1,0:T(8,128)}, u32[]{:S(2)}, u32[]{:S(2)}) collective-permute-start(f32[136,128]{1,0:T(8,128)S(1)} %concatenate.11), channel_id=1, source_target_pairs={{0,32},{1,33},{2,34},{3,35},{4,36},{5,37},{6,38},{7,39},{8,40},{9,... | collective-permute-start | bytes 208904 | tf_op jit(solution)/shard_map/ppermute | solution.py:116
  120.2 9.8 %copy-start.10 = (bf16[512,1280]{1,0:T(8,128)(2,1)}, bf16[512,1280]{1,0:T(8,128)(2,1)S(1)}, u32[]{:S(2)}) copy-start(bf16[512,1280]{1,0:T(8,128)(2,1)S(1)} %collective-permute-done.13.refs_5_) | copy-start | bytes 3932164
  122.4 24.5 %collective-permute-start.19 = (bf16[2,512,256]{2,1,0:T(8,128)(2,1)}, bf16[2,512,256]{2,1,0:T(8,128)(2,1)}, u32[]{:S(2)}, u32[]{:S(2)}) collective-permute-start(bf16[2,512,256]{2,1,0:T(8,128)(2,1)} %slice.91), channel_id=1, source_target_pairs={{0,2},{1,7},{2,0},{3,5},{4,6},{5,3},{6,4},{7,1},{8,10},{9,15},{10,... | collective-permute-start | bytes 1572872 | tf_op jit(solution)/shard_map/ppermute | solution.py:116
  125.3 21.6 %collective-permute-start.17 = (bf16[1024,256]{1,0:T(8,128)(2,1)}, bf16[1024,256]{1,0:T(8,128)(2,1)}, u32[]{:S(2)}, u32[]{:S(2)}) collective-permute-start(bf16[1024,256]{1,0:T(8,128)(2,1)} %fusion.6), channel_id=1, source_target_pairs={{0,6},{1,3},{2,4},{3,1},{4,2},{5,7},{6,0},{7,5},{8,14},{9,11},{10,... | collective-permute-start | bytes 1572872 | tf_op jit(solution)/shard_map/ppermute | solution.py:116
  128.7 18.3 %collective-permute-start.18 = (bf16[512,256]{1,0:T(8,128)(2,1)}, bf16[512,256]{1,0:T(8,128)(2,1)}, u32[]{:S(2)}, u32[]{:S(2)}) collective-permute-start(bf16[512,256]{1,0:T(8,128)(2,1)} %fusion.13), channel_id=1, source_target_pairs={{0,6},{1,3},{2,4},{3,1},{4,2},{5,7},{6,0},{7,5},{8,14},{9,11},{10,... | collective-permute-start | bytes 786440 | tf_op jit(solution)/shard_map/ppermute | solution.py:116
  129.4 16.6 %collective-permute-start.20 = (f32[136,128]{1,0:T(8,128)S(1)}, f32[136,128]{1,0:T(8,128)}, u32[]{:S(2)}, u32[]{:S(2)}) collective-permute-start(f32[136,128]{1,0:T(8,128)S(1)} %add.98), channel_id=1, source_target_pairs={{0,96},{1,97},{2,98},{3,99},{4,100},{5,101},{6,102},{7,103},{8,104... | collective-permute-start | bytes 208904 | tf_op jit(solution)/shard_map/ppermute | solution.py:116
  145.9 2.7 %copy-start.12 = (bf16[4,512,256]{2,1,0:T(8,128)(2,1)S(1)}, bf16[4,512,256]{2,1,0:T(8,128)(2,1)}, u32[]{:S(2)}) copy-start(bf16[4,512,256]{2,1,0:T(8,128)(2,1)} %get-tuple-element.154) | copy-start | bytes 3145732
  148.3 27.8 %copy-start.8 = (bf16[4,1024,256]{2,1,0:T(8,128)(2,1)S(1)}, bf16[4,1024,256]{2,1,0:T(8,128)(2,1)}, u32[]{:S(2)}) copy-start(bf16[4,1024,256]{2,1,0:T(8,128)(2,1)} %get-tuple-element.161) | copy-start | bytes 6291460
  148.3 17.7 %collective-permute-start.22 = (bf16[2,1024,256]{2,1,0:T(8,128)(2,1)S(1)}, bf16[2,1024,256]{2,1,0:T(8,128)(2,1)S(1)}, u32[]{:S(2)}, u32[]{:S(2)}) collective-permute-start(bf16[2,1024,256]{2,1,0:T(8,128)(2,1)S(1)} %slice.94), channel_id=1, source_target_pairs={{0,2},{1,7},{2,0},{3,5},{4,6},{5,3},{6,4},{7,1},{8,10},{9,15},{10,... | collective-permute-start | bytes 3145736 | tf_op jit(solution)/shard_map/ppermute | solution.py:116
  149.8 12.6 %collective-permute-start.21 = (bf16[512,256]{1,0:T(8,128)(2,1)S(1)}, bf16[512,256]{1,0:T(8,128)(2,1)S(1)}, u32[]{:S(2)}, u32[]{:S(2)}) collective-permute-start(bf16[512,256]{1,0:T(8,128)(2,1)S(1)} %fusion.14), channel_id=1, source_target_pairs={{0,6},{1,3},{2,4},{3,1},{4,2},{5,7},{6,0},{7,5},{8,14},{9,11},{10,... | collective-permute-start | bytes 786440 | tf_op jit(solution)/shard_map/ppermute | solution.py:116
  152.5 4.3 %collective-permute-start.23 = (f32[136,128]{1,0:T(8,128)S(1)}, f32[136,128]{1,0:T(8,128)S(1)}, u32[]{:S(2)}, u32[]{:S(2)}) collective-permute-start(f32[136,128]{1,0:T(8,128)S(1)} %add.101), channel_id=1, source_target_pairs={{0,8},{1,9},{2,10},{3,11},{4,12},{5,13},{6,14},{7,15},{8,0},{9,1},... | collective-permute-start | bytes 208904 | tf_op jit(solution)/shard_map/ppermute | solution.py:116
  156.8 5.6 %collective-permute-start.24 = (f32[136,128]{1,0:T(8,128)S(1)}, f32[136,128]{1,0:T(8,128)S(1)}, u32[]{:S(2)}, u32[]{:S(2)}) collective-permute-start(f32[136,128]{1,0:T(8,128)S(1)} %add.103), channel_id=1, source_target_pairs={{0,24},{1,25},{2,26},{3,27},{4,28},{5,29},{6,30},{7,31},{8,16},{9,... | collective-permute-start | bytes 208904 | tf_op jit(solution)/shard_map/ppermute | solution.py:116
  168.4 7.8 %copy-start.1 = (bf16[4,1024,256]{2,1,0:T(8,128)(2,1)S(1)}, bf16[4,1024,256]{2,1,0:T(8,128)(2,1)}, u32[]{:S(2)}) copy-start(bf16[4,1024,256]{2,1,0:T(8,128)(2,1)} %project.5) | copy-start | bytes 6291460
  168.5 10.9 %collective-permute-start.27 = (bf16[2,512,256]{2,1,0:T(8,128)(2,1)S(1)}, bf16[2,512,256]{2,1,0:T(8,128)(2,1)S(1)}, u32[]{:S(2)}, u32[]{:S(2)}) collective-permute-start(bf16[2,512,256]{2,1,0:T(8,128)(2,1)S(1)} %pad_maximum_fusion.1), channel_id=1, source_target_pairs={{1,24},{3,26},{5,28},{7,30},{9,16},{11,18},{13,20},{15,22},{16,9},... | collective-permute-start | bytes 1572872 | tf_op jit(solution)/shard_map/ppermute | solution.py:116
  169.3 15.1 %collective-permute-start.26 = (bf16[2,512,256]{2,1,0:T(8,128)(2,1)S(1)}, bf16[2,512,256]{2,1,0:T(8,128)(2,1)S(1)}, u32[]{:S(2)}, u32[]{:S(2)}) collective-permute-start(bf16[2,512,256]{2,1,0:T(8,128)(2,1)S(1)} %pad_maximum_fusion.1), channel_id=1, source_target_pairs={{0,24},{2,26},{4,28},{6,30},{8,16},{10,18},{12,20},{14,22},{17,9},... | collective-permute-start | bytes 1572872 | tf_op jit(solution)/shard_map/ppermute | solution.py:116
  176.1 20.1 %collective-permute-start.29 = (bf16[2,1024,256]{2,1,0:T(8,128)(2,1)S(1)}, bf16[2,1024,256]{2,1,0:T(8,128)(2,1)S(1)}, u32[]{:S(2)}, u32[]{:S(2)}) collective-permute-start(bf16[2,1024,256]{2,1,0:T(8,128)(2,1)S(1)} %slice.104), channel_id=1, source_target_pairs={{0,2},{1,7},{2,0},{3,5},{4,6},{5,3},{6,4},{7,1},{8,10},{9,15},{10,... | collective-permute-start | bytes 3145736 | tf_op jit(solution)/shard_map/ppermute | solution.py:116
  176.4 16.2 %collective-permute-start.28 = (bf16[1024,256]{1,0:T(8,128)(2,1)S(1)}, bf16[1024,256]{1,0:T(8,128)(2,1)S(1)}, u32[]{:S(2)}, u32[]{:S(2)}) collective-permute-start(bf16[1024,256]{1,0:T(8,128)(2,1)S(1)} %fusion.7), channel_id=1, source_target_pairs={{0,6},{1,3},{2,4},{3,1},{4,2},{5,7},{6,0},{7,5},{8,14},{9,11},{10,... | collective-permute-start | bytes 1572872 | tf_op jit(solution)/shard_map/ppermute | solution.py:116
  179.2 27.8 %copy-start.6 = (bf16[1024,256]{1,0:T(8,128)(2,1)}, bf16[1024,256]{1,0:T(8,128)(2,1)S(1)}, u32[]{:S(2)}) copy-start(bf16[1024,256]{1,0:T(8,128)(2,1)S(1)} %fusion.5) | copy-start | bytes 1572868
  179.3 13.3 %collective-permute-start.25 = (bf16[2,512,256]{2,1,0:T(8,128)(2,1)S(1)}, bf16[2,512,256]{2,1,0:T(8,128)(2,1)S(1)}, u32[]{:S(2)}, u32[]{:S(2)}) collective-permute-start(bf16[2,512,256]{2,1,0:T(8,128)(2,1)S(1)} %bitcast.61), channel_id=1, source_target_pairs={{0,1},{1,0},{2,3},{3,2},{4,5},{5,4},{6,7},{7,6},{8,9},{9,8},{10,11... | collective-permute-start | bytes 1572872 | tf_op jit(solution)/shard_map/ppermute | solution.py:116
  179.4 27.7 %copy-start.13 = (bf16[2,512,256]{2,1,0:T(8,128)(2,1)}, bf16[2,512,256]{2,1,0:T(8,128)(2,1)S(1)}, u32[]{:S(2)}) copy-start(bf16[2,512,256]{2,1,0:T(8,128)(2,1)S(1)} %collective-permute-done.27.other0) | copy-start | bytes 1572868
  184.4 22.6 %copy-start.14 = (bf16[2,512,256]{2,1,0:T(8,128)(2,1)}, bf16[2,512,256]{2,1,0:T(8,128)(2,1)S(1)}, u32[]{:S(2)}) copy-start(bf16[2,512,256]{2,1,0:T(8,128)(2,1)S(1)} %collective-permute-done.26.same0) | copy-start | bytes 1572868
  192.5 14.5 %copy-start.15 = (bf16[2,512,256]{2,1,0:T(8,128)(2,1)}, bf16[2,512,256]{2,1,0:T(8,128)(2,1)S(1)}, u32[]{:S(2)}) copy-start(bf16[2,512,256]{2,1,0:T(8,128)(2,1)S(1)} %collective-permute-done.25.near_in) | copy-start | bytes 1572868
  196.3 11.5 %copy-start.19 = (f32[2,64,128]{2,1,0:T(8,128)S(1)}, f32[2,64,128]{2,1,0:T(8,128)}, u32[]{:S(2)}) copy-start(f32[2,64,128]{2,1,0:T(8,128)} %pre_ref.3) | copy-start | bytes 196612
  196.3 10.5 %collective-permute-start.30 = (bf16[1024,256]{1,0:T(8,128)(2,1)S(1)}, bf16[1024,256]{1,0:T(8,128)(2,1)S(1)}, u32[]{:S(2)}, u32[]{:S(2)}) collective-permute-start(bf16[1024,256]{1,0:T(8,128)(2,1)S(1)} %fusion.8), channel_id=1, source_target_pairs={{0,6},{1,3},{2,4},{3,1},{4,2},{5,7},{6,0},{7,5},{8,14},{9,11},{10,... | collective-permute-start | bytes 1572872 | tf_op jit(solution)/shard_map/ppermute | solution.py:116
  198.2 10.3 %collective-permute-start.33 = (bf16[2,512,256]{2,1,0:T(8,128)(2,1)}, bf16[2,512,256]{2,1,0:T(8,128)(2,1)S(1)}, u32[]{:S(2)}, u32[]{:S(2)}) collective-permute-start(bf16[2,512,256]{2,1,0:T(8,128)(2,1)} %bitcast.23), channel_id=1, source_target_pairs={{1,24},{3,26},{5,28},{7,30},{9,16},{11,18},{13,20},{15,22},{16,9},... | collective-permute-start | bytes 1572872 | tf_op jit(solution)/shard_map/ppermute | solution.py:116
  198.9 13.5 %collective-permute-start.32 = (bf16[2,512,256]{2,1,0:T(8,128)(2,1)}, bf16[2,512,256]{2,1,0:T(8,128)(2,1)S(1)}, u32[]{:S(2)}, u32[]{:S(2)}) collective-permute-start(bf16[2,512,256]{2,1,0:T(8,128)(2,1)} %bitcast.23), channel_id=1, source_target_pairs={{0,24},{2,26},{4,28},{6,30},{8,16},{10,18},{12,20},{14,22},{17,9},... | collective-permute-start | bytes 1572872 | tf_op jit(solution)/shard_map/ppermute | solution.py:116
  207.1 5.2 %copy-start.7 = (bf16[1024,256]{1,0:T(8,128)(2,1)}, bf16[1024,256]{1,0:T(8,128)(2,1)S(1)}, u32[]{:S(2)}) copy-start(bf16[1024,256]{1,0:T(8,128)(2,1)S(1)} %fusion.3) | copy-start | bytes 1572868
  207.1 5.2 %collective-permute-start.31 = (bf16[2,512,256]{2,1,0:T(8,128)(2,1)S(1)}, bf16[2,512,256]{2,1,0:T(8,128)(2,1)S(1)}, u32[]{:S(2)}, u32[]{:S(2)}) collective-permute-start(bf16[2,512,256]{2,1,0:T(8,128)(2,1)S(1)} %bitcast.63), channel_id=1, source_target_pairs={{0,1},{1,0},{2,3},{3,2},{4,5},{5,4},{6,7},{7,6},{8,9},{9,8},{10,11... | collective-permute-start | bytes 1572872 | tf_op jit(solution)/shard_map/ppermute | solution.py:116
  208.5 3.8 %copy-start.16 = (bf16[2,512,256]{2,1,0:T(8,128)(2,1)}, bf16[2,512,256]{2,1,0:T(8,128)(2,1)S(1)}, u32[]{:S(2)}) copy-start(bf16[2,512,256]{2,1,0:T(8,128)(2,1)S(1)} %collective-permute-done.33.other1) | copy-start | bytes 1572868
  212.3 0.8 copy-start.17
  213.1 0.8 copy-start.18

commit v3 on v2

--- a/solution.py
+++ b/solution.py
@@ -41,31 +41,34 @@
         dk_acc[...]=jnp.zeros_like(dk_acc)
         dv_acc[...]=jnp.zeros_like(dv_acc)
     live=len_ref[prompt]
-    col=pl.multiple_of(h*HD,HD)
     for b in range(SEQ//QB):
         r0=b*QB; nk=PREFIX+r0+QB
-        q=q_ref[r0:r0+QB,:]
         rows=lax.broadcasted_iota(jnp.int32,(QB,HD),0)+r0
-        g=jnp.where(rows<live,g_ref[r0:r0+QB,:].astype(jnp.float32),0.0).astype(jnp.bfloat16)
-        s=dot(kj[0:nk,:],q,NT)
-        dp=dot(vj[0:nk,:],g,NT)
         key=lax.broadcasted_iota(jnp.int32,(QB,QB),0)
         row=lax.broadcasted_iota(jnp.int32,(QB,QB),1)
-        s=jnp.concatenate([s[:nk-QB],jnp.where(key<=row,s[nk-QB:],-1e30)],0)
-        top=jnp.max(s,0,keepdims=True)
-        e=jnp.exp((s-top)*inverse)
-        p=e*(1.0/jnp.sum(e,0,keepdims=True))
-        rt=jnp.sum(p*dp,0,keepdims=True)
-        ds=(p*(dp-rt)).astype(jnp.bfloat16)
-        pb=p.astype(jnp.bfloat16)
-        dk_acc[0:nk,:]+=dot(ds,q,NN)
-        dv_acc[0:nk,:]+=dot(pb,g,NN)
-        dqT=dot(kT[:,0:nk],ds,NN)*inverse
-        a=dqT[:HD//2]; c=dqT[HD//2:]
-        co=cosT_ref[:,r0:r0+QB]; si=sinT_ref[:,r0:r0+QB]
-        rot=jnp.concatenate([a*co+c*si,c*co-a*si],0)
-        out_ref[r0:r0+QB,pl.ds(col,HD)]=jnp.transpose(rot).astype(jnp.bfloat16)
-    @pl.when(h==GROUP-1)
+        seen=key<=row
+        qs=[];gs=[];dss=[];pbs=[]
+        for j in range(4):
+            q=q_ref[r0:r0+QB,j*HD:(j+1)*HD]
+            g=jnp.where(rows<live,g_ref[r0:r0+QB,j*HD:(j+1)*HD].astype(jnp.float32),0.0).astype(jnp.bfloat16)
+            s=dot(kj[0:nk,:],q,NT)
+            dp=dot(vj[0:nk,:],g,NT)
+            s=jnp.concatenate([s[:nk-QB],jnp.where(seen,s[nk-QB:],-1e30)],0)
+            top=jnp.max(s,0,keepdims=True)
+            e=jnp.exp((s-top)*inverse)
+            p=e*(1.0/jnp.sum(e,0,keepdims=True))
+            rt=jnp.sum(p*dp,0,keepdims=True)
+            dss.append((p*(dp-rt)).astype(jnp.bfloat16)); pbs.append(p.astype(jnp.bfloat16)); qs.append(q); gs.append(g)
+        dk_acc[0:nk,:]+=dot(jnp.concatenate(dss,1),jnp.concatenate(qs,0),NN)
+        dv_acc[0:nk,:]+=dot(jnp.concatenate(pbs,1),jnp.concatenate(gs,0),NN)
+        for j in range(4):
+            dqT=dot(kT[:,0:nk],dss[j],NN)*inverse
+            a=dqT[:HD//2]; c=dqT[HD//2:]
+            co=cosT_ref[:,r0:r0+QB]; si=sinT_ref[:,r0:r0+QB]
+            rot=jnp.concatenate([a*co+c*si,c*co-a*si],0)
+            col=pl.multiple_of((h*4+j)*HD,HD)
+            out_ref[r0:r0+QB,pl.ds(col,HD)]=jnp.transpose(rot).astype(jnp.bfloat16)
+    @pl.when(h==GROUP//4-1)
     def _():
         dk=dk_acc[...]*inverse
         pg_ref[0]=dk[0:PREFIX]
@@ -78,10 +81,10 @@
     whole=lambda shape: pl.BlockSpec(shape,lambda h:(0,)*len(shape))
     return pl.pallas_call(
         functools.partial(attn_kernel,prompt=prompt),
-        grid=(GROUP,),
+        grid=(GROUP//4,),
         in_specs=[pl.BlockSpec(memory_space=pltpu.SMEM),
-            pl.BlockSpec((SEQ,HD),lambda h:(prompt,h)),
-            pl.BlockSpec((SEQ,HD),lambda h:(prompt,h)),
+            pl.BlockSpec((SEQ,4*HD),lambda h:(prompt,h)),
+            pl.BlockSpec((SEQ,4*HD),lambda h:(prompt,h)),
             pl.BlockSpec((SEQ,HD),lambda h:(prompt,0)),
             pl.BlockSpec((SEQ,HD),lambda h:(prompt,0)),
             whole((2,PREFIX,HD)),whole((HD//2,SEQ)),whole((HD//2,SEQ)),whole((SEQ,HD)),whole((SEQ,HD))],
@@ -94,6 +97,7 @@
         name="attention_backward",
     )(lengths,queries,out_grad,key_rows,value_rows,prefix,*tables)
 
+
 AXES = ("x", "y", "z", "c")
 
 
@@ -167,8 +171,10 @@
 def project_kernel(plan, n_arrays, *refs):
     sides, groups, outs_of = plan
     arrays, rest = refs[:n_arrays], refs[n_arrays:]
-    outs, left, right, made, sems = rest[:outs_of], *rest[outs_of:]
-    width = right.shape[-1]
+    outs, left, right, made, sems = rest[: 2 * outs_of], *rest[2 * outs_of :]
+    cols, width = right.shape[1], right.shape[2] // 2
+    rows = left.shape[0] // len(sides)
+    places = arrays[0]
     sem = iter(range(sems.shape[0]))
 
     def begin(source, target):
@@ -176,76 +182,87 @@
         copy.start()
         return copy
 
-    side_loads = [
-        [begin(arrays[at], left.at[n, :, part * width : (part + 1) * width]) for part, at in enumerate(side)]
-        for n, side in enumerate(sides)
+    def load_side(n):
+        return [
+            begin(arrays[at], left.at[n * rows : (n + 1) * rows, part * width : (part + 1) * width])
+            for part, at in enumerate(sides[n])
+        ]
+
+    side_loads = load_side(0)
+    blocks = [pair for group, _ in groups for pair in group]
+    block_loads = [
+        [
+            begin(arrays[at].at[row : row + cols], right.at[slot, :, part * width : (part + 1) * width])
+            for part, (at, row) in enumerate(pair)
+        ]
+        for slot, pair in enumerate(blocks)
     ]
-    block_loads = []
-    for blocks, _ in groups:
-        for pair in blocks:
-            slot = len(block_loads)
-            block_loads.append(
-                [begin(arrays[at].at[row : row + right.shape[2]], right.at[slot, part]) for part, (at, row) in enumerate(pair)]
-            )
-    ready, stores, slot = set(), [], 0
-    for blocks, units in groups:
-        for index in range(len(blocks)):
-            for copy in block_loads[slot]:
-                copy.wait()
-            for side, places, out, row in units:
-                if side not in ready:
-                    ready.add(side)
-                    for copy in side_loads[side]:
-                        copy.wait()
-                total = dot(left[side, :, :width], right[slot, 0], NT) + dot(left[side, :, width:], right[slot, 1], NT)
-                at = len(stores)
-                made[at] = total.astype(jnp.bfloat16)
-                place = arrays[places][index]
-                stores.append(begin(made.at[at], outs[out].at[place, row : row + total.shape[0]]))
-            slot += 1
+    for n in range(1, len(sides)):
+        side_loads += load_side(n)
+    slot, done, ready, stores = 0, 0, set(), []
+    for group, (first, last, cuts) in groups:
+        for unit in range(first, last):
+            waits = [] if unit in ready else side_loads[2 * unit : 2 * unit + 2]
+            ready.add(unit)
+            for index in range(len(group)):
+                for copy in waits + (block_loads[slot + index] if unit == first else []):
+                    copy.wait()
+                waits = []
+                for cut in range(0, rows, 256):
+                    total = dot(left[unit * rows + cut : unit * rows + cut + 256], right[slot + index], NT)
+                    made[places[index], done + cut : done + cut + 256] = total.astype(jnp.bfloat16)
+            out, row = cuts[unit - first]
+            for part in range(2):
+                stores.append(
+                    begin(made.at[2 * part : 2 * part + 2, done : done + rows], outs[2 * out + part].at[:, row : row + rows])
+                )
+            done += rows
+        slot += len(group)
     for copy in stores:
         copy.wait()
 
 
-def project(groups, cols=256):
-    arrays, kinds = [], []
-
-    def slot_of(array, kind):
+def project(places, groups, cols=256):
+    arrays, kinds = [places], [pltpu.SMEM]
+
+    def slot_of(array):
         for at, known in enumerate(arrays):
             if known is array:
                 return at
         arrays.append(array)
-        kinds.append(kind)
+        kinds.append(pl.ANY)
         return len(arrays) - 1
 
-    sides, plan, out_rows = [], [], {}
-    for blocks, units in groups:
-        pairs = [tuple((slot_of(array, pl.ANY), row) for array, row in pair) for pair in blocks]
-        done = []
-        for (own, other), places, out, row in units:
-            side = (slot_of(own, pl.ANY), slot_of(other, pl.ANY))
+    sides, plan, out_rows, total = [], [], {}, 0
+    for blocks, lhs, cuts in groups:
+        pairs = [tuple((slot_of(array), row) for array, row in pair) for pair in blocks]
+        found = [(slot_of(own), slot_of(other)) for own, other in lhs]
+        for side in found:
             if side not in sides:
                 sides.append(side)
+        for (own, _), (out, row) in zip(lhs, cuts):
             out_rows[out] = max(out_rows.get(out, 0), row + own.shape[0])
-            done.append((sides.index(side), slot_of(places, pltpu.SMEM), out, row))
-        plan.append((pairs, done))
+            total += own.shape[0]
+        first = sides.index(found[0])
+        plan.append((pairs, (first, first + len(found), cuts)))
     rows, width = arrays[sides[0][0]].shape
-    n_blocks = sum(len(blocks) for blocks, _ in plan)
-    n_out = sum(len(blocks) * len(units) for blocks, units in plan)
-    return pl.pallas_call(
+    n_blocks = sum(len(pairs) for pairs, _ in plan)
+    hbm = pl.BlockSpec(memory_space=pl.ANY)
+    out = pl.pallas_call(
         functools.partial(project_kernel, (sides, plan, len(out_rows)), len(arrays)),
         in_specs=[pl.BlockSpec(memory_space=kind) for kind in kinds],
-        out_specs=[pl.BlockSpec(memory_space=pl.ANY)] * len(out_rows),
-        out_shape=[jax.ShapeDtypeStruct((4, out_rows[at], cols), jnp.bfloat16) for at in sorted(out_rows)],
+        out_specs=[hbm] * (2 * len(out_rows)),
+        out_shape=[jax.ShapeDtypeStruct((2, out_rows[at], cols), jnp.bfloat16) for at in sorted(out_rows) for _ in range(2)],
         scratch_shapes=[
-            pltpu.VMEM((len(sides), rows, 2 * width), jnp.bfloat16),
-            pltpu.VMEM((n_blocks, 2, cols, width), jnp.bfloat16),
-            pltpu.VMEM((n_out, rows, cols), jnp.bfloat16),
-            pltpu.SemaphoreType.DMA((2 * len(sides) + 2 * n_blocks + n_out,)),
+            pltpu.VMEM((len(sides) * rows, 2 * width), jnp.bfloat16),
+            pltpu.VMEM((n_blocks, cols, 2 * width), jnp.bfloat16),
+            pltpu.VMEM((4, total, cols), jnp.bfloat16),
+            pltpu.SemaphoreType.DMA((2 * len(sides) + 2 * n_blocks + 2 * (total // rows),)),
         ],
         compiler_params=pltpu.CompilerParams(vmem_limit_bytes=58 * 2**20),
         name="project",
     )(*arrays)
+    return [(out[2 * at], out[2 * at + 1]) for at in range(len(out_rows))]
 
 
 def arrange_kernel(info, near, mate, near_in, mate_in, same0, same1, other0, other1, out_ref):
@@ -330,7 +347,8 @@
     ]
 
     def start_unit(partial):
-        return partial, send(partial[2:], z_side)
+        keep, give = partial
+        return keep, send(give, z_side)
 
     def pass_on(held):
         partial, arrived = held
@@ -348,23 +366,23 @@
     mate_far = send(turned[2 * rows :], y_mate)
     pair1 = send(self1, y_partner)
     both0, both1, there0 = (self0, self0_other), (self1, self1_other), (pair0, pair0_other)
-    sn, p0n = project([(near_blocks, [(both0, places, 0, 0), (both1, places, 0, SEQ), (there0, places, 1, 0)])])
+    sn, p0n = project(places, [(near_blocks, [both0, both1, there0], [(0, 0), (0, SEQ), (1, 0)])])
+    terms = terms + send(terms, x_mate)
     mate_side, mate_turn, mate_far, pair1, there0, both0, both1, sn, p0n, mate, terms = gate(
         (mate_side, mate_turn, mate_far, pair1, there0, both0, both1, sn, p0n, mate, terms)
     )
     mate_blocks = [((array, 0), (array, rows)) for array in (mate, mate_side, mate_turn, mate_far)]
     pair1_other = send(pair1, sibling)
     sn, p0n = start_unit(sn), start_unit(p0n)
-    terms = terms + send(terms, x_mate)
-    p0m, sm = project([(mate_blocks, [(there0, places, 0, 0), (both0, places, 1, 0), (both1, places, 1, SEQ)])])
+    terms = terms + send(terms, x_cross)
+    p0m, sm = project(places, [(mate_blocks, [there0, both0, both1], [(0, 0), (1, 0), (1, SEQ)])])
     pair1_other, sn, p0n, p0m, pair1, terms, sm = gate((pair1_other, sn, p0n, p0m, pair1, terms, sm))
     sn, p0n, p0m = pass_on(sn), pass_on(p0n), start_unit(p0m)
     there1 = (pair1, pair1_other)
-    terms = terms + send(terms, x_cross)
-    p1 = project([(near_blocks, [(there1, places, 0, 0)]), (mate_blocks, [(there1, places, 0, SEQ)])])[0]
+    terms = terms + send(terms, y_mate)
+    p1 = project(places, [(near_blocks, [there1], [(0, 0)]), (mate_blocks, [there1], [(0, SEQ)])])[0]
     sn, p0n, p0m, p1, terms, sm = gate((sn, p0n, p0m, p1, terms, sm))
     p0m, p1 = pass_on(p0m), start_unit(p1)
-    terms = terms + send(terms, y_mate)
     terms = terms + send(terms, y_partner)
     p0m, p1, terms, p0n, sn, sm = gate((p0m, p1, terms, p0n, sn, sm))
     loss_scale = 16384.0 / terms[2 * PREFIX, 0]

time: 222 us -> 207 us (0.932)
  Pallas kernels: 84.2 us -> 60.9 us
  waiting for transfers between devices: 62.5 us -> 83.6 us
  local copies, waits for them, and re-layouts: 11.7 us -> 5 us
  other arithmetic: 13.2 us -> 9.68 us
  starting transfers between devices: 43.5 us -> 41 us
    ppermute x34, waiting for transfers between devices: 62.5 us -> 83.6 us  [send(): return lax.ppermute(array, AXES, pairs_of(move))]
    pallas_call x3, Pallas kernels: 53 us -> 37.6 us  [project(): pl.pallas_call(functools.partial(project_kernel, (sides, plan, len(out_ro...]
    pallas_call x2, Pallas kernels: 27.5 us -> 19.5 us  [attention(): pl.pallas_call(functools.partial(attn_kernel, prompt=prompt), grid=(GROUP...]
    slice x5 -> x0, local copies, waits for them, and re-layouts: 6.77 us -> none  [start_unit(): return (partial, send(partial[2:], z_side))]
    ppermute x34, starting transfers between devices: 43.5 us -> 41 us  [send(): return lax.ppermute(array, AXES, pairs_of(move))]
  transfers between devices with their start and end apart: 34 -> 34, of which waited for: 15 -> 16; matrix products, arithmetic and copies ran while one was open for 6% -> 3% of each run, Pallas kernels for 37% -> 28%
where the time goes in v3:
time: 207 us; the launch traced here: 203 us
  waiting for transfers between devices  83.6 us (40%)
  Pallas kernels  60.9 us (29%)
  starting transfers between devices  41 us (20%)
  other arithmetic  9.68 us (5%)
  local copies, waits for them, and re-layouts  5 us (2%)
  between operations  2.47 us (1%)
    ppermute x34, waiting for transfers between devices, send(): return lax.ppermute(array, AXES, pairs_of(move))  83.6 us
    ppermute x34, starting transfers between devices, send(): return lax.ppermute(array, AXES, pairs_of(move))  41 us
    pallas_call x3, Pallas kernels, project(): pl.pallas_call(functools.partial(project_kernel, (sides, plan, len(out_ro...  37.6 us
    pallas_call x2, Pallas kernels, attention(): pl.pallas_call(functools.partial(attn_kernel, prompt=prompt), grid=(GROUP...  19.5 us
  transfers between devices with their start and end apart: 34, of which 16 were waited for; matrix products, arithmetic and copies ran while one was open for 3% of the time, Pallas kernels for 28%

profile of v3, /device:TPU:2, one launch (start us, length us, event | category | flops | bytes accessed | tf_op | source)
XLA Modules:
  0.0 202.6 jit_solution(7348976003277084360)
XLA Ops:
  0.7 1.4 constant_dynamic-slice_fusion
  2.0 0.7 compare_select_fusion.2.refs_0_
  2.7 0.5 collective-permute-start
  3.2 0.7 collective-permute-start.1
  3.9 1.0 collective-permute-start.2
  4.8 9.8 %attention_backward.2 = (bf16[512,1280]{1,0:T(8,128)(2,1)}, f32[2,64,128]{2,1,0:T(8,128)}) custom-call(s32[2]{0:T(128)} %len_ref.3, bf16[1024,1024]{1,0:T(8,128)(2,1)} %q_ref.3, bf16[1024,1024]{1,0:T(8,128)(2,1)} %g_ref.3, bf16[1024,128]{1,0:T(8,128)(2,1)} %k_ref.2, bf16[1024,128]{1,0:T(8,128)(2,1)} %v_ref.3, f32[2,64,128]{2,1,0:T(8,128)} %pre_ref.3, ...), custom_call_target="tpu_custom_call" | custom-call | flops 3019898880 | bytes 4194304 | tf_op jit(solution)/shard_map/attention_backward/pallas_call | solution.py:82
  14.6 5.6 %collective-permute-done.refs_2_ = bf16[256,1280]{1,0:T(8,128)(2,1)S(1)} collective-permute-done((bf16[256,1280]{1,0:T(8,128)(2,1)S(1)}, bf16[256,1280]{1,0:T(8,128)(2,1)S(1)}, u32[]{:S(2)}, u32[]{:S(2)}) %collective-permute-start) | collective-permute-done | bytes 655392 | tf_op jit(solution)/shard_map/ppermute | solution.py:120
  20.3 1.8 pad_maximum_fusion
  22.1 1.4 collective-permute-start.3
  23.6 1.7 collective-permute-start.4
  25.3 2.2 %collective-permute-start.5 = (bf16[512,1280]{1,0:T(8,128)(2,1)}, bf16[512,1280]{1,0:T(8,128)(2,1)}, u32[]{:S(2)}, u32[]{:S(2)}) collective-permute-start(bf16[512,1280]{1,0:T(8,128)(2,1)} %get-tuple-element.137.refs_5_.refs_7_), channel_id=1, source_target_pairs={{0,24},{1,25},{2,26},{3,27},{4,28},{5,29},{6,30},{7,31},{8,16},{9,... | collective-permute-start | bytes 3932168 | tf_op jit(solution)/shard_map/ppermute | solution.py:120
  27.5 9.8 %attention_backward.3 = (bf16[512,1280]{1,0:T(8,128)(2,1)}, f32[2,64,128]{2,1,0:T(8,128)}) custom-call(s32[2]{0:T(128)} %len_ref.3, bf16[1024,1024]{1,0:T(8,128)(2,1)} %q_ref.3, bf16[1024,1024]{1,0:T(8,128)(2,1)} %g_ref.3, bf16[1024,128]{1,0:T(8,128)(2,1)} %k_ref.2, bf16[1024,128]{1,0:T(8,128)(2,1)} %v_ref.3, f32[2,64,128]{2,1,0:T(8,128)} %pre_ref.3, ...), custom_call_target="tpu_custom_call" | custom-call | flops 3019898880 | bytes 4194304 | tf_op jit(solution)/shard_map/attention_backward/pallas_call | solution.py:82
  37.3 15.6 %collective-permute-done.4.refs_1_.refs_7_ = bf16[512,1280]{1,0:T(8,128)(2,1)S(1)} collective-permute-done((bf16[512,1280]{1,0:T(8,128)(2,1)S(1)}, bf16[512,1280]{1,0:T(8,128)(2,1)S(1)}, u32[]{:S(2)}, u32[]{:S(2)}) %collective-permute-start.4) | collective-permute-done | bytes 1310752 | tf_op jit(solution)/shard_map/ppermute | solution.py:120
  52.9 3.0 %collective-permute-done.5.refs_9_.refs_5_ = bf16[512,1280]{1,0:T(8,128)(2,1)} collective-permute-done((bf16[512,1280]{1,0:T(8,128)(2,1)}, bf16[512,1280]{1,0:T(8,128)(2,1)}, u32[]{:S(2)}, u32[]{:S(2)}) %collective-permute-start.5) | collective-permute-done | bytes 1310752 | tf_op jit(solution)/shard_map/ppermute | solution.py:120
  56.0 0.9 reduce_sum.9
  57.5 0.8 add.97
  58.4 0.7 collective-permute-start.13
  59.1 2.2 %collective-permute-start.10 = (bf16[512,1280]{1,0:T(8,128)(2,1)}, bf16[512,1280]{1,0:T(8,128)(2,1)}, u32[]{:S(2)}, u32[]{:S(2)}) collective-permute-start(bf16[512,1280]{1,0:T(8,128)(2,1)} %get-tuple-element.139.refs_7_.refs_9_), channel_id=1, source_target_pairs={{0,24},{1,25},{2,26},{3,27},{4,28},{5,29},{6,30},{7,31},{8,16},{9,... | collective-permute-start | bytes 3932168 | tf_op jit(solution)/shard_map/ppermute | solution.py:120
  61.3 1.2 slice.69
  62.5 0.4 collective-permute-done.13
  62.9 1.1 collective-permute-start.7
  64.0 2.2 %collective-permute-start.8 = (bf16[512,1280]{1,0:T(8,128)(2,1)S(1)}, bf16[512,1280]{1,0:T(8,128)(2,1)S(1)}, u32[]{:S(2)}, u32[]{:S(2)}) collective-permute-start(bf16[512,1280]{1,0:T(8,128)(2,1)S(1)} %copy-done.5), channel_id=1, source_target_pairs={{0,96},{1,33},{2,98},{3,35},{4,100},{5,37},{6,102},{7,39},{8,104},... | collective-permute-start | bytes 3932168 | tf_op jit(solution)/shard_map/ppermute | solution.py:120
  66.2 13.3 %project.3 = (bf16[2,1024,256]{2,1,0:T(8,128)(2,1)}, bf16[2,1024,256]{2,1,0:T(8,128)(2,1)}, bf16[2,512,256]{2,1,0:T(8,128)(2,1)}, bf16[2,512,256]{2,1,0:T(8,128)(2,1)}) custom-call(s32[4]{0:T(128)} %compare_select_fusion.2.refs_0_, bf16[512,1280]{1,0:T(8,128)(2,1)} %copy-done.1, bf16[256,1280]{1,0:T(8,128)(2,1)} %copy-done.2, bf16[256,1280]{1,0:T(8,128)(2,1)} %copy-done.3, ...), custom_call_target="tpu_custom_call" | custom-call | tf_op jit(solution)/shard_map/project/pallas_call | solution.py:251
  79.5 14.1 %collective-permute-done.9.refs_4_.refs_10_ = bf16[512,1280]{1,0:T(8,128)(2,1)S(1)} collective-permute-done((bf16[512,1280]{1,0:T(8,128)(2,1)}, bf16[512,1280]{1,0:T(8,128)(2,1)S(1)}, u32[]{:S(2)}, u32[]{:S(2)}) %collective-permute-start.9) | collective-permute-done | bytes 1310752 | tf_op jit(solution)/shard_map/ppermute | solution.py:120
  93.5 0.1 collective-permute-done.8.refs_3_.refs_9_
  93.7 0.7 collective-permute-start.14
  94.3 1.9 collective-permute-start.15
  96.4 1.5 collective-permute-start.17
  97.9 13.3 %project.4 = (bf16[2,512,256]{2,1,0:T(8,128)(2,1)}, bf16[2,512,256]{2,1,0:T(8,128)(2,1)}, bf16[2,1024,256]{2,1,0:T(8,128)(2,1)}, bf16[2,1024,256]{2,1,0:T(8,128)(2,1)}) custom-call(s32[4]{0:T(128)} %compare_select_fusion.2.refs_0_, bf16[512,1280]{1,0:T(8,128)(2,1)} %copy-done.4, bf16[512,1280]{1,0:T(8,128)(2,1)} %copy-done.7, bf16[512,1280]{1,0:T(8,128)(2,1)} %copy-done.8, ...), custom_call_target="tpu_custom_call" | custom-call | tf_op jit(solution)/shard_map/project/pallas_call | solution.py:251
  111.3 3.7 %collective-permute-done.16 = bf16[2,512,256]{2,1,0:T(8,128)(2,1)S(1)} collective-permute-done((bf16[2,512,256]{2,1,0:T(8,128)(2,1)}, bf16[2,512,256]{2,1,0:T(8,128)(2,1)S(1)}, u32[]{:S(2)}, u32[]{:S(2)}) %collective-permute-start.16) | collective-permute-done | bytes 524320 | tf_op jit(solution)/shard_map/ppermute | solution.py:120
  115.0 1.8 fusion.6
  116.8 4.1 %collective-permute-start.18 = (bf16[1024,256]{1,0:T(8,128)(2,1)S(1)}, bf16[1024,256]{1,0:T(8,128)(2,1)S(1)}, u32[]{:S(2)}, u32[]{:S(2)}) collective-permute-start(bf16[1024,256]{1,0:T(8,128)(2,1)S(1)} %fusion.6), channel_id=1, source_target_pairs={{0,6},{1,3},{2,4},{3,1},{4,2},{5,7},{6,0},{7,5},{8,14},{9,11},{10,... | collective-permute-start | bytes 1572872 | tf_op jit(solution)/shard_map/ppermute | solution.py:120
  121.0 0.6 collective-permute-start.19
  121.6 1.6 collective-permute-start.21
  123.2 11.0 %project.5 = (bf16[2,1024,256]{2,1,0:T(8,128)(2,1)}, bf16[2,1024,256]{2,1,0:T(8,128)(2,1)}) custom-call(s32[4]{0:T(128)} %compare_select_fusion.2.refs_0_, bf16[512,1280]{1,0:T(8,128)(2,1)} %copy-done.1, bf16[256,1280]{1,0:T(8,128)(2,1)} %copy-done.2, bf16[256,1280]{1,0:T(8,128)(2,1)} %copy-done.3, bf16[1024,1280]{1,0:T(8,128)(2,1)} %copy-done, ...), custom_call_target="tpu_custom_call" | custom-call | tf_op jit(solution)/shard_map/project/pallas_call | solution.py:251
  134.2 2.0 collective-permute-done.19
  136.2 0.2 collective-permute-start.23
  136.5 2.8 %collective-permute-start.22 = (bf16[512,256]{1,0:T(8,128)(2,1)S(1)}, bf16[512,256]{1,0:T(8,128)(2,1)S(1)}, u32[]{:S(2)}, u32[]{:S(2)}) collective-permute-start(bf16[512,256]{1,0:T(8,128)(2,1)S(1)} %fusion.14), channel_id=1, source_target_pairs={{0,6},{1,3},{2,4},{3,1},{4,2},{5,7},{6,0},{7,5},{8,14},{9,11},{10,... | collective-permute-start | bytes 786440 | tf_op jit(solution)/shard_map/ppermute | solution.py:120
  139.3 2.6 %collective-permute-start.24 = (f32[136,128]{1,0:T(8,128)S(1)}, f32[136,128]{1,0:T(8,128)S(1)}, u32[]{:S(2)}, u32[]{:S(2)}) collective-permute-start(f32[136,128]{1,0:T(8,128)S(1)} %add.102), channel_id=1, source_target_pairs={{0,24},{1,25},{2,26},{3,27},{4,28},{5,29},{6,30},{7,31},{8,16},{9,... | collective-permute-start | bytes 208904 | tf_op jit(solution)/shard_map/ppermute | solution.py:120
  141.9 2.9 %collective-permute-done.24 = f32[136,128]{1,0:T(8,128)S(1)} collective-permute-done((f32[136,128]{1,0:T(8,128)S(1)}, f32[136,128]{1,0:T(8,128)S(1)}, u32[]{:S(2)}, u32[]{:S(2)}) %collective-permute-start.24) | collective-permute-done | bytes 69664 | tf_op jit(solution)/shard_map/ppermute | solution.py:120
  144.8 2.2 %collective-permute-done.22 = bf16[512,256]{1,0:T(8,128)(2,1)S(1)} collective-permute-done((bf16[512,256]{1,0:T(8,128)(2,1)S(1)}, bf16[512,256]{1,0:T(8,128)(2,1)S(1)}, u32[]{:S(2)}, u32[]{:S(2)}) %collective-permute-start.22) | collective-permute-done | bytes 262176 | tf_op jit(solution)/shard_map/ppermute | solution.py:120
  147.0 7.0 %collective-permute-done.23 = bf16[2,1024,256]{2,1,0:T(8,128)(2,1)S(1)} collective-permute-done((bf16[2,1024,256]{2,1,0:T(8,128)(2,1)}, bf16[2,1024,256]{2,1,0:T(8,128)(2,1)S(1)}, u32[]{:S(2)}, u32[]{:S(2)}) %collective-permute-start.23) | collective-permute-done | bytes 1048608 | tf_op jit(solution)/shard_map/ppermute | solution.py:120
  154.0 0.5 slice.78
  155.2 0.2 fusion.15
  155.5 4.6 %collective-permute-start.26 = (bf16[2,512,256]{2,1,0:T(8,128)(2,1)S(1)}, bf16[2,512,256]{2,1,0:T(8,128)(2,1)S(1)}, u32[]{:S(2)}, u32[]{:S(2)}) collective-permute-start(bf16[2,512,256]{2,1,0:T(8,128)(2,1)S(1)} %pad_maximum_fusion.1), channel_id=1, source_target_pairs={{0,24},{2,26},{4,28},{6,30},{8,16},{10,18},{12,20},{14,22},{17,9},... | collective-permute-start | bytes 1572872 | tf_op jit(solution)/shard_map/ppermute | solution.py:120
  160.1 0.9 collective-permute-start.27
  161.3 1.0 collective-permute-start.28
  162.3 1.3 fusion.5
  163.6 0.3 collective-permute-start.25
  163.9 13.5 %collective-permute-done.28 = bf16[1024,256]{1,0:T(8,128)(2,1)S(1)} collective-permute-done((bf16[1024,256]{1,0:T(8,128)(2,1)S(1)}, bf16[1024,256]{1,0:T(8,128)(2,1)S(1)}, u32[]{:S(2)}, u32[]{:S(2)}) %collective-permute-start.28) | collective-permute-done | bytes 524320 | tf_op jit(solution)/shard_map/ppermute | solution.py:120
  177.4 4.2 %collective-permute-done.29 = bf16[2,1024,256]{2,1,0:T(8,128)(2,1)S(1)} collective-permute-done((bf16[2,1024,256]{2,1,0:T(8,128)(2,1)S(1)}, bf16[2,1024,256]{2,1,0:T(8,128)(2,1)S(1)}, u32[]{:S(2)}, u32[]{:S(2)}) %collective-permute-start.29) | collective-permute-done | bytes 1048608 | tf_op jit(solution)/shard_map/ppermute | solution.py:120
  181.7 0.7 collective-permute-start.30
  182.4 0.2 fusion.1
  182.7 2.8 %collective-permute-start.32 = (bf16[2,512,256]{2,1,0:T(8,128)(2,1)S(1)}, bf16[2,512,256]{2,1,0:T(8,128)(2,1)S(1)}, u32[]{:S(2)}, u32[]{:S(2)}) collective-permute-start(bf16[2,512,256]{2,1,0:T(8,128)(2,1)S(1)} %bitcast.67), channel_id=1, source_target_pairs={{0,24},{2,26},{4,28},{6,30},{8,16},{10,18},{12,20},{14,22},{17,9},... | collective-permute-start | bytes 1572872 | tf_op jit(solution)/shard_map/ppermute | solution.py:120
  185.5 0.7 collective-permute-start.33
  186.2 6.0 %collective-permute-done.30 = bf16[1024,256]{1,0:T(8,128)(2,1)S(1)} collective-permute-done((bf16[1024,256]{1,0:T(8,128)(2,1)S(1)}, bf16[1024,256]{1,0:T(8,128)(2,1)S(1)}, u32[]{:S(2)}, u32[]{:S(2)}) %collective-permute-start.30) | collective-permute-done | bytes 524320 | tf_op jit(solution)/shard_map/ppermute | solution.py:120
  192.2 0.2 fusion.3
  192.5 0.7 pad_add_fusion.info
  193.2 0.6 sub.26
  193.8 3.2 %collective-permute-done.32.same1 = bf16[2,512,256]{2,1,0:T(8,128)(2,1)S(1)} collective-permute-done((bf16[2,512,256]{2,1,0:T(8,128)(2,1)S(1)}, bf16[2,512,256]{2,1,0:T(8,128)(2,1)S(1)}, u32[]{:S(2)}, u32[]{:S(2)}) %collective-permute-start.32) | collective-permute-done | bytes 524320 | tf_op jit(solution)/shard_map/ppermute | solution.py:120
  197.1 0.8 copy-done.20
  197.8 0.2 copy-done.21
  198.0 0.8 copy-done.22
  198.8 3.8 %arrange.1 = bf16[1024,1024]{1,0:T(8,128)(2,1)} custom-call(s32[3]{0:T(128)} %pad_add_fusion.info, bf16[2,512,256]{2,1,0:T(8,128)(2,1)} %bitcast.62, bf16[2,512,256]{2,1,0:T(8,128)(2,1)} %bitcast.64, bf16[2,512,256]{2,1,0:T(8,128)(2,1)} %copy-done.18, bf16[2,512,256]{2,1,0:T(8,128)(2,1)} %copy-done.22, bf16[2,512,256]{2,1,0:T(8,128)(2,1)} %copy-done.15, ...), custom_call_target="tpu_custom_call" | custom-call | tf_op jit(solution)/shard_map/arrange/pallas_call | solution.py:295
  (91 shorter events, 1.3 us)
Async XLA Ops:
  2.7 17.5 %collective-permute-start = (bf16[256,1280]{1,0:T(8,128)(2,1)S(1)}, bf16[256,1280]{1,0:T(8,128)(2,1)S(1)}, u32[]{:S(2)}, u32[]{:S(2)}) collective-permute-start(bf16[256,1280]{1,0:T(8,128)(2,1)S(1)} %get-tuple-element.103), channel_id=1, source_target_pairs={{0,32},{1,97},{2,34},{3,99},{4,36},{5,101},{6,38},{7,103},{8,40},{... | collective-permute-start | bytes 1966088 | tf_op jit(solution)/shard_map/ppermute | solution.py:120
  3.2 17.2 %collective-permute-start.1 = (bf16[256,1280]{1,0:T(8,128)(2,1)S(1)}, bf16[256,1280]{1,0:T(8,128)(2,1)S(1)}, u32[]{:S(2)}, u32[]{:S(2)}) collective-permute-start(bf16[256,1280]{1,0:T(8,128)(2,1)S(1)} %get-tuple-element.100), channel_id=1, source_target_pairs={{0,97},{1,32},{2,99},{3,34},{4,101},{5,36},{6,103},{7,38},{8,105},... | collective-permute-start | bytes 1966088 | tf_op jit(solution)/shard_map/ppermute | solution.py:120
  3.9 16.4 %collective-permute-start.2 = (bf16[256,1280]{1,0:T(8,128)(2,1)S(1)}, bf16[256,1280]{1,0:T(8,128)(2,1)S(1)}, u32[]{:S(2)}, u32[]{:S(2)}) collective-permute-start(bf16[256,1280]{1,0:T(8,128)(2,1)S(1)} %get-tuple-element.100), channel_id=1, source_target_pairs={{0,1},{1,0},{2,3},{3,2},{4,5},{5,4},{6,7},{7,6},{8,9},{9,8},{10,11... | collective-permute-start | bytes 1966088 | tf_op jit(solution)/shard_map/ppermute | solution.py:120
  20.2 1.9 copy-start.2
  20.3 1.8 copy-start.3
  22.1 33.8 %collective-permute-start.3 = (bf16[1024,1280]{1,0:T(8,128)(2,1)}, bf16[1024,1280]{1,0:T(8,128)(2,1)S(1)}, u32[]{:S(2)}, u32[]{:S(2)}) collective-permute-start(bf16[1024,1280]{1,0:T(8,128)(2,1)} %pad_maximum_fusion), channel_id=1, source_target_pairs={{0,96},{1,33},{2,98},{3,35},{4,100},{5,37},{6,102},{7,39},{8,104},... | collective-permute-start | bytes 7864328 | tf_op jit(solution)/shard_map/ppermute | solution.py:120
  23.6 13.7 %copy-start.1 = (bf16[512,1280]{1,0:T(8,128)(2,1)}, bf16[512,1280]{1,0:T(8,128)(2,1)S(1)}, u32[]{:S(2)}) copy-start(bf16[512,1280]{1,0:T(8,128)(2,1)S(1)} %constant_dynamic-update-slice_fusion.refs_1_) | copy-start | bytes 3932164
  23.6 32.4 %copy-start.26 = (s32[2]{0:T(128)S(1)}, s32[2]{0:T(128)}, u32[]{:S(2)}) copy-start(s32[2]{0:T(128)} %len_ref.3) | copy-start | bytes 28
  23.6 33.9 %copy-start.24 = (f32[2,64,128]{2,1,0:T(8,128)S(1)}, f32[2,64,128]{2,1,0:T(8,128)}, u32[]{:S(2)}) copy-start(f32[2,64,128]{2,1,0:T(8,128)} %get-tuple-element.124) | copy-start | bytes 196612
  23.6 29.3 %collective-permute-start.4 = (bf16[512,1280]{1,0:T(8,128)(2,1)S(1)}, bf16[512,1280]{1,0:T(8,128)(2,1)S(1)}, u32[]{:S(2)}, u32[]{:S(2)}) collective-permute-start(bf16[512,1280]{1,0:T(8,128)(2,1)S(1)} %constant_dynamic-update-slice_fusion.refs_1_), channel_id=1, source_target_pairs={{0,8},{1,9},{2,10},{3,11},{4,12},{5,13},{6,14},{7,15},{8,0},{9,1},... | collective-permute-start | bytes 3932168 | tf_op jit(solution)/shard_map/ppermute | solution.py:120
  25.3 30.6 %collective-permute-start.5 = (bf16[512,1280]{1,0:T(8,128)(2,1)}, bf16[512,1280]{1,0:T(8,128)(2,1)}, u32[]{:S(2)}, u32[]{:S(2)}) collective-permute-start(bf16[512,1280]{1,0:T(8,128)(2,1)} %get-tuple-element.137.refs_5_.refs_7_), channel_id=1, source_target_pairs={{0,24},{1,25},{2,26},{3,27},{4,28},{5,29},{6,30},{7,31},{8,16},{9,... | collective-permute-start | bytes 3932168 | tf_op jit(solution)/shard_map/ppermute | solution.py:120
  27.5 28.4 %collective-permute-start.6 = (bf16[512,1280]{1,0:T(8,128)(2,1)}, bf16[512,1280]{1,0:T(8,128)(2,1)}, u32[]{:S(2)}, u32[]{:S(2)}) collective-permute-start(bf16[512,1280]{1,0:T(8,128)(2,1)} %get-tuple-element.137.refs_5_.refs_7_), channel_id=1, source_target_pairs={{0,1},{1,0},{2,3},{3,2},{4,5},{5,4},{6,7},{7,6},{8,9},{9,8},{10,11... | collective-permute-start | bytes 3932168 | tf_op jit(solution)/shard_map/ppermute | solution.py:120
  52.9 3.0 %copy-start.4 = (bf16[512,1280]{1,0:T(8,128)(2,1)}, bf16[512,1280]{1,0:T(8,128)(2,1)S(1)}, u32[]{:S(2)}) copy-start(bf16[512,1280]{1,0:T(8,128)(2,1)S(1)} %collective-permute-done.4.refs_1_.refs_7_) | copy-start | bytes 3932164
  55.9 6.5 %copy-start = (bf16[1024,1280]{1,0:T(8,128)(2,1)}, bf16[1024,1280]{1,0:T(8,128)(2,1)S(1)}, u32[]{:S(2)}) copy-start(bf16[1024,1280]{1,0:T(8,128)(2,1)S(1)} %collective-permute-done.3.refs_4_) | copy-start | bytes 7864324
  55.9 8.1 %collective-permute-start.11 = (bf16[512,1280]{1,0:T(8,128)(2,1)}, bf16[512,1280]{1,0:T(8,128)(2,1)}, u32[]{:S(2)}, u32[]{:S(2)}) collective-permute-start(bf16[512,1280]{1,0:T(8,128)(2,1)} %collective-permute-done.5.refs_9_.refs_5_), channel_id=1, source_target_pairs={{0,1},{1,0},{2,3},{3,2},{4,5},{5,4},{6,7},{7,6},{8,9},{9,8},{10,11... | collective-permute-start | bytes 3932168 | tf_op jit(solution)/shard_map/ppermute | solution.py:120
  58.4 4.5 %copy-start.5 = (bf16[512,1280]{1,0:T(8,128)(2,1)S(1)}, bf16[512,1280]{1,0:T(8,128)(2,1)}, u32[]{:S(2)}) copy-start(bf16[512,1280]{1,0:T(8,128)(2,1)} %copy-done.4) | copy-start | bytes 3932164
  58.4 4.5 %collective-permute-start.13 = (f32[136,128]{1,0:T(8,128)S(1)}, f32[136,128]{1,0:T(8,128)S(1)}, u32[]{:S(2)}, u32[]{:S(2)}) collective-permute-start(f32[136,128]{1,0:T(8,128)S(1)} %concatenate.11), channel_id=1, source_target_pairs={{0,32},{1,33},{2,34},{3,35},{4,36},{5,37},{6,38},{7,39},{8,40},{9,... | collective-permute-start | bytes 208904 | tf_op jit(solution)/shard_map/ppermute | solution.py:120
  59.0 7.1 %collective-permute-start.12 = (bf16[512,1280]{1,0:T(8,128)(2,1)}, bf16[512,1280]{1,0:T(8,128)(2,1)}, u32[]{:S(2)}, u32[]{:S(2)}) collective-permute-start(bf16[512,1280]{1,0:T(8,128)(2,1)} %get-tuple-element.139.refs_7_.refs_9_), channel_id=1, source_target_pairs={{0,1},{1,0},{2,3},{3,2},{4,5},{5,4},{6,7},{7,6},{8,9},{9,8},{10,11... | collective-permute-start | bytes 3932168 | tf_op jit(solution)/shard_map/ppermute | solution.py:120
  59.1 34.4 %collective-permute-start.10 = (bf16[512,1280]{1,0:T(8,128)(2,1)}, bf16[512,1280]{1,0:T(8,128)(2,1)}, u32[]{:S(2)}, u32[]{:S(2)}) collective-permute-start(bf16[512,1280]{1,0:T(8,128)(2,1)} %get-tuple-element.139.refs_7_.refs_9_), channel_id=1, source_target_pairs={{0,24},{1,25},{2,26},{3,27},{4,28},{5,29},{6,30},{7,31},{8,16},{9,... | collective-permute-start | bytes 3932168 | tf_op jit(solution)/shard_map/ppermute | solution.py:120
  62.4 31.1 %collective-permute-start.9 = (bf16[512,1280]{1,0:T(8,128)(2,1)}, bf16[512,1280]{1,0:T(8,128)(2,1)S(1)}, u32[]{:S(2)}, u32[]{:S(2)}) collective-permute-start(bf16[512,1280]{1,0:T(8,128)(2,1)} %slice.69), channel_id=1, source_target_pairs={{0,8},{1,9},{2,10},{3,11},{4,12},{5,13},{6,14},{7,15},{8,0},{9,1},... | collective-permute-start | bytes 3932168 | tf_op jit(solution)/shard_map/ppermute | solution.py:120
  62.9 30.7 %collective-permute-start.7 = (bf16[512,1280]{1,0:T(8,128)(2,1)S(1)}, bf16[512,1280]{1,0:T(8,128)(2,1)S(1)}, u32[]{:S(2)}, u32[]{:S(2)}) collective-permute-start(bf16[512,1280]{1,0:T(8,128)(2,1)S(1)} %copy-done.5), channel_id=1, source_target_pairs={{0,32},{1,97},{2,34},{3,99},{4,36},{5,101},{6,38},{7,103},{8,40},{... | collective-permute-start | bytes 3932168 | tf_op jit(solution)/shard_map/ppermute | solution.py:120
  64.0 29.7 %collective-permute-start.8 = (bf16[512,1280]{1,0:T(8,128)(2,1)S(1)}, bf16[512,1280]{1,0:T(8,128)(2,1)S(1)}, u32[]{:S(2)}, u32[]{:S(2)}) collective-permute-start(bf16[512,1280]{1,0:T(8,128)(2,1)S(1)} %copy-done.5), channel_id=1, source_target_pairs={{0,96},{1,33},{2,98},{3,35},{4,100},{5,37},{6,102},{7,39},{8,104},... | collective-permute-start | bytes 3932168 | tf_op jit(solution)/shard_map/ppermute | solution.py:120
  93.5 4.4 %copy-start.6 = (bf16[512,1280]{1,0:T(8,128)(2,1)}, bf16[512,1280]{1,0:T(8,128)(2,1)S(1)}, u32[]{:S(2)}) copy-start(bf16[512,1280]{1,0:T(8,128)(2,1)S(1)} %collective-permute-done.9.refs_4_.refs_10_) | copy-start | bytes 3932164
  93.5 4.4 %copy-start.7 = (bf16[512,1280]{1,0:T(8,128)(2,1)}, bf16[512,1280]{1,0:T(8,128)(2,1)S(1)}, u32[]{:S(2)}) copy-start(bf16[512,1280]{1,0:T(8,128)(2,1)S(1)} %collective-permute-done.7.refs_2_.refs_8_) | copy-start | bytes 3932164
  93.7 4.2 %copy-start.8 = (bf16[512,1280]{1,0:T(8,128)(2,1)}, bf16[512,1280]{1,0:T(8,128)(2,1)S(1)}, u32[]{:S(2)}) copy-start(bf16[512,1280]{1,0:T(8,128)(2,1)S(1)} %collective-permute-done.8.refs_3_.refs_9_) | copy-start | bytes 3932164
  93.7 21.3 %collective-permute-start.14 = (bf16[512,1280]{1,0:T(8,128)(2,1)}, bf16[512,1280]{1,0:T(8,128)(2,1)S(1)}, u32[]{:S(2)}, u32[]{:S(2)}) collective-permute-start(bf16[512,1280]{1,0:T(8,128)(2,1)} %collective-permute-done.10.refs_5_), channel_id=1, source_target_pairs={{0,1},{1,0},{2,3},{3,2},{4,5},{5,4},{6,7},{7,6},{8,9},{9,8},{10,11... | collective-permute-start | bytes 3932168 | tf_op jit(solution)/shard_map/ppermute | solution.py:120
  94.3 20.6 %collective-permute-start.15 = (bf16[2,1024,256]{2,1,0:T(8,128)(2,1)}, bf16[2,1024,256]{2,1,0:T(8,128)(2,1)}, u32[]{:S(2)}, u32[]{:S(2)}) collective-permute-start(bf16[2,1024,256]{2,1,0:T(8,128)(2,1)} %get-tuple-element.128), channel_id=1, source_target_pairs={{0,2},{1,7},{2,0},{3,5},{4,6},{5,3},{6,4},{7,1},{8,10},{9,15},{10,... | collective-permute-start | bytes 3145736 | tf_op jit(solution)/shard_map/ppermute | solution.py:120
  96.3 18.7 %collective-permute-start.16 = (bf16[2,512,256]{2,1,0:T(8,128)(2,1)}, bf16[2,512,256]{2,1,0:T(8,128)(2,1)S(1)}, u32[]{:S(2)}, u32[]{:S(2)}) collective-permute-start(bf16[2,512,256]{2,1,0:T(8,128)(2,1)} %get-tuple-element.130), channel_id=1, source_target_pairs={{0,2},{1,7},{2,0},{3,5},{4,6},{5,3},{6,4},{7,1},{8,10},{9,15},{10,... | collective-permute-start | bytes 1572872 | tf_op jit(solution)/shard_map/ppermute | solution.py:120
  96.4 14.9 %collective-permute-start.17 = (f32[136,128]{1,0:T(8,128)S(1)}, f32[136,128]{1,0:T(8,128)S(1)}, u32[]{:S(2)}, u32[]{:S(2)}) collective-permute-start(f32[136,128]{1,0:T(8,128)S(1)} %pad_add_fusion.1), channel_id=1, source_target_pairs={{0,96},{1,97},{2,98},{3,99},{4,100},{5,101},{6,102},{7,103},{8,104... | collective-permute-start | bytes 208904 | tf_op jit(solution)/shard_map/ppermute | solution.py:120
  111.3 9.7 %copy-start.16 = (bf16[2,512,256]{2,1,0:T(8,128)(2,1)S(1)}, bf16[2,512,256]{2,1,0:T(8,128)(2,1)}, u32[]{:S(2)}) copy-start(bf16[2,512,256]{2,1,0:T(8,128)(2,1)} %get-tuple-element.176) | copy-start | bytes 1572868
  115.0 8.2 %copy-start.11 = (bf16[512,1280]{1,0:T(8,128)(2,1)}, bf16[512,1280]{1,0:T(8,128)(2,1)S(1)}, u32[]{:S(2)}) copy-start(bf16[512,1280]{1,0:T(8,128)(2,1)S(1)} %collective-permute-done.14.refs_6_) | copy-start | bytes 3932164
  116.8 19.4 %collective-permute-start.18 = (bf16[1024,256]{1,0:T(8,128)(2,1)S(1)}, bf16[1024,256]{1,0:T(8,128)(2,1)S(1)}, u32[]{:S(2)}, u32[]{:S(2)}) collective-permute-start(bf16[1024,256]{1,0:T(8,128)(2,1)S(1)} %fusion.6), channel_id=1, source_target_pairs={{0,6},{1,3},{2,4},{3,1},{4,2},{5,7},{6,0},{7,5},{8,14},{9,11},{10,... | collective-permute-start | bytes 1572872 | tf_op jit(solution)/shard_map/ppermute | solution.py:120
  120.9 15.3 %collective-permute-start.20 = (bf16[2,512,256]{2,1,0:T(8,128)(2,1)}, bf16[2,512,256]{2,1,0:T(8,128)(2,1)S(1)}, u32[]{:S(2)}, u32[]{:S(2)}) collective-permute-start(bf16[2,512,256]{2,1,0:T(8,128)(2,1)} %get-tuple-element.151), channel_id=1, source_target_pairs={{0,2},{1,7},{2,0},{3,5},{4,6},{5,3},{6,4},{7,1},{8,10},{9,15},{10,... | collective-permute-start | bytes 1572872 | tf_op jit(solution)/shard_map/ppermute | solution.py:120
  121.0 15.4 %copy-start.19 = (bf16[2,512,256]{2,1,0:T(8,128)(2,1)S(1)}, bf16[2,512,256]{2,1,0:T(8,128)(2,1)}, u32[]{:S(2)}) copy-start(bf16[2,512,256]{2,1,0:T(8,128)(2,1)} %get-tuple-element.179) | copy-start | bytes 1572868
  121.0 15.2 %collective-permute-start.19 = (bf16[512,256]{1,0:T(8,128)(2,1)S(1)}, bf16[512,256]{1,0:T(8,128)(2,1)S(1)}, u32[]{:S(2)}, u32[]{:S(2)}) collective-permute-start(bf16[512,256]{1,0:T(8,128)(2,1)S(1)} %fusion.13), channel_id=1, source_target_pairs={{0,6},{1,3},{2,4},{3,1},{4,2},{5,7},{6,0},{7,5},{8,14},{9,11},{10,... | collective-permute-start | bytes 786440 | tf_op jit(solution)/shard_map/ppermute | solution.py:120
  121.6 12.6 %collective-permute-start.21 = (f32[136,128]{1,0:T(8,128)S(1)}, f32[136,128]{1,0:T(8,128)S(1)}, u32[]{:S(2)}, u32[]{:S(2)}) collective-permute-start(f32[136,128]{1,0:T(8,128)S(1)} %add.99), channel_id=1, source_target_pairs={{0,8},{1,9},{2,10},{3,11},{4,12},{5,13},{6,14},{7,15},{8,0},{9,1},... | collective-permute-start | bytes 208904 | tf_op jit(solution)/shard_map/ppermute | solution.py:120
  136.2 17.8 %collective-permute-start.23 = (bf16[2,1024,256]{2,1,0:T(8,128)(2,1)}, bf16[2,1024,256]{2,1,0:T(8,128)(2,1)S(1)}, u32[]{:S(2)}, u32[]{:S(2)}) collective-permute-start(bf16[2,1024,256]{2,1,0:T(8,128)(2,1)} %get-tuple-element.162), channel_id=1, source_target_pairs={{0,2},{1,7},{2,0},{3,5},{4,6},{5,3},{6,4},{7,1},{8,10},{9,15},{10,... | collective-permute-start | bytes 3145736 | tf_op jit(solution)/shard_map/ppermute | solution.py:120
  136.5 10.5 %collective-permute-start.22 = (bf16[512,256]{1,0:T(8,128)(2,1)S(1)}, bf16[512,256]{1,0:T(8,128)(2,1)S(1)}, u32[]{:S(2)}, u32[]{:S(2)}) collective-permute-start(bf16[512,256]{1,0:T(8,128)(2,1)S(1)} %fusion.14), channel_id=1, source_target_pairs={{0,6},{1,3},{2,4},{3,1},{4,2},{5,7},{6,0},{7,5},{8,14},{9,11},{10,... | collective-permute-start | bytes 786440 | tf_op jit(solution)/shard_map/ppermute | solution.py:120
  139.3 5.5 %collective-permute-start.24 = (f32[136,128]{1,0:T(8,128)S(1)}, f32[136,128]{1,0:T(8,128)S(1)}, u32[]{:S(2)}, u32[]{:S(2)}) collective-permute-start(f32[136,128]{1,0:T(8,128)S(1)} %add.102), channel_id=1, source_target_pairs={{0,24},{1,25},{2,26},{3,27},{4,28},{5,29},{6,30},{7,31},{8,16},{9,... | collective-permute-start | bytes 208904 | tf_op jit(solution)/shard_map/ppermute | solution.py:120
  155.2 5.8 %copy-start.25 = (bf16[2,1024,256]{2,1,0:T(8,128)(2,1)S(1)}, bf16[2,1024,256]{2,1,0:T(8,128)(2,1)}, u32[]{:S(2)}) copy-start(bf16[2,1024,256]{2,1,0:T(8,128)(2,1)} %get-tuple-element.185) | copy-start | bytes 3145732
  155.2 5.9 %copy-start.14 = (bf16[2,1024,256]{2,1,0:T(8,128)(2,1)S(1)}, bf16[2,1024,256]{2,1,0:T(8,128)(2,1)}, u32[]{:S(2)}) copy-start(bf16[2,1024,256]{2,1,0:T(8,128)(2,1)} %get-tuple-element.192) | copy-start | bytes 3145732
  155.5 6.8 %copy-start.13 = (bf16[2,1024,256]{2,1,0:T(8,128)(2,1)S(1)}, bf16[2,1024,256]{2,1,0:T(8,128)(2,1)}, u32[]{:S(2)}) copy-start(bf16[2,1024,256]{2,1,0:T(8,128)(2,1)} %get-tuple-element.172) | copy-start | bytes 3145732
  155.5 21.8 %collective-permute-start.26 = (bf16[2,512,256]{2,1,0:T(8,128)(2,1)S(1)}, bf16[2,512,256]{2,1,0:T(8,128)(2,1)S(1)}, u32[]{:S(2)}, u32[]{:S(2)}) collective-permute-start(bf16[2,512,256]{2,1,0:T(8,128)(2,1)S(1)} %pad_maximum_fusion.1), channel_id=1, source_target_pairs={{0,24},{2,26},{4,28},{6,30},{8,16},{10,18},{12,20},{14,22},{17,9},... | collective-permute-start | bytes 1572872 | tf_op jit(solution)/shard_map/ppermute | solution.py:120
  160.1 17.2 %collective-permute-start.27 = (bf16[2,512,256]{2,1,0:T(8,128)(2,1)S(1)}, bf16[2,512,256]{2,1,0:T(8,128)(2,1)S(1)}, u32[]{:S(2)}, u32[]{:S(2)}) collective-permute-start(bf16[2,512,256]{2,1,0:T(8,128)(2,1)S(1)} %pad_maximum_fusion.1), channel_id=1, source_target_pairs={{1,24},{3,26},{5,28},{7,30},{9,16},{11,18},{13,20},{15,22},{16,9},... | collective-permute-start | bytes 1572872 | tf_op jit(solution)/shard_map/ppermute | solution.py:120
  161.1 20.5 %collective-permute-start.29 = (bf16[2,1024,256]{2,1,0:T(8,128)(2,1)S(1)}, bf16[2,1024,256]{2,1,0:T(8,128)(2,1)S(1)}, u32[]{:S(2)}, u32[]{:S(2)}) collective-permute-start(bf16[2,1024,256]{2,1,0:T(8,128)(2,1)S(1)} %copy-done.25), channel_id=1, source_target_pairs={{0,2},{1,7},{2,0},{3,5},{4,6},{5,3},{6,4},{7,1},{8,10},{9,15},{10,... | collective-permute-start | bytes 3145736 | tf_op jit(solution)/shard_map/ppermute | solution.py:120
  161.3 20.3 %copy-start.12 = (bf16[2,1024,256]{2,1,0:T(8,128)(2,1)S(1)}, bf16[2,1024,256]{2,1,0:T(8,128)(2,1)}, u32[]{:S(2)}) copy-start(bf16[2,1024,256]{2,1,0:T(8,128)(2,1)} %get-tuple-element.187) | copy-start | bytes 3145732
  161.3 16.0 %collective-permute-start.28 = (bf16[1024,256]{1,0:T(8,128)(2,1)S(1)}, bf16[1024,256]{1,0:T(8,128)(2,1)S(1)}, u32[]{:S(2)}, u32[]{:S(2)}) collective-permute-start(bf16[1024,256]{1,0:T(8,128)(2,1)S(1)} %fusion.7), channel_id=1, source_target_pairs={{0,6},{1,3},{2,4},{3,1},{4,2},{5,7},{6,0},{7,5},{8,14},{9,11},{10,... | collective-permute-start | bytes 1572872 | tf_op jit(solution)/shard_map/ppermute | solution.py:120
  163.6 19.1 %copy-start.9 = (bf16[1024,256]{1,0:T(8,128)(2,1)}, bf16[1024,256]{1,0:T(8,128)(2,1)S(1)}, u32[]{:S(2)}) copy-start(bf16[1024,256]{1,0:T(8,128)(2,1)S(1)} %fusion.5) | copy-start | bytes 1572868
  163.6 13.8 %collective-permute-start.25 = (bf16[2,512,256]{2,1,0:T(8,128)(2,1)S(1)}, bf16[2,512,256]{2,1,0:T(8,128)(2,1)S(1)}, u32[]{:S(2)}, u32[]{:S(2)}) collective-permute-start(bf16[2,512,256]{2,1,0:T(8,128)(2,1)S(1)} %bitcast.61), channel_id=1, source_target_pairs={{0,1},{1,0},{2,3},{3,2},{4,5},{5,4},{6,7},{7,6},{8,9},{9,8},{10,11... | collective-permute-start | bytes 1572872 | tf_op jit(solution)/shard_map/ppermute | solution.py:120
  177.3 5.3 %copy-start.15 = (bf16[2,512,256]{2,1,0:T(8,128)(2,1)}, bf16[2,512,256]{2,1,0:T(8,128)(2,1)S(1)}, u32[]{:S(2)}) copy-start(bf16[2,512,256]{2,1,0:T(8,128)(2,1)S(1)} %collective-permute-done.26.same0) | copy-start | bytes 1572868
  177.3 5.3 %copy-start.17 = (bf16[2,512,256]{2,1,0:T(8,128)(2,1)}, bf16[2,512,256]{2,1,0:T(8,128)(2,1)S(1)}, u32[]{:S(2)}) copy-start(bf16[2,512,256]{2,1,0:T(8,128)(2,1)S(1)} %collective-permute-done.27.other0) | copy-start | bytes 1572868
  177.4 5.3 %copy-start.18 = (bf16[2,512,256]{2,1,0:T(8,128)(2,1)}, bf16[2,512,256]{2,1,0:T(8,128)(2,1)S(1)}, u32[]{:S(2)}) copy-start(bf16[2,512,256]{2,1,0:T(8,128)(2,1)S(1)} %collective-permute-done.25.near_in) | copy-start | bytes 1572868
  181.7 10.5 %collective-permute-start.30 = (bf16[1024,256]{1,0:T(8,128)(2,1)S(1)}, bf16[1024,256]{1,0:T(8,128)(2,1)S(1)}, u32[]{:S(2)}, u32[]{:S(2)}) collective-permute-start(bf16[1024,256]{1,0:T(8,128)(2,1)S(1)} %fusion.8), channel_id=1, source_target_pairs={{0,6},{1,3},{2,4},{3,1},{4,2},{5,7},{6,0},{7,5},{8,14},{9,11},{10,... | collective-permute-start | bytes 1572872 | tf_op jit(solution)/shard_map/ppermute | solution.py:120
  182.7 10.5 %copy-start.23 = (f32[2,64,128]{2,1,0:T(8,128)S(1)}, f32[2,64,128]{2,1,0:T(8,128)}, u32[]{:S(2)}) copy-start(f32[2,64,128]{2,1,0:T(8,128)} %pre_ref.3) | copy-start | bytes 196612
  182.7 14.4 %collective-permute-start.32 = (bf16[2,512,256]{2,1,0:T(8,128)(2,1)S(1)}, bf16[2,512,256]{2,1,0:T(8,128)(2,1)S(1)}, u32[]{:S(2)}, u32[]{:S(2)}) collective-permute-start(bf16[2,512,256]{2,1,0:T(8,128)(2,1)S(1)} %bitcast.67), channel_id=1, source_target_pairs={{0,24},{2,26},{4,28},{6,30},{8,16},{10,18},{12,20},{14,22},{17,9},... | collective-permute-start | bytes 1572872 | tf_op jit(solution)/shard_map/ppermute | solution.py:120
  185.5 11.6 %collective-permute-start.33 = (bf16[2,512,256]{2,1,0:T(8,128)(2,1)S(1)}, bf16[2,512,256]{2,1,0:T(8,128)(2,1)S(1)}, u32[]{:S(2)}, u32[]{:S(2)}) collective-permute-start(bf16[2,512,256]{2,1,0:T(8,128)(2,1)S(1)} %bitcast.68), channel_id=1, source_target_pairs={{1,24},{3,26},{5,28},{7,30},{9,16},{11,18},{13,20},{15,22},{16,9},... | collective-permute-start | bytes 1572872 | tf_op jit(solution)/shard_map/ppermute | solution.py:120
  192.4 4.7 %copy-start.10 = (bf16[1024,256]{1,0:T(8,128)(2,1)}, bf16[1024,256]{1,0:T(8,128)(2,1)S(1)}, u32[]{:S(2)}) copy-start(bf16[1024,256]{1,0:T(8,128)(2,1)S(1)} %fusion.3) | copy-start | bytes 1572868
  192.4 4.6 %collective-permute-start.31 = (bf16[2,512,256]{2,1,0:T(8,128)(2,1)S(1)}, bf16[2,512,256]{2,1,0:T(8,128)(2,1)S(1)}, u32[]{:S(2)}, u32[]{:S(2)}) collective-permute-start(bf16[2,512,256]{2,1,0:T(8,128)(2,1)S(1)} %bitcast.63), channel_id=1, source_target_pairs={{0,1},{1,0},{2,3},{3,2},{4,5},{5,4},{6,7},{7,6},{8,9},{9,8},{10,11... | collective-permute-start | bytes 1572872 | tf_op jit(solution)/shard_map/ppermute | solution.py:120
  197.0 0.8 copy-start.20
  197.0 1.0 copy-start.21
  198.0 0.8 copy-start.22

commit v4 on v3

--- a/solution.py
+++ b/solution.py
@@ -265,38 +265,45 @@
     return [(out[2 * at], out[2 * at + 1]) for at in range(len(out_rows))]
 
 
-def arrange_kernel(info, near, mate, near_in, mate_in, same0, same1, other0, other1, out_ref):
+def arrange_kernel(info, near, mate, near_in, mate_in, same0, same1, other0, other1, out_ref, sems):
     at_home, near_at, own_at = info[0], info[1], info[2]
     size = near.shape[1]
 
-    def put(value, row, base, core_at):
-        col = pl.multiple_of(base * 512 + core_at * 256, 256)
-        out_ref[row * size : (row + 1) * size, pl.ds(col, 256)] = value
+    def put(pieces):
+        copies = []
+        for value, row, base, core_at in pieces:
+            col = pl.multiple_of(base * 512 + core_at * 256, 256)
+            target = out_ref.at[row * size : (row + 1) * size, pl.ds(col, 256)]
+            copies.append(pltpu.make_async_copy(value, target, sems.at[len(copies)]))
+            copies[-1].start()
+        for copy in copies:
+            copy.wait()
 
     @pl.when(at_home == 1)
     def _():
+        pieces = []
         for row in range(2):
-            put(near[row], row, near_at, own_at)
-            put(mate[row], row, 1 - near_at, own_at)
-            put(near_in[row], row, near_at, 1 - own_at)
-            put(mate_in[row], row, 1 - near_at, 1 - own_at)
+            pieces += [(near.at[row], row, near_at, own_at), (mate.at[row], row, 1 - near_at, own_at)]
+            pieces += [(near_in.at[row], row, near_at, 1 - own_at), (mate_in.at[row], row, 1 - near_at, 1 - own_at)]
+        put(pieces)
 
     @pl.when(at_home == 0)
     def _():
+        pieces = []
         for row, (same, other) in enumerate(((same0, other0), (same1, other1))):
-            put(same[0], row, near_at, own_at)
-            put(same[1], row, 1 - near_at, own_at)
-            put(other[0], row, near_at, 1 - own_at)
-            put(other[1], row, 1 - near_at, 1 - own_at)
+            pieces += [(same.at[0], row, near_at, own_at), (same.at[1], row, 1 - near_at, own_at)]
+            pieces += [(other.at[0], row, near_at, 1 - own_at), (other.at[1], row, 1 - near_at, 1 - own_at)]
+        put(pieces)
 
 
 def arrange(info, *parts):
-    vmem = pl.BlockSpec(memory_space=pltpu.VMEM)
+    hbm = pl.BlockSpec(memory_space=pl.ANY)
     return pl.pallas_call(
         arrange_kernel,
-        in_specs=[pl.BlockSpec(memory_space=pltpu.SMEM)] + [vmem] * 8,
-        out_specs=vmem,
+        in_specs=[pl.BlockSpec(memory_space=pltpu.SMEM)] + [hbm] * 8,
+        out_specs=pl.BlockSpec(memory_space=pltpu.VMEM),
         out_shape=jax.ShapeDtypeStruct((1024, 1024), jnp.bfloat16),
+        scratch_shapes=[pltpu.SemaphoreType.DMA((8,))],
         compiler_params=pltpu.CompilerParams(vmem_limit_bytes=58 * 2**20),
         name="arrange",
     )(info, *parts)
@@ -338,7 +345,6 @@
     turned, mate, pair0, self0_other, self1, terms1, terms0, mine, self0 = gate(
         (turned, mate, pair0, self0_other, self1, terms1, terms0, mine, self0)
     )
-    terms = jnp.concatenate([(terms0 + terms1).reshape(2 * PREFIX, HD), count_row], 0)
     near_blocks = [
         ((mine, 0), (mine, rows)),
         ((side_a, 0), (side_b, 0)),
@@ -366,29 +372,31 @@
     mate_far = send(turned[2 * rows :], y_mate)
     pair1 = send(self1, y_partner)
     both0, both1, there0 = (self0, self0_other), (self1, self1_other), (pair0, pair0_other)
-    sn, p0n = project(places, [(near_blocks, [both0, both1, there0], [(0, 0), (0, SEQ), (1, 0)])])
-    terms = terms + send(terms, x_mate)
-    mate_side, mate_turn, mate_far, pair1, there0, both0, both1, sn, p0n, mate, terms = gate(
-        (mate_side, mate_turn, mate_far, pair1, there0, both0, both1, sn, p0n, mate, terms)
+    early = project(places, [(near_blocks, [both0, both1, there0], [(0, 0), (0, SEQ), (0, 2 * SEQ)])])[0]
+    mate_side, mate_turn, mate_far, pair1, there0, both0, both1, early, mate, terms0, terms1 = gate(
+        (mate_side, mate_turn, mate_far, pair1, there0, both0, both1, early, mate, terms0, terms1)
     )
     mate_blocks = [((array, 0), (array, rows)) for array in (mate, mate_side, mate_turn, mate_far)]
     pair1_other = send(pair1, sibling)
-    sn, p0n = start_unit(sn), start_unit(p0n)
+    early = start_unit(early)
+    terms = jnp.concatenate([(terms0 + terms1).reshape(2 * PREFIX, HD), count_row], 0)
+    terms = terms + send(terms, x_mate)
+    p0m, sm = project(places, [(mate_blocks, [there0, both0, both1], [(0, 0), (1, 0), (1, SEQ)])])
+    pair1_other, early, p0m, pair1, terms, sm = gate((pair1_other, early, p0m, pair1, terms, sm))
+    early, p0m = pass_on(early), start_unit(p0m)
+    there1 = (pair1, pair1_other)
     terms = terms + send(terms, x_cross)
-    p0m, sm = project(places, [(mate_blocks, [there0, both0, both1], [(0, 0), (1, 0), (1, SEQ)])])
-    pair1_other, sn, p0n, p0m, pair1, terms, sm = gate((pair1_other, sn, p0n, p0m, pair1, terms, sm))
-    sn, p0n, p0m = pass_on(sn), pass_on(p0n), start_unit(p0m)
-    there1 = (pair1, pair1_other)
+    p1 = project(places, [(near_blocks, [there1], [(0, 0)]), (mate_blocks, [there1], [(0, SEQ)])])[0]
+    early, p0m, p1, terms, sm = gate((early, p0m, p1, terms, sm))
+    p0m, p1 = pass_on(p0m), start_unit(p1)
     terms = terms + send(terms, y_mate)
-    p1 = project(places, [(near_blocks, [there1], [(0, 0)]), (mate_blocks, [there1], [(0, SEQ)])])[0]
-    sn, p0n, p0m, p1, terms, sm = gate((sn, p0n, p0m, p1, terms, sm))
-    p0m, p1 = pass_on(p0m), start_unit(p1)
     terms = terms + send(terms, y_partner)
-    p0m, p1, terms, p0n, sn, sm = gate((p0m, p1, terms, p0n, sn, sm))
+    p0m, p1, terms, early, sm = gate((p0m, p1, terms, early, sm))
     loss_scale = 16384.0 / terms[2 * PREFIX, 0]
     p1, sm = pass_on(p1), start_unit(sm)
-    near = finish(sn).reshape(2, SEQ, 256)
-    pair0 = jnp.stack([finish(p0n), finish(p0m)])
+    early = finish(early)
+    near = early[: 2 * SEQ].reshape(2, SEQ, 256)
+    pair0 = jnp.stack([early[2 * SEQ :], finish(p0m)])
     same0, other0 = send(pair0, home_same), send(pair0, home_other)
     near_in = send(near, sibling)
     near_in, same0, other0, p1, sm, loss_scale, near = gate((near_in, same0, other0, p1, sm, loss_scale, near))

time: 207 us -> 197 us (0.952)
  waiting for transfers between devices: 83.6 us -> 72.2 us
  starting transfers between devices: 41 us -> 43.9 us
    ppermute x34 -> x32, waiting for transfers between devices: 83.6 us -> 72.2 us  [send(): return lax.ppermute(array, AXES, pairs_of(move))]
    ppermute x34 -> x32, starting transfers between devices: 41 us -> 43.9 us  [send(): return lax.ppermute(array, AXES, pairs_of(move))]
  transfers between devices with their start and end apart: 34 -> 32, of which waited for: 16 -> 15; matrix products, arithmetic and copies ran while one was open for 3% -> 4% of each run, Pallas kernels for 28% -> 29%
where the time goes in v4:
time: 197 us; the launch traced here: 194 us
  waiting for transfers between devices  72.2 us (37%)
  Pallas kernels  60.6 us (31%)
  starting transfers between devices  43.9 us (22%)
  other arithmetic  9.04 us (5%)
  local copies, waits for them, and re-layouts  5.63 us (3%)
  between operations  2.69 us (1%)
    ppermute x32, waiting for transfers between devices, send(): return lax.ppermute(array, AXES, pairs_of(move))  72.2 us
    ppermute x32, starting transfers between devices, send(): return lax.ppermute(array, AXES, pairs_of(move))  43.9 us
    pallas_call x3, Pallas kernels, project(): pl.pallas_call(functools.partial(project_kernel, (sides, plan, len(out_ro...  37.5 us
    pallas_call x2, Pallas kernels, attention(): pl.pallas_call(functools.partial(attn_kernel, prompt=prompt), grid=(GROUP...  19.6 us
  transfers between devices with their start and end apart: 32, of which 15 were waited for; matrix products, arithmetic and copies ran while one was open for 4% of the time, Pallas kernels for 29%

profile of v4, /device:TPU:2, one launch (start us, length us, event | category | flops | bytes accessed | tf_op | source)
XLA Modules:
  0.0 194.1 jit_solution(2432898193868183924)
XLA Ops:
  0.7 1.4 constant_dynamic-slice_fusion
  2.0 0.7 compare_select_fusion.2.refs_0_
  2.7 0.5 collective-permute-start
  3.2 0.7 collective-permute-start.1
  3.9 1.0 collective-permute-start.2
  4.8 9.8 %attention_backward.2 = (bf16[512,1280]{1,0:T(8,128)(2,1)}, f32[2,64,128]{2,1,0:T(8,128)}) custom-call(s32[2]{0:T(128)} %len_ref.3, bf16[1024,1024]{1,0:T(8,128)(2,1)} %q_ref.3, bf16[1024,1024]{1,0:T(8,128)(2,1)} %g_ref.3, bf16[1024,128]{1,0:T(8,128)(2,1)} %k_ref.2, bf16[1024,128]{1,0:T(8,128)(2,1)} %v_ref.3, f32[2,64,128]{2,1,0:T(8,128)} %pre_ref.3, ...), custom_call_target="tpu_custom_call" | custom-call | flops 3019898880 | bytes 4194304 | tf_op jit(solution)/shard_map/attention_backward/pallas_call | solution.py:82
  14.6 5.6 %collective-permute-done.refs_2_ = bf16[256,1280]{1,0:T(8,128)(2,1)S(1)} collective-permute-done((bf16[256,1280]{1,0:T(8,128)(2,1)S(1)}, bf16[256,1280]{1,0:T(8,128)(2,1)S(1)}, u32[]{:S(2)}, u32[]{:S(2)}) %collective-permute-start) | collective-permute-done | bytes 655392 | tf_op jit(solution)/shard_map/ppermute | solution.py:120
  20.3 1.8 pad_maximum_fusion
  22.1 1.4 collective-permute-start.3
  23.6 1.7 collective-permute-start.4
  25.3 2.2 %collective-permute-start.5 = (bf16[512,1280]{1,0:T(8,128)(2,1)}, bf16[512,1280]{1,0:T(8,128)(2,1)}, u32[]{:S(2)}, u32[]{:S(2)}) collective-permute-start(bf16[512,1280]{1,0:T(8,128)(2,1)} %get-tuple-element.122.refs_5_.refs_7_), channel_id=1, source_target_pairs={{0,24},{1,25},{2,26},{3,27},{4,28},{5,29},{6,30},{7,31},{8,16},{9,... | collective-permute-start | bytes 3932168 | tf_op jit(solution)/shard_map/ppermute | solution.py:120
  27.5 9.8 %attention_backward.3 = (bf16[512,1280]{1,0:T(8,128)(2,1)}, f32[2,64,128]{2,1,0:T(8,128)}) custom-call(s32[2]{0:T(128)} %len_ref.3, bf16[1024,1024]{1,0:T(8,128)(2,1)} %q_ref.3, bf16[1024,1024]{1,0:T(8,128)(2,1)} %g_ref.3, bf16[1024,128]{1,0:T(8,128)(2,1)} %k_ref.2, bf16[1024,128]{1,0:T(8,128)(2,1)} %v_ref.3, f32[2,64,128]{2,1,0:T(8,128)} %pre_ref.3, ...), custom_call_target="tpu_custom_call" | custom-call | flops 3019898880 | bytes 4194304 | tf_op jit(solution)/shard_map/attention_backward/pallas_call | solution.py:82
  37.3 15.6 %collective-permute-done.4.refs_1_.refs_7_ = bf16[512,1280]{1,0:T(8,128)(2,1)S(1)} collective-permute-done((bf16[512,1280]{1,0:T(8,128)(2,1)S(1)}, bf16[512,1280]{1,0:T(8,128)(2,1)S(1)}, u32[]{:S(2)}, u32[]{:S(2)}) %collective-permute-start.4) | collective-permute-done | bytes 1310752 | tf_op jit(solution)/shard_map/ppermute | solution.py:120
  52.9 3.0 %collective-permute-done.5.refs_9_.refs_5_ = bf16[512,1280]{1,0:T(8,128)(2,1)} collective-permute-done((bf16[512,1280]{1,0:T(8,128)(2,1)}, bf16[512,1280]{1,0:T(8,128)(2,1)}, u32[]{:S(2)}, u32[]{:S(2)}) %collective-permute-start.5) | collective-permute-done | bytes 1310752 | tf_op jit(solution)/shard_map/ppermute | solution.py:120
  56.0 0.5 collective-permute-start.12
  56.5 2.2 %collective-permute-start.10 = (bf16[512,1280]{1,0:T(8,128)(2,1)}, bf16[512,1280]{1,0:T(8,128)(2,1)}, u32[]{:S(2)}, u32[]{:S(2)}) collective-permute-start(bf16[512,1280]{1,0:T(8,128)(2,1)} %get-tuple-element.124.refs_7_.refs_9_), channel_id=1, source_target_pairs={{0,24},{1,25},{2,26},{3,27},{4,28},{5,29},{6,30},{7,31},{8,16},{9,... | collective-permute-start | bytes 3932168 | tf_op jit(solution)/shard_map/ppermute | solution.py:120
  58.7 1.2 slice.63
  59.8 0.7 collective-permute-start.7
  60.5 2.1 %collective-permute-start.8 = (bf16[512,1280]{1,0:T(8,128)(2,1)S(1)}, bf16[512,1280]{1,0:T(8,128)(2,1)}, u32[]{:S(2)}, u32[]{:S(2)}) collective-permute-start(bf16[512,1280]{1,0:T(8,128)(2,1)S(1)} %collective-permute-done.4.refs_1_.refs_7_), channel_id=1, source_target_pairs={{0,96},{1,33},{2,98},{3,35},{4,100},{5,37},{6,102},{7,39},{8,104},... | collective-permute-start | bytes 3932168 | tf_op jit(solution)/shard_map/ppermute | solution.py:120
  62.6 13.2 %project.3 = (bf16[2,1536,256]{2,1,0:T(8,128)(2,1)}, bf16[2,1536,256]{2,1,0:T(8,128)(2,1)}) custom-call(s32[4]{0:T(128)} %compare_select_fusion.2.refs_0_, bf16[512,1280]{1,0:T(8,128)(2,1)} %copy-done.1, bf16[256,1280]{1,0:T(8,128)(2,1)} %copy-done.2, bf16[256,1280]{1,0:T(8,128)(2,1)} %copy-done.3, bf16[1024,1280]{1,0:T(8,128)(2,1)} %copy-done, ...), custom_call_target="tpu_custom_call" | custom-call | tf_op jit(solution)/shard_map/project/pallas_call | solution.py:251
  75.9 14.6 %collective-permute-done.9.refs_4_.refs_10_ = bf16[512,1280]{1,0:T(8,128)(2,1)S(1)} collective-permute-done((bf16[512,1280]{1,0:T(8,128)(2,1)}, bf16[512,1280]{1,0:T(8,128)(2,1)S(1)}, u32[]{:S(2)}, u32[]{:S(2)}) %collective-permute-start.9) | collective-permute-done | bytes 1310752 | tf_op jit(solution)/shard_map/ppermute | solution.py:120
  90.5 0.5 collective-permute-done.7.refs_2_.refs_8_
  91.0 0.6 copy-done.5
  91.6 1.9 collective-permute-start.14
  93.5 1.7 collective-permute-start.13
  95.2 0.7 reduce_sum.9
  96.7 0.9 collective-permute-start.15
  97.7 13.2 %project.4 = (bf16[2,512,256]{2,1,0:T(8,128)(2,1)}, bf16[2,512,256]{2,1,0:T(8,128)(2,1)}, bf16[2,1024,256]{2,1,0:T(8,128)(2,1)}, bf16[2,1024,256]{2,1,0:T(8,128)(2,1)}) custom-call(s32[4]{0:T(128)} %compare_select_fusion.2.refs_0_, bf16[512,1280]{1,0:T(8,128)(2,1)} %copy-done.4, bf16[512,1280]{1,0:T(8,128)(2,1)} %collective-permute-done.7.refs_2_.refs_8_, ...), custom_call_target="tpu_custom_call" | custom-call | tf_op jit(solution)/shard_map/project/pallas_call | solution.py:251
  111.0 1.2 collective-permute-done.14
  112.2 0.2 fusion.6
  112.4 4.1 %collective-permute-start.16 = (bf16[1536,256]{1,0:T(8,128)(2,1)S(1)}, bf16[1536,256]{1,0:T(8,128)(2,1)}, u32[]{:S(2)}, u32[]{:S(2)}) collective-permute-start(bf16[1536,256]{1,0:T(8,128)(2,1)S(1)} %fusion.6), channel_id=1, source_target_pairs={{0,6},{1,3},{2,4},{3,1},{4,2},{5,7},{6,0},{7,5},{8,14},{9,11},{10,... | collective-permute-start | bytes 2359304 | tf_op jit(solution)/shard_map/ppermute | solution.py:120
  116.6 2.2 %collective-permute-start.18 = (f32[136,128]{1,0:T(8,128)S(1)}, f32[136,128]{1,0:T(8,128)S(1)}, u32[]{:S(2)}, u32[]{:S(2)}) collective-permute-start(f32[136,128]{1,0:T(8,128)S(1)} %pad_add_fusion.1), channel_id=1, source_target_pairs={{0,96},{1,97},{2,98},{3,99},{4,100},{5,101},{6,102},{7,103},{8,104... | collective-permute-start | bytes 208904 | tf_op jit(solution)/shard_map/ppermute | solution.py:120
  118.7 11.0 %project.5 = (bf16[2,1024,256]{2,1,0:T(8,128)(2,1)}, bf16[2,1024,256]{2,1,0:T(8,128)(2,1)}) custom-call(s32[4]{0:T(128)} %compare_select_fusion.2.refs_0_, bf16[512,1280]{1,0:T(8,128)(2,1)} %copy-done.1, bf16[256,1280]{1,0:T(8,128)(2,1)} %copy-done.2, bf16[256,1280]{1,0:T(8,128)(2,1)} %copy-done.3, bf16[1024,1280]{1,0:T(8,128)(2,1)} %copy-done, ...), custom_call_target="tpu_custom_call" | custom-call | tf_op jit(solution)/shard_map/project/pallas_call | solution.py:251
  129.7 0.6 collective-permute-done.17
  130.3 1.5 collective-permute-done.16
  131.8 0.3 collective-permute-start.20
  132.1 1.0 fusion.11
  133.2 2.7 %collective-permute-start.19 = (bf16[512,256]{1,0:T(8,128)(2,1)S(1)}, bf16[512,256]{1,0:T(8,128)(2,1)S(1)}, u32[]{:S(2)}, u32[]{:S(2)}) collective-permute-start(bf16[512,256]{1,0:T(8,128)(2,1)S(1)} %fusion.11), channel_id=1, source_target_pairs={{0,6},{1,3},{2,4},{3,1},{4,2},{5,7},{6,0},{7,5},{8,14},{9,11},{10,... | collective-permute-start | bytes 786440 | tf_op jit(solution)/shard_map/ppermute | solution.py:120
  135.9 1.9 collective-permute-start.21
  137.8 2.4 %collective-permute-done.21 = f32[136,128]{1,0:T(8,128)S(1)} collective-permute-done((f32[136,128]{1,0:T(8,128)S(1)}, f32[136,128]{1,0:T(8,128)S(1)}, u32[]{:S(2)}, u32[]{:S(2)}) %collective-permute-start.21) | collective-permute-done | bytes 69664 | tf_op jit(solution)/shard_map/ppermute | solution.py:120
  140.2 1.1 collective-permute-start.22
  141.3 4.5 %collective-permute-done.22 = f32[136,128]{1,0:T(8,128)S(1)} collective-permute-done((f32[136,128]{1,0:T(8,128)S(1)}, f32[136,128]{1,0:T(8,128)S(1)}, u32[]{:S(2)}, u32[]{:S(2)}) %collective-permute-start.22) | collective-permute-done | bytes 69664 | tf_op jit(solution)/shard_map/ppermute | solution.py:120
  145.8 3.8 %collective-permute-done.20 = bf16[2,1024,256]{2,1,0:T(8,128)(2,1)S(1)} collective-permute-done((bf16[2,1024,256]{2,1,0:T(8,128)(2,1)}, bf16[2,1024,256]{2,1,0:T(8,128)(2,1)S(1)}, u32[]{:S(2)}, u32[]{:S(2)}) %collective-permute-start.20) | collective-permute-done | bytes 1048608 | tf_op jit(solution)/shard_map/ppermute | solution.py:120
  149.6 0.5 slice.70
  150.1 0.3 collective-permute-start.27
  151.2 1.1 fusion.12
  152.2 1.5 fusion.1
  153.8 3.1 %collective-permute-start.24 = (bf16[2,512,256]{2,1,0:T(8,128)(2,1)S(1)}, bf16[2,512,256]{2,1,0:T(8,128)(2,1)S(1)}, u32[]{:S(2)}, u32[]{:S(2)}) collective-permute-start(bf16[2,512,256]{2,1,0:T(8,128)(2,1)S(1)} %pad_maximum_fusion.1), channel_id=1, source_target_pairs={{0,24},{2,26},{4,28},{6,30},{8,16},{10,18},{12,20},{14,22},{17,9},... | collective-permute-start | bytes 1572872 | tf_op jit(solution)/shard_map/ppermute | solution.py:120
  157.0 0.7 collective-permute-start.25
  157.8 1.5 collective-permute-start.26
  159.4 0.8 collective-permute-start.23
  160.1 9.5 %collective-permute-done.26 = bf16[1024,256]{1,0:T(8,128)(2,1)S(1)} collective-permute-done((bf16[1024,256]{1,0:T(8,128)(2,1)S(1)}, bf16[1024,256]{1,0:T(8,128)(2,1)S(1)}, u32[]{:S(2)}, u32[]{:S(2)}) %collective-permute-start.26) | collective-permute-done | bytes 524320 | tf_op jit(solution)/shard_map/ppermute | solution.py:120
  169.9 3.0 %collective-permute-start.28 = (bf16[1024,256]{1,0:T(8,128)(2,1)S(1)}, bf16[1024,256]{1,0:T(8,128)(2,1)S(1)}, u32[]{:S(2)}, u32[]{:S(2)}) collective-permute-start(bf16[1024,256]{1,0:T(8,128)(2,1)S(1)} %fusion.8), channel_id=1, source_target_pairs={{0,6},{1,3},{2,4},{3,1},{4,2},{5,7},{6,0},{7,5},{8,14},{9,11},{10,... | collective-permute-start | bytes 1572872 | tf_op jit(solution)/shard_map/ppermute | solution.py:120
  172.9 0.2 fusion.3
  173.2 3.7 %collective-permute-start.30 = (bf16[2,512,256]{2,1,0:T(8,128)(2,1)S(1)}, bf16[2,512,256]{2,1,0:T(8,128)(2,1)S(1)}, u32[]{:S(2)}, u32[]{:S(2)}) collective-permute-start(bf16[2,512,256]{2,1,0:T(8,128)(2,1)S(1)} %bitcast.57), channel_id=1, source_target_pairs={{0,24},{2,26},{4,28},{6,30},{8,16},{10,18},{12,20},{14,22},{17,9},... | collective-permute-start | bytes 1572872 | tf_op jit(solution)/shard_map/ppermute | solution.py:120
  177.0 0.7 collective-permute-start.31
  177.7 2.7 %collective-permute-done.28 = bf16[1024,256]{1,0:T(8,128)(2,1)S(1)} collective-permute-done((bf16[1024,256]{1,0:T(8,128)(2,1)S(1)}, bf16[1024,256]{1,0:T(8,128)(2,1)S(1)}, u32[]{:S(2)}, u32[]{:S(2)}) %collective-permute-start.28) | collective-permute-done | bytes 524320 | tf_op jit(solution)/shard_map/ppermute | solution.py:120
  180.4 0.2 fusion.5
  180.7 0.6 pad_add_fusion.info
  181.4 0.6 sub.26
  182.0 6.5 %collective-permute-done.30.same1 = bf16[2,512,256]{2,1,0:T(8,128)(2,1)S(1)} collective-permute-done((bf16[2,512,256]{2,1,0:T(8,128)(2,1)S(1)}, bf16[2,512,256]{2,1,0:T(8,128)(2,1)S(1)}, u32[]{:S(2)}, u32[]{:S(2)}) %collective-permute-start.30) | collective-permute-done | bytes 524320 | tf_op jit(solution)/shard_map/ppermute | solution.py:120
  188.6 0.8 copy-done.15
  189.5 0.8 copy-done.17
  190.3 3.6 %arrange.1 = bf16[1024,1024]{1,0:T(8,128)(2,1)} custom-call(s32[3]{0:T(128)} %pad_add_fusion.info, bf16[2,512,256]{2,1,0:T(8,128)(2,1)} %bitcast.54, bf16[2,512,256]{2,1,0:T(8,128)(2,1)} %bitcast.52, bf16[2,512,256]{2,1,0:T(8,128)(2,1)} %copy-done.14, bf16[2,512,256]{2,1,0:T(8,128)(2,1)} %copy-done.17, bf16[2,512,256]{2,1,0:T(8,128)(2,1)} %copy-done.12, ...), custom_call_target="tpu_custom_call" | custom-call | tf_op jit(solution)/shard_map/arrange/pallas_call | solution.py:301
  (80 shorter events, 1.2 us)
Async XLA Ops:
  2.7 17.5 %collective-permute-start = (bf16[256,1280]{1,0:T(8,128)(2,1)S(1)}, bf16[256,1280]{1,0:T(8,128)(2,1)S(1)}, u32[]{:S(2)}, u32[]{:S(2)}) collective-permute-start(bf16[256,1280]{1,0:T(8,128)(2,1)S(1)} %get-tuple-element.92), channel_id=1, source_target_pairs={{0,32},{1,97},{2,34},{3,99},{4,36},{5,101},{6,38},{7,103},{8,40},{... | collective-permute-start | bytes 1966088 | tf_op jit(solution)/shard_map/ppermute | solution.py:120
  3.2 17.2 %collective-permute-start.1 = (bf16[256,1280]{1,0:T(8,128)(2,1)S(1)}, bf16[256,1280]{1,0:T(8,128)(2,1)S(1)}, u32[]{:S(2)}, u32[]{:S(2)}) collective-permute-start(bf16[256,1280]{1,0:T(8,128)(2,1)S(1)} %get-tuple-element.89), channel_id=1, source_target_pairs={{0,97},{1,32},{2,99},{3,34},{4,101},{5,36},{6,103},{7,38},{8,105},... | collective-permute-start | bytes 1966088 | tf_op jit(solution)/shard_map/ppermute | solution.py:120
  3.9 16.4 %collective-permute-start.2 = (bf16[256,1280]{1,0:T(8,128)(2,1)S(1)}, bf16[256,1280]{1,0:T(8,128)(2,1)S(1)}, u32[]{:S(2)}, u32[]{:S(2)}) collective-permute-start(bf16[256,1280]{1,0:T(8,128)(2,1)S(1)} %get-tuple-element.89), channel_id=1, source_target_pairs={{0,1},{1,0},{2,3},{3,2},{4,5},{5,4},{6,7},{7,6},{8,9},{9,8},{10,11... | collective-permute-start | bytes 1966088 | tf_op jit(solution)/shard_map/ppermute | solution.py:120
  20.2 1.9 copy-start.2
  20.3 1.8 copy-start.3
  22.1 33.8 %collective-permute-start.3 = (bf16[1024,1280]{1,0:T(8,128)(2,1)}, bf16[1024,1280]{1,0:T(8,128)(2,1)S(1)}, u32[]{:S(2)}, u32[]{:S(2)}) collective-permute-start(bf16[1024,1280]{1,0:T(8,128)(2,1)} %pad_maximum_fusion), channel_id=1, source_target_pairs={{0,96},{1,33},{2,98},{3,35},{4,100},{5,37},{6,102},{7,39},{8,104},... | collective-permute-start | bytes 7864328 | tf_op jit(solution)/shard_map/ppermute | solution.py:120
  23.6 13.6 %copy-start.1 = (bf16[512,1280]{1,0:T(8,128)(2,1)}, bf16[512,1280]{1,0:T(8,128)(2,1)S(1)}, u32[]{:S(2)}) copy-start(bf16[512,1280]{1,0:T(8,128)(2,1)S(1)} %constant_dynamic-update-slice_fusion.refs_1_) | copy-start | bytes 3932164
  23.6 29.3 %collective-permute-start.4 = (bf16[512,1280]{1,0:T(8,128)(2,1)S(1)}, bf16[512,1280]{1,0:T(8,128)(2,1)S(1)}, u32[]{:S(2)}, u32[]{:S(2)}) collective-permute-start(bf16[512,1280]{1,0:T(8,128)(2,1)S(1)} %constant_dynamic-update-slice_fusion.refs_1_), channel_id=1, source_target_pairs={{0,8},{1,9},{2,10},{3,11},{4,12},{5,13},{6,14},{7,15},{8,0},{9,1},... | collective-permute-start | bytes 3932168 | tf_op jit(solution)/shard_map/ppermute | solution.py:120
  25.3 30.6 %collective-permute-start.5 = (bf16[512,1280]{1,0:T(8,128)(2,1)}, bf16[512,1280]{1,0:T(8,128)(2,1)}, u32[]{:S(2)}, u32[]{:S(2)}) collective-permute-start(bf16[512,1280]{1,0:T(8,128)(2,1)} %get-tuple-element.122.refs_5_.refs_7_), channel_id=1, source_target_pairs={{0,24},{1,25},{2,26},{3,27},{4,28},{5,29},{6,30},{7,31},{8,16},{9,... | collective-permute-start | bytes 3932168 | tf_op jit(solution)/shard_map/ppermute | solution.py:120
  27.5 28.4 %collective-permute-start.6 = (bf16[512,1280]{1,0:T(8,128)(2,1)}, bf16[512,1280]{1,0:T(8,128)(2,1)}, u32[]{:S(2)}, u32[]{:S(2)}) collective-permute-start(bf16[512,1280]{1,0:T(8,128)(2,1)} %get-tuple-element.122.refs_5_.refs_7_), channel_id=1, source_target_pairs={{0,1},{1,0},{2,3},{3,2},{4,5},{5,4},{6,7},{7,6},{8,9},{9,8},{10,11... | collective-permute-start | bytes 3932168 | tf_op jit(solution)/shard_map/ppermute | solution.py:120
  52.9 23.0 %copy-start.4 = (bf16[512,1280]{1,0:T(8,128)(2,1)}, bf16[512,1280]{1,0:T(8,128)(2,1)S(1)}, u32[]{:S(2)}) copy-start(bf16[512,1280]{1,0:T(8,128)(2,1)S(1)} %collective-permute-done.4.refs_1_.refs_7_) | copy-start | bytes 3932164
  55.9 6.7 %copy-start = (bf16[1024,1280]{1,0:T(8,128)(2,1)}, bf16[1024,1280]{1,0:T(8,128)(2,1)S(1)}, u32[]{:S(2)}) copy-start(bf16[1024,1280]{1,0:T(8,128)(2,1)S(1)} %collective-permute-done.3.refs_4_) | copy-start | bytes 7864324
  55.9 4.6 %collective-permute-start.11 = (bf16[512,1280]{1,0:T(8,128)(2,1)}, bf16[512,1280]{1,0:T(8,128)(2,1)}, u32[]{:S(2)}, u32[]{:S(2)}) collective-permute-start(bf16[512,1280]{1,0:T(8,128)(2,1)} %collective-permute-done.5.refs_9_.refs_5_), channel_id=1, source_target_pairs={{0,1},{1,0},{2,3},{3,2},{4,5},{5,4},{6,7},{7,6},{8,9},{9,8},{10,11... | collective-permute-start | bytes 3932168 | tf_op jit(solution)/shard_map/ppermute | solution.py:120
  56.0 6.6 %collective-permute-start.12 = (bf16[512,1280]{1,0:T(8,128)(2,1)}, bf16[512,1280]{1,0:T(8,128)(2,1)}, u32[]{:S(2)}, u32[]{:S(2)}) collective-permute-start(bf16[512,1280]{1,0:T(8,128)(2,1)} %get-tuple-element.124.refs_7_.refs_9_), channel_id=1, source_target_pairs={{0,1},{1,0},{2,3},{3,2},{4,5},{5,4},{6,7},{7,6},{8,9},{9,8},{10,11... | collective-permute-start | bytes 3932168 | tf_op jit(solution)/shard_map/ppermute | solution.py:120
  56.5 34.1 %collective-permute-start.10 = (bf16[512,1280]{1,0:T(8,128)(2,1)}, bf16[512,1280]{1,0:T(8,128)(2,1)}, u32[]{:S(2)}, u32[]{:S(2)}) collective-permute-start(bf16[512,1280]{1,0:T(8,128)(2,1)} %get-tuple-element.124.refs_7_.refs_9_), channel_id=1, source_target_pairs={{0,24},{1,25},{2,26},{3,27},{4,28},{5,29},{6,30},{7,31},{8,16},{9,... | collective-permute-start | bytes 3932168 | tf_op jit(solution)/shard_map/ppermute | solution.py:120
  59.8 35.4 %copy-start.22 = (s32[2]{0:T(128)S(1)}, s32[2]{0:T(128)}, u32[]{:S(2)}) copy-start(s32[2]{0:T(128)} %len_ref.3) | copy-start | bytes 28
  59.8 36.8 %copy-start.20 = (f32[2,64,128]{2,1,0:T(8,128)S(1)}, f32[2,64,128]{2,1,0:T(8,128)}, u32[]{:S(2)}) copy-start(f32[2,64,128]{2,1,0:T(8,128)} %get-tuple-element.128) | copy-start | bytes 196612
  59.8 36.9 %copy-start.21 = (f32[2,64,128]{2,1,0:T(8,128)S(1)}, f32[2,64,128]{2,1,0:T(8,128)}, u32[]{:S(2)}) copy-start(f32[2,64,128]{2,1,0:T(8,128)} %get-tuple-element.129) | copy-start | bytes 196612
  59.8 30.7 %collective-permute-start.9 = (bf16[512,1280]{1,0:T(8,128)(2,1)}, bf16[512,1280]{1,0:T(8,128)(2,1)S(1)}, u32[]{:S(2)}, u32[]{:S(2)}) collective-permute-start(bf16[512,1280]{1,0:T(8,128)(2,1)} %slice.63), channel_id=1, source_target_pairs={{0,8},{1,9},{2,10},{3,11},{4,12},{5,13},{6,14},{7,15},{8,0},{9,1},... | collective-permute-start | bytes 3932168 | tf_op jit(solution)/shard_map/ppermute | solution.py:120
  59.8 31.2 %collective-permute-start.7 = (bf16[512,1280]{1,0:T(8,128)(2,1)S(1)}, bf16[512,1280]{1,0:T(8,128)(2,1)}, u32[]{:S(2)}, u32[]{:S(2)}) collective-permute-start(bf16[512,1280]{1,0:T(8,128)(2,1)S(1)} %collective-permute-done.4.refs_1_.refs_7_), channel_id=1, source_target_pairs={{0,32},{1,97},{2,34},{3,99},{4,36},{5,101},{6,38},{7,103},{8,40},{... | collective-permute-start | bytes 3932168 | tf_op jit(solution)/shard_map/ppermute | solution.py:120
  60.5 30.5 %collective-permute-start.8 = (bf16[512,1280]{1,0:T(8,128)(2,1)S(1)}, bf16[512,1280]{1,0:T(8,128)(2,1)}, u32[]{:S(2)}, u32[]{:S(2)}) collective-permute-start(bf16[512,1280]{1,0:T(8,128)(2,1)S(1)} %collective-permute-done.4.refs_1_.refs_7_), channel_id=1, source_target_pairs={{0,96},{1,33},{2,98},{3,35},{4,100},{5,37},{6,102},{7,39},{8,104},... | collective-permute-start | bytes 3932168 | tf_op jit(solution)/shard_map/ppermute | solution.py:120
  90.5 1.1 copy-start.5
  91.6 20.6 %collective-permute-start.14 = (bf16[2,1536,256]{2,1,0:T(8,128)(2,1)}, bf16[2,1536,256]{2,1,0:T(8,128)(2,1)S(1)}, u32[]{:S(2)}, u32[]{:S(2)}) collective-permute-start(bf16[2,1536,256]{2,1,0:T(8,128)(2,1)} %get-tuple-element.115), channel_id=1, source_target_pairs={{0,2},{1,7},{2,0},{3,5},{4,6},{5,3},{6,4},{7,1},{8,10},{9,15},{10,... | collective-permute-start | bytes 4718600 | tf_op jit(solution)/shard_map/ppermute | solution.py:120
  93.5 17.5 %collective-permute-start.13 = (bf16[512,1280]{1,0:T(8,128)(2,1)}, bf16[512,1280]{1,0:T(8,128)(2,1)S(1)}, u32[]{:S(2)}, u32[]{:S(2)}) collective-permute-start(bf16[512,1280]{1,0:T(8,128)(2,1)} %collective-permute-done.10.refs_5_), channel_id=1, source_target_pairs={{0,1},{1,0},{2,3},{3,2},{4,5},{5,4},{6,7},{7,6},{8,9},{9,8},{10,11... | collective-permute-start | bytes 3932168 | tf_op jit(solution)/shard_map/ppermute | solution.py:120
  96.7 15.5 %copy-start.8 = (bf16[2,1536,256]{2,1,0:T(8,128)(2,1)S(1)}, bf16[2,1536,256]{2,1,0:T(8,128)(2,1)}, u32[]{:S(2)}) copy-start(bf16[2,1536,256]{2,1,0:T(8,128)(2,1)} %get-tuple-element.153) | copy-start | bytes 4718596
  96.7 14.2 %collective-permute-start.15 = (f32[136,128]{1,0:T(8,128)S(1)}, f32[136,128]{1,0:T(8,128)S(1)}, u32[]{:S(2)}, u32[]{:S(2)}) collective-permute-start(f32[136,128]{1,0:T(8,128)S(1)} %concatenate.11), channel_id=1, source_target_pairs={{0,32},{1,33},{2,34},{3,35},{4,36},{5,37},{6,38},{7,39},{8,40},{9,... | collective-permute-start | bytes 208904 | tf_op jit(solution)/shard_map/ppermute | solution.py:120
  111.0 7.7 %copy-start.9 = (bf16[512,1280]{1,0:T(8,128)(2,1)}, bf16[512,1280]{1,0:T(8,128)(2,1)S(1)}, u32[]{:S(2)}) copy-start(bf16[512,1280]{1,0:T(8,128)(2,1)S(1)} %collective-permute-done.13.refs_6_) | copy-start | bytes 3932164
  112.4 19.7 %copy-start.18 = (bf16[2,512,256]{2,1,0:T(8,128)(2,1)S(1)}, bf16[2,512,256]{2,1,0:T(8,128)(2,1)}, u32[]{:S(2)}) copy-start(bf16[2,512,256]{2,1,0:T(8,128)(2,1)} %get-tuple-element.157) | copy-start | bytes 1572868
  112.4 19.4 %collective-permute-start.16 = (bf16[1536,256]{1,0:T(8,128)(2,1)S(1)}, bf16[1536,256]{1,0:T(8,128)(2,1)}, u32[]{:S(2)}, u32[]{:S(2)}) collective-permute-start(bf16[1536,256]{1,0:T(8,128)(2,1)S(1)} %fusion.6), channel_id=1, source_target_pairs={{0,6},{1,3},{2,4},{3,1},{4,2},{5,7},{6,0},{7,5},{8,14},{9,11},{10,... | collective-permute-start | bytes 2359304 | tf_op jit(solution)/shard_map/ppermute | solution.py:120
  116.6 13.7 %collective-permute-start.17 = (bf16[2,512,256]{2,1,0:T(8,128)(2,1)}, bf16[2,512,256]{2,1,0:T(8,128)(2,1)}, u32[]{:S(2)}, u32[]{:S(2)}) collective-permute-start(bf16[2,512,256]{2,1,0:T(8,128)(2,1)} %get-tuple-element.135), channel_id=1, source_target_pairs={{0,2},{1,7},{2,0},{3,5},{4,6},{5,3},{6,4},{7,1},{8,10},{9,15},{10,... | collective-permute-start | bytes 1572872 | tf_op jit(solution)/shard_map/ppermute | solution.py:120
  116.6 13.1 %collective-permute-start.18 = (f32[136,128]{1,0:T(8,128)S(1)}, f32[136,128]{1,0:T(8,128)S(1)}, u32[]{:S(2)}, u32[]{:S(2)}) collective-permute-start(f32[136,128]{1,0:T(8,128)S(1)} %pad_add_fusion.1), channel_id=1, source_target_pairs={{0,96},{1,97},{2,98},{3,99},{4,100},{5,101},{6,102},{7,103},{8,104... | collective-permute-start | bytes 208904 | tf_op jit(solution)/shard_map/ppermute | solution.py:120
  131.8 17.8 %collective-permute-start.20 = (bf16[2,1024,256]{2,1,0:T(8,128)(2,1)}, bf16[2,1024,256]{2,1,0:T(8,128)(2,1)S(1)}, u32[]{:S(2)}, u32[]{:S(2)}) collective-permute-start(bf16[2,1024,256]{2,1,0:T(8,128)(2,1)} %get-tuple-element.146), channel_id=1, source_target_pairs={{0,2},{1,7},{2,0},{3,5},{4,6},{5,3},{6,4},{7,1},{8,10},{9,15},{10,... | collective-permute-start | bytes 3145736 | tf_op jit(solution)/shard_map/ppermute | solution.py:120
  133.2 12.6 %collective-permute-start.19 = (bf16[512,256]{1,0:T(8,128)(2,1)S(1)}, bf16[512,256]{1,0:T(8,128)(2,1)S(1)}, u32[]{:S(2)}, u32[]{:S(2)}) collective-permute-start(bf16[512,256]{1,0:T(8,128)(2,1)S(1)} %fusion.11), channel_id=1, source_target_pairs={{0,6},{1,3},{2,4},{3,1},{4,2},{5,7},{6,0},{7,5},{8,14},{9,11},{10,... | collective-permute-start | bytes 786440 | tf_op jit(solution)/shard_map/ppermute | solution.py:120
  135.9 4.3 %collective-permute-start.21 = (f32[136,128]{1,0:T(8,128)S(1)}, f32[136,128]{1,0:T(8,128)S(1)}, u32[]{:S(2)}, u32[]{:S(2)}) collective-permute-start(f32[136,128]{1,0:T(8,128)S(1)} %add.87), channel_id=1, source_target_pairs={{0,8},{1,9},{2,10},{3,11},{4,12},{5,13},{6,14},{7,15},{8,0},{9,1},... | collective-permute-start | bytes 208904 | tf_op jit(solution)/shard_map/ppermute | solution.py:120
  140.2 5.6 %collective-permute-start.22 = (f32[136,128]{1,0:T(8,128)S(1)}, f32[136,128]{1,0:T(8,128)S(1)}, u32[]{:S(2)}, u32[]{:S(2)}) collective-permute-start(f32[136,128]{1,0:T(8,128)S(1)} %add.89), channel_id=1, source_target_pairs={{0,24},{1,25},{2,26},{3,27},{4,28},{5,29},{6,30},{7,31},{8,16},{9,... | collective-permute-start | bytes 208904 | tf_op jit(solution)/shard_map/ppermute | solution.py:120
  150.1 19.6 %collective-permute-start.27 = (bf16[2,1024,256]{2,1,0:T(8,128)(2,1)}, bf16[2,1024,256]{2,1,0:T(8,128)(2,1)S(1)}, u32[]{:S(2)}, u32[]{:S(2)}) collective-permute-start(bf16[2,1024,256]{2,1,0:T(8,128)(2,1)} %get-tuple-element.163), channel_id=1, source_target_pairs={{0,2},{1,7},{2,0},{3,5},{4,6},{5,3},{6,4},{7,1},{8,10},{9,15},{10,... | collective-permute-start | bytes 3145736 | tf_op jit(solution)/shard_map/ppermute | solution.py:120
  153.7 3.9 %copy-start.11 = (bf16[2,1024,256]{2,1,0:T(8,128)(2,1)S(1)}, bf16[2,1024,256]{2,1,0:T(8,128)(2,1)}, u32[]{:S(2)}) copy-start(bf16[2,1024,256]{2,1,0:T(8,128)(2,1)} %get-tuple-element.170) | copy-start | bytes 3145732
  153.8 15.9 %copy-start.10 = (bf16[2,1024,256]{2,1,0:T(8,128)(2,1)S(1)}, bf16[2,1024,256]{2,1,0:T(8,128)(2,1)}, u32[]{:S(2)}) copy-start(bf16[2,1024,256]{2,1,0:T(8,128)(2,1)} %get-tuple-element.165) | copy-start | bytes 3145732
  153.8 15.9 %collective-permute-start.24 = (bf16[2,512,256]{2,1,0:T(8,128)(2,1)S(1)}, bf16[2,512,256]{2,1,0:T(8,128)(2,1)S(1)}, u32[]{:S(2)}, u32[]{:S(2)}) collective-permute-start(bf16[2,512,256]{2,1,0:T(8,128)(2,1)S(1)} %pad_maximum_fusion.1), channel_id=1, source_target_pairs={{0,24},{2,26},{4,28},{6,30},{8,16},{10,18},{12,20},{14,22},{17,9},... | collective-permute-start | bytes 1572872 | tf_op jit(solution)/shard_map/ppermute | solution.py:120
  157.0 12.7 %collective-permute-start.25 = (bf16[2,512,256]{2,1,0:T(8,128)(2,1)S(1)}, bf16[2,512,256]{2,1,0:T(8,128)(2,1)S(1)}, u32[]{:S(2)}, u32[]{:S(2)}) collective-permute-start(bf16[2,512,256]{2,1,0:T(8,128)(2,1)S(1)} %pad_maximum_fusion.1), channel_id=1, source_target_pairs={{1,24},{3,26},{5,28},{7,30},{9,16},{11,18},{13,20},{15,22},{16,9},... | collective-permute-start | bytes 1572872 | tf_op jit(solution)/shard_map/ppermute | solution.py:120
  157.8 11.9 %collective-permute-start.26 = (bf16[1024,256]{1,0:T(8,128)(2,1)S(1)}, bf16[1024,256]{1,0:T(8,128)(2,1)S(1)}, u32[]{:S(2)}, u32[]{:S(2)}) collective-permute-start(bf16[1024,256]{1,0:T(8,128)(2,1)S(1)} %fusion.7), channel_id=1, source_target_pairs={{0,6},{1,3},{2,4},{3,1},{4,2},{5,7},{6,0},{7,5},{8,14},{9,11},{10,... | collective-permute-start | bytes 1572872 | tf_op jit(solution)/shard_map/ppermute | solution.py:120
  159.4 13.8 %copy-start.7 = (bf16[1024,256]{1,0:T(8,128)(2,1)}, bf16[1024,256]{1,0:T(8,128)(2,1)S(1)}, u32[]{:S(2)}) copy-start(bf16[1024,256]{1,0:T(8,128)(2,1)S(1)} %slice.84) | copy-start | bytes 1572868
  159.4 10.3 %collective-permute-start.23 = (bf16[2,512,256]{2,1,0:T(8,128)(2,1)S(1)}, bf16[2,512,256]{2,1,0:T(8,128)(2,1)S(1)}, u32[]{:S(2)}, u32[]{:S(2)}) collective-permute-start(bf16[2,512,256]{2,1,0:T(8,128)(2,1)S(1)} %bitcast.53), channel_id=1, source_target_pairs={{0,1},{1,0},{2,3},{3,2},{4,5},{5,4},{6,7},{7,6},{8,9},{9,8},{10,11... | collective-permute-start | bytes 1572872 | tf_op jit(solution)/shard_map/ppermute | solution.py:120
  169.7 3.5 %copy-start.12 = (bf16[2,512,256]{2,1,0:T(8,128)(2,1)}, bf16[2,512,256]{2,1,0:T(8,128)(2,1)S(1)}, u32[]{:S(2)}) copy-start(bf16[2,512,256]{2,1,0:T(8,128)(2,1)S(1)} %collective-permute-done.24.same0) | copy-start | bytes 1572868
  169.7 3.5 %copy-start.13 = (bf16[2,512,256]{2,1,0:T(8,128)(2,1)}, bf16[2,512,256]{2,1,0:T(8,128)(2,1)S(1)}, u32[]{:S(2)}) copy-start(bf16[2,512,256]{2,1,0:T(8,128)(2,1)S(1)} %collective-permute-done.25.other0) | copy-start | bytes 1572868
  169.7 3.5 %copy-start.14 = (bf16[2,512,256]{2,1,0:T(8,128)(2,1)}, bf16[2,512,256]{2,1,0:T(8,128)(2,1)S(1)}, u32[]{:S(2)}) copy-start(bf16[2,512,256]{2,1,0:T(8,128)(2,1)S(1)} %collective-permute-done.23.near_in) | copy-start | bytes 1572868
  169.9 10.5 %collective-permute-start.28 = (bf16[1024,256]{1,0:T(8,128)(2,1)S(1)}, bf16[1024,256]{1,0:T(8,128)(2,1)S(1)}, u32[]{:S(2)}, u32[]{:S(2)}) collective-permute-start(bf16[1024,256]{1,0:T(8,128)(2,1)S(1)} %fusion.8), channel_id=1, source_target_pairs={{0,6},{1,3},{2,4},{3,1},{4,2},{5,7},{6,0},{7,5},{8,14},{9,11},{10,... | collective-permute-start | bytes 1572872 | tf_op jit(solution)/shard_map/ppermute | solution.py:120
  173.2 8.2 %copy-start.19 = (f32[2,64,128]{2,1,0:T(8,128)S(1)}, f32[2,64,128]{2,1,0:T(8,128)}, u32[]{:S(2)}) copy-start(f32[2,64,128]{2,1,0:T(8,128)} %pre_ref.3) | copy-start | bytes 196612
  173.2 15.3 %collective-permute-start.30 = (bf16[2,512,256]{2,1,0:T(8,128)(2,1)S(1)}, bf16[2,512,256]{2,1,0:T(8,128)(2,1)S(1)}, u32[]{:S(2)}, u32[]{:S(2)}) collective-permute-start(bf16[2,512,256]{2,1,0:T(8,128)(2,1)S(1)} %bitcast.57), channel_id=1, source_target_pairs={{0,24},{2,26},{4,28},{6,30},{8,16},{10,18},{12,20},{14,22},{17,9},... | collective-permute-start | bytes 1572872 | tf_op jit(solution)/shard_map/ppermute | solution.py:120
  177.0 11.6 %collective-permute-start.31 = (bf16[2,512,256]{2,1,0:T(8,128)(2,1)S(1)}, bf16[2,512,256]{2,1,0:T(8,128)(2,1)S(1)}, u32[]{:S(2)}, u32[]{:S(2)}) collective-permute-start(bf16[2,512,256]{2,1,0:T(8,128)(2,1)S(1)} %bitcast.58), channel_id=1, source_target_pairs={{1,24},{3,26},{5,28},{7,30},{9,16},{11,18},{13,20},{15,22},{16,9},... | collective-permute-start | bytes 1572872 | tf_op jit(solution)/shard_map/ppermute | solution.py:120
  180.6 8.0 %copy-start.6 = (bf16[1024,256]{1,0:T(8,128)(2,1)}, bf16[1024,256]{1,0:T(8,128)(2,1)S(1)}, u32[]{:S(2)}) copy-start(bf16[1024,256]{1,0:T(8,128)(2,1)S(1)} %fusion.5) | copy-start | bytes 1572868
  180.6 7.9 %collective-permute-start.29 = (bf16[2,512,256]{2,1,0:T(8,128)(2,1)S(1)}, bf16[2,512,256]{2,1,0:T(8,128)(2,1)S(1)}, u32[]{:S(2)}, u32[]{:S(2)}) collective-permute-start(bf16[2,512,256]{2,1,0:T(8,128)(2,1)S(1)} %bitcast.51), channel_id=1, source_target_pairs={{0,1},{1,0},{2,3},{3,2},{4,5},{5,4},{6,7},{7,6},{8,9},{9,8},{10,11... | collective-permute-start | bytes 1572872 | tf_op jit(solution)/shard_map/ppermute | solution.py:120
  188.5 0.8 copy-start.15
  188.5 1.0 copy-start.16
  189.5 0.8 copy-start.17

commit v5 on v4

--- a/solution.py
+++ b/solution.py
@@ -336,20 +336,21 @@
     self0, terms0 = attention(0, lengths, queries, out_grad, key_rows, value_rows, prefix, tables)
     side_a, side_b, taken, self0, terms0, key_rows, kept = gate((side_a, side_b, taken, self0, terms0, key_rows, kept))
     mine = jnp.concatenate([kept, taken], 0)
-    turned = send(jnp.concatenate([kept, taken, side_a, side_b], 0), x_turn)
+    turned = send(mine, x_turn)
+    turned_far = send(jnp.concatenate([side_a, side_b], 0), x_turn)
     mate = send(mine, y_mate)
     pair0 = send(self0, y_partner)
     self0_other = send(self0, sibling)
     self1, terms1 = attention(1, lengths, queries, out_grad, key_rows, value_rows, prefix, tables)
     count_row = jnp.full((8, HD), jnp.sum(lengths).astype(jnp.float32))
-    turned, mate, pair0, self0_other, self1, terms1, terms0, mine, self0 = gate(
-        (turned, mate, pair0, self0_other, self1, terms1, terms0, mine, self0)
+    turned, turned_far, mate, pair0, self0_other, self1, terms1, terms0, mine, self0 = gate(
+        (turned, turned_far, mate, pair0, self0_other, self1, terms1, terms0, mine, self0)
     )
     near_blocks = [
         ((mine, 0), (mine, rows)),
         ((side_a, 0), (side_b, 0)),
         ((turned, 0), (turned, rows)),
-        ((turned, 2 * rows), (turned, 3 * rows)),
+        ((turned_far, 0), (turned_far, rows)),
     ]
 
     def start_unit(partial):
@@ -369,7 +370,7 @@
     pair0_other = send(pair0, sibling)
     mate_side = send(mate, x_side)
     mate_turn = send(mate, x_turn)
-    mate_far = send(turned[2 * rows :], y_mate)
+    mate_far = send(turned_far, y_mate)
     pair1 = send(self1, y_partner)
     both0, both1, there0 = (self0, self0_other), (self1, self1_other), (pair0, pair0_other)
     early = project(places, [(near_blocks, [both0, both1, there0], [(0, 0), (0, SEQ), (0, 2 * SEQ)])])[0]

time: 197 us -> 196 us (level)
  starting transfers between devices: 43.9 us -> 47.1 us
    ppermute x32 -> x33, starting transfers between devices: 43.9 us -> 47.1 us  [send(): return lax.ppermute(array, AXES, pairs_of(move))]
    ppermute x32 -> x33, waiting for transfers between devices: 72.2 us -> 70.7 us  [send(): return lax.ppermute(array, AXES, pairs_of(move))]
  transfers between devices with their start and end apart: 32 -> 33, of which waited for: 15 -> 16; matrix products, arithmetic and copies ran while one was open for 4% -> 2% of each run, Pallas kernels for 29% -> 30%
where the time goes in v5:
time: 196 us; the launch traced here: 193 us
  waiting for transfers between devices  70.7 us (36%)
  Pallas kernels  60.6 us (31%)
  starting transfers between devices  47.1 us (24%)
  other arithmetic  7.85 us (4%)
  local copies, waits for them, and re-layouts  3.93 us (2%)
  between operations  2.71 us (1%)
    ppermute x33, waiting for transfers between devices, send(): return lax.ppermute(array, AXES, pairs_of(move))  70.7 us
    ppermute x33, starting transfers between devices, send(): return lax.ppermute(array, AXES, pairs_of(move))  47.1 us
    pallas_call x3, Pallas kernels, project(): pl.pallas_call(functools.partial(project_kernel, (sides, plan, len(out_ro...  37.5 us
    pallas_call x2, Pallas kernels, attention(): pl.pallas_call(functools.partial(attn_kernel, prompt=prompt), grid=(GROUP...  19.5 us
  transfers between devices with their start and end apart: 33, of which 16 were waited for; matrix products, arithmetic and copies ran while one was open for 2% of the time, Pallas kernels for 30%

profile of v5, /device:TPU:2, one launch (start us, length us, event | category | flops | bytes accessed | tf_op | source)
XLA Modules:
  0.0 192.9 jit_solution(14828575302453708232)
XLA Ops:
  0.7 1.4 constant_dynamic-slice_fusion
  2.0 0.6 compare_select_fusion.2.refs_0_
  2.7 0.5 collective-permute-start
  3.1 0.7 collective-permute-start.1
  3.8 1.0 collective-permute-start.2
  4.8 9.7 %attention_backward.2 = (bf16[512,1280]{1,0:T(8,128)(2,1)}, f32[2,64,128]{2,1,0:T(8,128)}) custom-call(s32[2]{0:T(128)} %len_ref.3, bf16[1024,1024]{1,0:T(8,128)(2,1)} %q_ref.3, bf16[1024,1024]{1,0:T(8,128)(2,1)} %g_ref.3, bf16[1024,128]{1,0:T(8,128)(2,1)} %k_ref.2, bf16[1024,128]{1,0:T(8,128)(2,1)} %v_ref.3, f32[2,64,128]{2,1,0:T(8,128)} %pre_ref.3, ...), custom_call_target="tpu_custom_call" | custom-call | flops 3019898880 | bytes 4194304 | tf_op jit(solution)/shard_map/attention_backward/pallas_call | solution.py:82
  14.5 5.6 %collective-permute-done.refs_2_ = bf16[256,1280]{1,0:T(8,128)(2,1)S(1)} collective-permute-done((bf16[256,1280]{1,0:T(8,128)(2,1)S(1)}, bf16[256,1280]{1,0:T(8,128)(2,1)S(1)}, u32[]{:S(2)}, u32[]{:S(2)}) %collective-permute-start) | collective-permute-done | bytes 655392 | tf_op jit(solution)/shard_map/ppermute | solution.py:120
  20.3 1.3 pad_maximum_fusion
  21.6 1.4 collective-permute-start.4
  23.1 0.7 collective-permute-start.3
  23.8 1.6 collective-permute-start.5
  25.4 2.2 %collective-permute-start.6 = (bf16[512,1280]{1,0:T(8,128)(2,1)}, bf16[512,1280]{1,0:T(8,128)(2,1)}, u32[]{:S(2)}, u32[]{:S(2)}) collective-permute-start(bf16[512,1280]{1,0:T(8,128)(2,1)} %get-tuple-element.124.refs_6_.refs_7_), channel_id=1, source_target_pairs={{0,24},{1,25},{2,26},{3,27},{4,28},{5,29},{6,30},{7,31},{8,16},{9,... | collective-permute-start | bytes 3932168 | tf_op jit(solution)/shard_map/ppermute | solution.py:120
  27.6 9.8 %attention_backward.3 = (bf16[512,1280]{1,0:T(8,128)(2,1)}, f32[2,64,128]{2,1,0:T(8,128)}) custom-call(s32[2]{0:T(128)} %len_ref.3, bf16[1024,1024]{1,0:T(8,128)(2,1)} %q_ref.3, bf16[1024,1024]{1,0:T(8,128)(2,1)} %g_ref.3, bf16[1024,128]{1,0:T(8,128)(2,1)} %k_ref.2, bf16[1024,128]{1,0:T(8,128)(2,1)} %v_ref.3, f32[2,64,128]{2,1,0:T(8,128)} %pre_ref.3, ...), custom_call_target="tpu_custom_call" | custom-call | flops 3019898880 | bytes 4194304 | tf_op jit(solution)/shard_map/attention_backward/pallas_call | solution.py:82
  37.4 2.0 %collective-permute-done.4.refs_5_ = bf16[512,1280]{1,0:T(8,128)(2,1)S(1)} collective-permute-done((bf16[512,1280]{1,0:T(8,128)(2,1)}, bf16[512,1280]{1,0:T(8,128)(2,1)S(1)}, u32[]{:S(2)}, u32[]{:S(2)}) %collective-permute-start.4) | collective-permute-done | bytes 1310752 | tf_op jit(solution)/shard_map/ppermute | solution.py:120
  39.4 14.0 %collective-permute-done.3.refs_4_ = bf16[512,1280]{1,0:T(8,128)(2,1)S(1)} collective-permute-done((bf16[512,1280]{1,0:T(8,128)(2,1)S(1)}, bf16[512,1280]{1,0:T(8,128)(2,1)S(1)}, u32[]{:S(2)}, u32[]{:S(2)}) %collective-permute-start.3) | collective-permute-done | bytes 1310752 | tf_op jit(solution)/shard_map/ppermute | solution.py:120
  53.5 2.2 %collective-permute-done.6.refs_10_.refs_5_ = bf16[512,1280]{1,0:T(8,128)(2,1)} collective-permute-done((bf16[512,1280]{1,0:T(8,128)(2,1)}, bf16[512,1280]{1,0:T(8,128)(2,1)}, u32[]{:S(2)}, u32[]{:S(2)}) %collective-permute-start.6) | collective-permute-done | bytes 1310752 | tf_op jit(solution)/shard_map/ppermute | solution.py:120
  55.8 0.5 collective-permute-start.13
  56.3 2.2 %collective-permute-start.11 = (bf16[512,1280]{1,0:T(8,128)(2,1)}, bf16[512,1280]{1,0:T(8,128)(2,1)}, u32[]{:S(2)}, u32[]{:S(2)}) collective-permute-start(bf16[512,1280]{1,0:T(8,128)(2,1)} %get-tuple-element.126.refs_8_.refs_9_), channel_id=1, source_target_pairs={{0,24},{1,25},{2,26},{3,27},{4,28},{5,29},{6,30},{7,31},{8,16},{9,... | collective-permute-start | bytes 3932168 | tf_op jit(solution)/shard_map/ppermute | solution.py:120
  58.5 1.5 collective-permute-start.8
  59.9 2.2 %collective-permute-start.9 = (bf16[512,1280]{1,0:T(8,128)(2,1)S(1)}, bf16[512,1280]{1,0:T(8,128)(2,1)}, u32[]{:S(2)}, u32[]{:S(2)}) collective-permute-start(bf16[512,1280]{1,0:T(8,128)(2,1)S(1)} %collective-permute-done.5.refs_1_.refs_8_), channel_id=1, source_target_pairs={{0,96},{1,33},{2,98},{3,35},{4,100},{5,37},{6,102},{7,39},{8,104},... | collective-permute-start | bytes 3932168 | tf_op jit(solution)/shard_map/ppermute | solution.py:120
  62.1 13.3 %project.3 = (bf16[2,1536,256]{2,1,0:T(8,128)(2,1)}, bf16[2,1536,256]{2,1,0:T(8,128)(2,1)}) custom-call(s32[4]{0:T(128)} %compare_select_fusion.2.refs_0_, bf16[512,1280]{1,0:T(8,128)(2,1)} %copy-done, bf16[256,1280]{1,0:T(8,128)(2,1)} %copy-done.1, bf16[256,1280]{1,0:T(8,128)(2,1)} %copy-done.2, bf16[512,1280]{1,0:T(8,128)(2,1)} %copy-done.4, ...), custom_call_target="tpu_custom_call" | custom-call | tf_op jit(solution)/shard_map/project/pallas_call | solution.py:251
  75.4 13.6 %collective-permute-done.10.refs_4_.refs_11_ = bf16[512,1280]{1,0:T(8,128)(2,1)S(1)} collective-permute-done((bf16[512,1280]{1,0:T(8,128)(2,1)S(1)}, bf16[512,1280]{1,0:T(8,128)(2,1)S(1)}, u32[]{:S(2)}, u32[]{:S(2)}) %collective-permute-start.10) | collective-permute-done | bytes 1310752 | tf_op jit(solution)/shard_map/ppermute | solution.py:120
  89.0 0.2 collective-permute-done.8.refs_2_.refs_9_
  89.3 1.9 collective-permute-start.15
  91.2 2.6 %collective-permute-start.14 = (bf16[512,1280]{1,0:T(8,128)(2,1)}, bf16[512,1280]{1,0:T(8,128)(2,1)}, u32[]{:S(2)}, u32[]{:S(2)}) collective-permute-start(bf16[512,1280]{1,0:T(8,128)(2,1)} %collective-permute-done.11.refs_6_), channel_id=1, source_target_pairs={{0,1},{1,0},{2,3},{3,2},{4,5},{5,4},{6,7},{7,6},{8,9},{9,8},{10,11... | collective-permute-start | bytes 3932168 | tf_op jit(solution)/shard_map/ppermute | solution.py:120
  93.8 0.7 reduce_sum.9
  95.3 1.8 collective-permute-start.16
  97.1 13.3 %project.4 = (bf16[2,512,256]{2,1,0:T(8,128)(2,1)}, bf16[2,512,256]{2,1,0:T(8,128)(2,1)}, bf16[2,1024,256]{2,1,0:T(8,128)(2,1)}, bf16[2,1024,256]{2,1,0:T(8,128)(2,1)}) custom-call(s32[4]{0:T(128)} %compare_select_fusion.2.refs_0_, bf16[512,1280]{1,0:T(8,128)(2,1)} %copy-done.5, bf16[512,1280]{1,0:T(8,128)(2,1)} %collective-permute-done.8.refs_2_.refs_9_, ...), custom_call_target="tpu_custom_call" | custom-call | tf_op jit(solution)/shard_map/project/pallas_call | solution.py:251
  110.4 1.4 fusion.6
  111.8 3.6 %collective-permute-start.17 = (bf16[1536,256]{1,0:T(8,128)(2,1)S(1)}, bf16[1536,256]{1,0:T(8,128)(2,1)S(1)}, u32[]{:S(2)}, u32[]{:S(2)}) collective-permute-start(bf16[1536,256]{1,0:T(8,128)(2,1)S(1)} %fusion.6), channel_id=1, source_target_pairs={{0,6},{1,3},{2,4},{3,1},{4,2},{5,7},{6,0},{7,5},{8,14},{9,11},{10,... | collective-permute-start | bytes 2359304 | tf_op jit(solution)/shard_map/ppermute | solution.py:120
  115.5 2.8 %collective-permute-start.19 = (f32[136,128]{1,0:T(8,128)S(1)}, f32[136,128]{1,0:T(8,128)S(1)}, u32[]{:S(2)}, u32[]{:S(2)}) collective-permute-start(f32[136,128]{1,0:T(8,128)S(1)} %pad_add_fusion.1), channel_id=1, source_target_pairs={{0,96},{1,97},{2,98},{3,99},{4,100},{5,101},{6,102},{7,103},{8,104... | collective-permute-start | bytes 208904 | tf_op jit(solution)/shard_map/ppermute | solution.py:120
  118.2 11.0 %project.5 = (bf16[2,1024,256]{2,1,0:T(8,128)(2,1)}, bf16[2,1024,256]{2,1,0:T(8,128)(2,1)}) custom-call(s32[4]{0:T(128)} %compare_select_fusion.2.refs_0_, bf16[512,1280]{1,0:T(8,128)(2,1)} %copy-done, bf16[256,1280]{1,0:T(8,128)(2,1)} %copy-done.1, bf16[256,1280]{1,0:T(8,128)(2,1)} %copy-done.2, bf16[512,1280]{1,0:T(8,128)(2,1)} %copy-done.4, ...), custom_call_target="tpu_custom_call" | custom-call | tf_op jit(solution)/shard_map/project/pallas_call | solution.py:251
  129.2 0.7 collective-permute-done.18
  130.0 1.1 collective-permute-done.17
  131.1 0.3 collective-permute-start.21
  131.4 3.0 %collective-permute-start.20 = (bf16[512,256]{1,0:T(8,128)(2,1)S(1)}, bf16[512,256]{1,0:T(8,128)(2,1)S(1)}, u32[]{:S(2)}, u32[]{:S(2)}) collective-permute-start(bf16[512,256]{1,0:T(8,128)(2,1)S(1)} %fusion.11), channel_id=1, source_target_pairs={{0,6},{1,3},{2,4},{3,1},{4,2},{5,7},{6,0},{7,5},{8,14},{9,11},{10,... | collective-permute-start | bytes 786440 | tf_op jit(solution)/shard_map/ppermute | solution.py:120
  134.4 2.0 %collective-permute-start.22 = (f32[136,128]{1,0:T(8,128)S(1)}, f32[136,128]{1,0:T(8,128)S(1)}, u32[]{:S(2)}, u32[]{:S(2)}) collective-permute-start(f32[136,128]{1,0:T(8,128)S(1)} %add.87), channel_id=1, source_target_pairs={{0,8},{1,9},{2,10},{3,11},{4,12},{5,13},{6,14},{7,15},{8,0},{9,1},... | collective-permute-start | bytes 208904 | tf_op jit(solution)/shard_map/ppermute | solution.py:120
  136.4 2.3 %collective-permute-done.22 = f32[136,128]{1,0:T(8,128)S(1)} collective-permute-done((f32[136,128]{1,0:T(8,128)S(1)}, f32[136,128]{1,0:T(8,128)S(1)}, u32[]{:S(2)}, u32[]{:S(2)}) %collective-permute-start.22) | collective-permute-done | bytes 69664 | tf_op jit(solution)/shard_map/ppermute | solution.py:120
  138.7 1.1 collective-permute-start.23
  139.9 4.5 %collective-permute-done.23 = f32[136,128]{1,0:T(8,128)S(1)} collective-permute-done((f32[136,128]{1,0:T(8,128)S(1)}, f32[136,128]{1,0:T(8,128)S(1)}, u32[]{:S(2)}, u32[]{:S(2)}) %collective-permute-start.23) | collective-permute-done | bytes 69664 | tf_op jit(solution)/shard_map/ppermute | solution.py:120
  144.3 4.5 %collective-permute-done.21 = bf16[2,1024,256]{2,1,0:T(8,128)(2,1)S(1)} collective-permute-done((bf16[2,1024,256]{2,1,0:T(8,128)(2,1)}, bf16[2,1024,256]{2,1,0:T(8,128)(2,1)S(1)}, u32[]{:S(2)}, u32[]{:S(2)}) %collective-permute-start.21) | collective-permute-done | bytes 1048608 | tf_op jit(solution)/shard_map/ppermute | solution.py:120
  148.9 0.5 slice.66
  149.4 0.3 collective-permute-start.28
  150.5 1.5 fusion.1
  152.1 3.2 %collective-permute-start.25 = (bf16[2,512,256]{2,1,0:T(8,128)(2,1)S(1)}, bf16[2,512,256]{2,1,0:T(8,128)(2,1)S(1)}, u32[]{:S(2)}, u32[]{:S(2)}) collective-permute-start(bf16[2,512,256]{2,1,0:T(8,128)(2,1)S(1)} %pad_maximum_fusion.1), channel_id=1, source_target_pairs={{0,24},{2,26},{4,28},{6,30},{8,16},{10,18},{12,20},{14,22},{17,9},... | collective-permute-start | bytes 1572872 | tf_op jit(solution)/shard_map/ppermute | solution.py:120
  155.3 0.7 collective-permute-start.26
  156.0 0.1 fusion.7
  156.1 1.0 collective-permute-start.27
  157.2 1.5 collective-permute-start.24
  158.7 10.5 %collective-permute-done.27 = bf16[1024,256]{1,0:T(8,128)(2,1)S(1)} collective-permute-done((bf16[1024,256]{1,0:T(8,128)(2,1)S(1)}, bf16[1024,256]{1,0:T(8,128)(2,1)S(1)}, u32[]{:S(2)}, u32[]{:S(2)}) %collective-permute-start.27) | collective-permute-done | bytes 524320 | tf_op jit(solution)/shard_map/ppermute | solution.py:120
  169.2 0.1 fusion.8
  169.4 3.0 %collective-permute-start.29 = (bf16[1024,256]{1,0:T(8,128)(2,1)S(1)}, bf16[1024,256]{1,0:T(8,128)(2,1)S(1)}, u32[]{:S(2)}, u32[]{:S(2)}) collective-permute-start(bf16[1024,256]{1,0:T(8,128)(2,1)S(1)} %fusion.8), channel_id=1, source_target_pairs={{0,6},{1,3},{2,4},{3,1},{4,2},{5,7},{6,0},{7,5},{8,14},{9,11},{10,... | collective-permute-start | bytes 1572872 | tf_op jit(solution)/shard_map/ppermute | solution.py:120
  172.4 0.2 fusion.3
  172.7 3.1 %collective-permute-start.31 = (bf16[2,512,256]{2,1,0:T(8,128)(2,1)S(1)}, bf16[2,512,256]{2,1,0:T(8,128)(2,1)S(1)}, u32[]{:S(2)}, u32[]{:S(2)}) collective-permute-start(bf16[2,512,256]{2,1,0:T(8,128)(2,1)S(1)} %bitcast.57), channel_id=1, source_target_pairs={{0,24},{2,26},{4,28},{6,30},{8,16},{10,18},{12,20},{14,22},{17,9},... | collective-permute-start | bytes 1572872 | tf_op jit(solution)/shard_map/ppermute | solution.py:120
  175.8 0.7 collective-permute-start.32
  176.5 3.3 %collective-permute-done.29 = bf16[1024,256]{1,0:T(8,128)(2,1)S(1)} collective-permute-done((bf16[1024,256]{1,0:T(8,128)(2,1)S(1)}, bf16[1024,256]{1,0:T(8,128)(2,1)S(1)}, u32[]{:S(2)}, u32[]{:S(2)}) %collective-permute-start.29) | collective-permute-done | bytes 524320 | tf_op jit(solution)/shard_map/ppermute | solution.py:120
  179.8 0.2 fusion.5
  180.2 0.6 pad_add_fusion.info
  180.9 0.6 sub.26
  181.5 5.9 %collective-permute-done.31.same1 = bf16[2,512,256]{2,1,0:T(8,128)(2,1)S(1)} collective-permute-done((bf16[2,512,256]{2,1,0:T(8,128)(2,1)S(1)}, bf16[2,512,256]{2,1,0:T(8,128)(2,1)S(1)}, u32[]{:S(2)}, u32[]{:S(2)}) %collective-permute-start.31) | collective-permute-done | bytes 524320 | tf_op jit(solution)/shard_map/ppermute | solution.py:120
  187.4 0.8 copy-done.15
  188.2 0.2 copy-done.16
  188.4 0.8 copy-done.17
  189.2 3.6 %arrange.1 = bf16[1024,1024]{1,0:T(8,128)(2,1)} custom-call(s32[3]{0:T(128)} %pad_add_fusion.info, bf16[2,512,256]{2,1,0:T(8,128)(2,1)} %bitcast.54, bf16[2,512,256]{2,1,0:T(8,128)(2,1)} %bitcast.52, bf16[2,512,256]{2,1,0:T(8,128)(2,1)} %copy-done.14, bf16[2,512,256]{2,1,0:T(8,128)(2,1)} %copy-done.17, bf16[2,512,256]{2,1,0:T(8,128)(2,1)} %copy-done.12, ...), custom_call_target="tpu_custom_call" | custom-call | tf_op jit(solution)/shard_map/arrange/pallas_call | solution.py:301
  (85 shorter events, 1.0 us)
Async XLA Ops:
  2.7 17.5 %collective-permute-start = (bf16[256,1280]{1,0:T(8,128)(2,1)S(1)}, bf16[256,1280]{1,0:T(8,128)(2,1)S(1)}, u32[]{:S(2)}, u32[]{:S(2)}) collective-permute-start(bf16[256,1280]{1,0:T(8,128)(2,1)S(1)} %get-tuple-element.93), channel_id=1, source_target_pairs={{0,32},{1,97},{2,34},{3,99},{4,36},{5,101},{6,38},{7,103},{8,40},{... | collective-permute-start | bytes 1966088 | tf_op jit(solution)/shard_map/ppermute | solution.py:120
  3.1 17.2 %collective-permute-start.1 = (bf16[256,1280]{1,0:T(8,128)(2,1)S(1)}, bf16[256,1280]{1,0:T(8,128)(2,1)S(1)}, u32[]{:S(2)}, u32[]{:S(2)}) collective-permute-start(bf16[256,1280]{1,0:T(8,128)(2,1)S(1)} %get-tuple-element.90), channel_id=1, source_target_pairs={{0,97},{1,32},{2,99},{3,34},{4,101},{5,36},{6,103},{7,38},{8,105},... | collective-permute-start | bytes 1966088 | tf_op jit(solution)/shard_map/ppermute | solution.py:120
  3.8 16.4 %collective-permute-start.2 = (bf16[256,1280]{1,0:T(8,128)(2,1)S(1)}, bf16[256,1280]{1,0:T(8,128)(2,1)S(1)}, u32[]{:S(2)}, u32[]{:S(2)}) collective-permute-start(bf16[256,1280]{1,0:T(8,128)(2,1)S(1)} %get-tuple-element.90), channel_id=1, source_target_pairs={{0,1},{1,0},{2,3},{3,2},{4,5},{5,4},{6,7},{7,6},{8,9},{9,8},{10,11... | collective-permute-start | bytes 1966088 | tf_op jit(solution)/shard_map/ppermute | solution.py:120
  20.1 1.5 copy-start.1
  20.3 1.4 copy-start.2
  21.6 17.8 %collective-permute-start.4 = (bf16[512,1280]{1,0:T(8,128)(2,1)}, bf16[512,1280]{1,0:T(8,128)(2,1)S(1)}, u32[]{:S(2)}, u32[]{:S(2)}) collective-permute-start(bf16[512,1280]{1,0:T(8,128)(2,1)} %pad_maximum_fusion), channel_id=1, source_target_pairs={{0,96},{1,33},{2,98},{3,35},{4,100},{5,37},{6,102},{7,39},{8,104},... | collective-permute-start | bytes 3932168 | tf_op jit(solution)/shard_map/ppermute | solution.py:120
  23.1 14.3 %copy-start = (bf16[512,1280]{1,0:T(8,128)(2,1)}, bf16[512,1280]{1,0:T(8,128)(2,1)S(1)}, u32[]{:S(2)}) copy-start(bf16[512,1280]{1,0:T(8,128)(2,1)S(1)} %constant_dynamic-update-slice_fusion.refs_1_) | copy-start | bytes 3932164
  23.1 30.4 %collective-permute-start.3 = (bf16[512,1280]{1,0:T(8,128)(2,1)S(1)}, bf16[512,1280]{1,0:T(8,128)(2,1)S(1)}, u32[]{:S(2)}, u32[]{:S(2)}) collective-permute-start(bf16[512,1280]{1,0:T(8,128)(2,1)S(1)} %constant_dynamic-update-slice_fusion.refs_1_), channel_id=1, source_target_pairs={{0,96},{1,33},{2,98},{3,35},{4,100},{5,37},{6,102},{7,39},{8,104},... | collective-permute-start | bytes 3932168 | tf_op jit(solution)/shard_map/ppermute | solution.py:120
  23.8 29.7 %collective-permute-start.5 = (bf16[512,1280]{1,0:T(8,128)(2,1)S(1)}, bf16[512,1280]{1,0:T(8,128)(2,1)S(1)}, u32[]{:S(2)}, u32[]{:S(2)}) collective-permute-start(bf16[512,1280]{1,0:T(8,128)(2,1)S(1)} %constant_dynamic-update-slice_fusion.refs_1_), channel_id=1, source_target_pairs={{0,8},{1,9},{2,10},{3,11},{4,12},{5,13},{6,14},{7,15},{8,0},{9,1},... | collective-permute-start | bytes 3932168 | tf_op jit(solution)/shard_map/ppermute | solution.py:120
  25.4 30.3 %collective-permute-start.6 = (bf16[512,1280]{1,0:T(8,128)(2,1)}, bf16[512,1280]{1,0:T(8,128)(2,1)}, u32[]{:S(2)}, u32[]{:S(2)}) collective-permute-start(bf16[512,1280]{1,0:T(8,128)(2,1)} %get-tuple-element.124.refs_6_.refs_7_), channel_id=1, source_target_pairs={{0,24},{1,25},{2,26},{3,27},{4,28},{5,29},{6,30},{7,31},{8,16},{9,... | collective-permute-start | bytes 3932168 | tf_op jit(solution)/shard_map/ppermute | solution.py:120
  27.6 28.1 %collective-permute-start.7 = (bf16[512,1280]{1,0:T(8,128)(2,1)}, bf16[512,1280]{1,0:T(8,128)(2,1)}, u32[]{:S(2)}, u32[]{:S(2)}) collective-permute-start(bf16[512,1280]{1,0:T(8,128)(2,1)} %get-tuple-element.124.refs_6_.refs_7_), channel_id=1, source_target_pairs={{0,1},{1,0},{2,3},{3,2},{4,5},{5,4},{6,7},{7,6},{8,9},{9,8},{10,11... | collective-permute-start | bytes 3932168 | tf_op jit(solution)/shard_map/ppermute | solution.py:120
  39.4 22.6 %copy-start.3 = (bf16[512,1280]{1,0:T(8,128)(2,1)}, bf16[512,1280]{1,0:T(8,128)(2,1)S(1)}, u32[]{:S(2)}) copy-start(bf16[512,1280]{1,0:T(8,128)(2,1)S(1)} %collective-permute-done.4.refs_5_) | copy-start | bytes 3932164
  53.5 8.6 %copy-start.4 = (bf16[512,1280]{1,0:T(8,128)(2,1)}, bf16[512,1280]{1,0:T(8,128)(2,1)S(1)}, u32[]{:S(2)}) copy-start(bf16[512,1280]{1,0:T(8,128)(2,1)S(1)} %collective-permute-done.3.refs_4_) | copy-start | bytes 3932164
  53.5 21.9 %copy-start.5 = (bf16[512,1280]{1,0:T(8,128)(2,1)}, bf16[512,1280]{1,0:T(8,128)(2,1)S(1)}, u32[]{:S(2)}) copy-start(bf16[512,1280]{1,0:T(8,128)(2,1)S(1)} %collective-permute-done.5.refs_1_.refs_8_) | copy-start | bytes 3932164
  55.7 38.1 %copy-start.24 = (s32[2]{0:T(128)S(1)}, s32[2]{0:T(128)}, u32[]{:S(2)}) copy-start(s32[2]{0:T(128)} %len_ref.3) | copy-start | bytes 28
  55.7 39.5 %copy-start.20 = (f32[2,64,128]{2,1,0:T(8,128)S(1)}, f32[2,64,128]{2,1,0:T(8,128)}, u32[]{:S(2)}) copy-start(f32[2,64,128]{2,1,0:T(8,128)} %get-tuple-element.130) | copy-start | bytes 196612
  55.7 39.5 %copy-start.21 = (f32[2,64,128]{2,1,0:T(8,128)S(1)}, f32[2,64,128]{2,1,0:T(8,128)}, u32[]{:S(2)}) copy-start(f32[2,64,128]{2,1,0:T(8,128)} %get-tuple-element.131) | copy-start | bytes 196612
  55.7 4.2 %collective-permute-start.12 = (bf16[512,1280]{1,0:T(8,128)(2,1)}, bf16[512,1280]{1,0:T(8,128)(2,1)}, u32[]{:S(2)}, u32[]{:S(2)}) collective-permute-start(bf16[512,1280]{1,0:T(8,128)(2,1)} %collective-permute-done.6.refs_10_.refs_5_), channel_id=1, source_target_pairs={{0,1},{1,0},{2,3},{3,2},{4,5},{5,4},{6,7},{7,6},{8,9},{9,8},{10,11... | collective-permute-start | bytes 3932168 | tf_op jit(solution)/shard_map/ppermute | solution.py:120
  55.8 6.3 %collective-permute-start.13 = (bf16[512,1280]{1,0:T(8,128)(2,1)}, bf16[512,1280]{1,0:T(8,128)(2,1)}, u32[]{:S(2)}, u32[]{:S(2)}) collective-permute-start(bf16[512,1280]{1,0:T(8,128)(2,1)} %get-tuple-element.126.refs_8_.refs_9_), channel_id=1, source_target_pairs={{0,1},{1,0},{2,3},{3,2},{4,5},{5,4},{6,7},{7,6},{8,9},{9,8},{10,11... | collective-permute-start | bytes 3932168 | tf_op jit(solution)/shard_map/ppermute | solution.py:120
  56.3 32.7 %collective-permute-start.11 = (bf16[512,1280]{1,0:T(8,128)(2,1)}, bf16[512,1280]{1,0:T(8,128)(2,1)}, u32[]{:S(2)}, u32[]{:S(2)}) collective-permute-start(bf16[512,1280]{1,0:T(8,128)(2,1)} %get-tuple-element.126.refs_8_.refs_9_), channel_id=1, source_target_pairs={{0,24},{1,25},{2,26},{3,27},{4,28},{5,29},{6,30},{7,31},{8,16},{9,... | collective-permute-start | bytes 3932168 | tf_op jit(solution)/shard_map/ppermute | solution.py:120
  58.5 30.5 %collective-permute-start.10 = (bf16[512,1280]{1,0:T(8,128)(2,1)S(1)}, bf16[512,1280]{1,0:T(8,128)(2,1)S(1)}, u32[]{:S(2)}, u32[]{:S(2)}) collective-permute-start(bf16[512,1280]{1,0:T(8,128)(2,1)S(1)} %collective-permute-done.4.refs_5_), channel_id=1, source_target_pairs={{0,8},{1,9},{2,10},{3,11},{4,12},{5,13},{6,14},{7,15},{8,0},{9,1},... | collective-permute-start | bytes 3932168 | tf_op jit(solution)/shard_map/ppermute | solution.py:120
  58.5 30.7 %collective-permute-start.8 = (bf16[512,1280]{1,0:T(8,128)(2,1)S(1)}, bf16[512,1280]{1,0:T(8,128)(2,1)}, u32[]{:S(2)}, u32[]{:S(2)}) collective-permute-start(bf16[512,1280]{1,0:T(8,128)(2,1)S(1)} %collective-permute-done.5.refs_1_.refs_8_), channel_id=1, source_target_pairs={{0,32},{1,97},{2,34},{3,99},{4,36},{5,101},{6,38},{7,103},{8,40},{... | collective-permute-start | bytes 3932168 | tf_op jit(solution)/shard_map/ppermute | solution.py:120
  59.9 29.4 %collective-permute-start.9 = (bf16[512,1280]{1,0:T(8,128)(2,1)S(1)}, bf16[512,1280]{1,0:T(8,128)(2,1)}, u32[]{:S(2)}, u32[]{:S(2)}) collective-permute-start(bf16[512,1280]{1,0:T(8,128)(2,1)S(1)} %collective-permute-done.5.refs_1_.refs_8_), channel_id=1, source_target_pairs={{0,96},{1,33},{2,98},{3,35},{4,100},{5,37},{6,102},{7,39},{8,104},... | collective-permute-start | bytes 3932168 | tf_op jit(solution)/shard_map/ppermute | solution.py:120
  89.0 8.1 %copy-start.6 = (bf16[512,1280]{1,0:T(8,128)(2,1)}, bf16[512,1280]{1,0:T(8,128)(2,1)S(1)}, u32[]{:S(2)}) copy-start(bf16[512,1280]{1,0:T(8,128)(2,1)S(1)} %collective-permute-done.10.refs_4_.refs_11_) | copy-start | bytes 3932164
  89.3 21.2 %collective-permute-start.15 = (bf16[2,1536,256]{2,1,0:T(8,128)(2,1)}, bf16[2,1536,256]{2,1,0:T(8,128)(2,1)}, u32[]{:S(2)}, u32[]{:S(2)}) collective-permute-start(bf16[2,1536,256]{2,1,0:T(8,128)(2,1)} %get-tuple-element.117), channel_id=1, source_target_pairs={{0,2},{1,7},{2,0},{3,5},{4,6},{5,3},{6,4},{7,1},{8,10},{9,15},{10,... | collective-permute-start | bytes 4718600 | tf_op jit(solution)/shard_map/ppermute | solution.py:120
  91.2 19.2 %collective-permute-start.14 = (bf16[512,1280]{1,0:T(8,128)(2,1)}, bf16[512,1280]{1,0:T(8,128)(2,1)}, u32[]{:S(2)}, u32[]{:S(2)}) collective-permute-start(bf16[512,1280]{1,0:T(8,128)(2,1)} %collective-permute-done.11.refs_6_), channel_id=1, source_target_pairs={{0,1},{1,0},{2,3},{3,2},{4,5},{5,4},{6,7},{7,6},{8,9},{9,8},{10,11... | collective-permute-start | bytes 3932168 | tf_op jit(solution)/shard_map/ppermute | solution.py:120
  95.2 15.2 %copy-start.9 = (bf16[2,1536,256]{2,1,0:T(8,128)(2,1)S(1)}, bf16[2,1536,256]{2,1,0:T(8,128)(2,1)}, u32[]{:S(2)}) copy-start(bf16[2,1536,256]{2,1,0:T(8,128)(2,1)} %get-tuple-element.155) | copy-start | bytes 4718596
  95.3 15.1 %collective-permute-start.16 = (f32[136,128]{1,0:T(8,128)S(1)}, f32[136,128]{1,0:T(8,128)S(1)}, u32[]{:S(2)}, u32[]{:S(2)}) collective-permute-start(f32[136,128]{1,0:T(8,128)S(1)} %concatenate.11), channel_id=1, source_target_pairs={{0,32},{1,33},{2,34},{3,35},{4,36},{5,37},{6,38},{7,39},{8,40},{9,... | collective-permute-start | bytes 208904 | tf_op jit(solution)/shard_map/ppermute | solution.py:120
  110.4 5.1 %copy-start.23 = (bf16[2,512,256]{2,1,0:T(8,128)(2,1)S(1)}, bf16[2,512,256]{2,1,0:T(8,128)(2,1)}, u32[]{:S(2)}) copy-start(bf16[2,512,256]{2,1,0:T(8,128)(2,1)} %get-tuple-element.137) | copy-start | bytes 1572868
  111.8 19.5 %copy-start.18 = (bf16[2,512,256]{2,1,0:T(8,128)(2,1)S(1)}, bf16[2,512,256]{2,1,0:T(8,128)(2,1)}, u32[]{:S(2)}) copy-start(bf16[2,512,256]{2,1,0:T(8,128)(2,1)} %get-tuple-element.159) | copy-start | bytes 1572868
  111.8 19.2 %collective-permute-start.17 = (bf16[1536,256]{1,0:T(8,128)(2,1)S(1)}, bf16[1536,256]{1,0:T(8,128)(2,1)S(1)}, u32[]{:S(2)}, u32[]{:S(2)}) collective-permute-start(bf16[1536,256]{1,0:T(8,128)(2,1)S(1)} %fusion.6), channel_id=1, source_target_pairs={{0,6},{1,3},{2,4},{3,1},{4,2},{5,7},{6,0},{7,5},{8,14},{9,11},{10,... | collective-permute-start | bytes 2359304 | tf_op jit(solution)/shard_map/ppermute | solution.py:120
  115.5 14.5 %collective-permute-start.18 = (bf16[2,512,256]{2,1,0:T(8,128)(2,1)S(1)}, bf16[2,512,256]{2,1,0:T(8,128)(2,1)S(1)}, u32[]{:S(2)}, u32[]{:S(2)}) collective-permute-start(bf16[2,512,256]{2,1,0:T(8,128)(2,1)S(1)} %copy-done.23), channel_id=1, source_target_pairs={{0,2},{1,7},{2,0},{3,5},{4,6},{5,3},{6,4},{7,1},{8,10},{9,15},{10,... | collective-permute-start | bytes 1572872 | tf_op jit(solution)/shard_map/ppermute | solution.py:120
  115.5 13.7 %collective-permute-start.19 = (f32[136,128]{1,0:T(8,128)S(1)}, f32[136,128]{1,0:T(8,128)S(1)}, u32[]{:S(2)}, u32[]{:S(2)}) collective-permute-start(f32[136,128]{1,0:T(8,128)S(1)} %pad_add_fusion.1), channel_id=1, source_target_pairs={{0,96},{1,97},{2,98},{3,99},{4,100},{5,101},{6,102},{7,103},{8,104... | collective-permute-start | bytes 208904 | tf_op jit(solution)/shard_map/ppermute | solution.py:120
  129.2 20.2 %copy-start.22 = (bf16[2,1024,256]{2,1,0:T(8,128)(2,1)S(1)}, bf16[2,1024,256]{2,1,0:T(8,128)(2,1)}, u32[]{:S(2)}) copy-start(bf16[2,1024,256]{2,1,0:T(8,128)(2,1)} %get-tuple-element.165) | copy-start | bytes 3145732
  131.1 17.8 %collective-permute-start.21 = (bf16[2,1024,256]{2,1,0:T(8,128)(2,1)}, bf16[2,1024,256]{2,1,0:T(8,128)(2,1)S(1)}, u32[]{:S(2)}, u32[]{:S(2)}) collective-permute-start(bf16[2,1024,256]{2,1,0:T(8,128)(2,1)} %get-tuple-element.148), channel_id=1, source_target_pairs={{0,2},{1,7},{2,0},{3,5},{4,6},{5,3},{6,4},{7,1},{8,10},{9,15},{10,... | collective-permute-start | bytes 3145736 | tf_op jit(solution)/shard_map/ppermute | solution.py:120
  131.4 12.9 %collective-permute-start.20 = (bf16[512,256]{1,0:T(8,128)(2,1)S(1)}, bf16[512,256]{1,0:T(8,128)(2,1)S(1)}, u32[]{:S(2)}, u32[]{:S(2)}) collective-permute-start(bf16[512,256]{1,0:T(8,128)(2,1)S(1)} %fusion.11), channel_id=1, source_target_pairs={{0,6},{1,3},{2,4},{3,1},{4,2},{5,7},{6,0},{7,5},{8,14},{9,11},{10,... | collective-permute-start | bytes 786440 | tf_op jit(solution)/shard_map/ppermute | solution.py:120
  134.4 4.3 %collective-permute-start.22 = (f32[136,128]{1,0:T(8,128)S(1)}, f32[136,128]{1,0:T(8,128)S(1)}, u32[]{:S(2)}, u32[]{:S(2)}) collective-permute-start(f32[136,128]{1,0:T(8,128)S(1)} %add.87), channel_id=1, source_target_pairs={{0,8},{1,9},{2,10},{3,11},{4,12},{5,13},{6,14},{7,15},{8,0},{9,1},... | collective-permute-start | bytes 208904 | tf_op jit(solution)/shard_map/ppermute | solution.py:120
  138.7 5.6 %collective-permute-start.23 = (f32[136,128]{1,0:T(8,128)S(1)}, f32[136,128]{1,0:T(8,128)S(1)}, u32[]{:S(2)}, u32[]{:S(2)}) collective-permute-start(f32[136,128]{1,0:T(8,128)S(1)} %add.89), channel_id=1, source_target_pairs={{0,24},{1,25},{2,26},{3,27},{4,28},{5,29},{6,30},{7,31},{8,16},{9,... | collective-permute-start | bytes 208904 | tf_op jit(solution)/shard_map/ppermute | solution.py:120
  149.4 19.8 %collective-permute-start.28 = (bf16[2,1024,256]{2,1,0:T(8,128)(2,1)S(1)}, bf16[2,1024,256]{2,1,0:T(8,128)(2,1)S(1)}, u32[]{:S(2)}, u32[]{:S(2)}) collective-permute-start(bf16[2,1024,256]{2,1,0:T(8,128)(2,1)S(1)} %copy-done.22), channel_id=1, source_target_pairs={{0,2},{1,7},{2,0},{3,5},{4,6},{5,3},{6,4},{7,1},{8,10},{9,15},{10,... | collective-permute-start | bytes 3145736 | tf_op jit(solution)/shard_map/ppermute | solution.py:120
  152.0 4.0 %copy-start.11 = (bf16[2,1024,256]{2,1,0:T(8,128)(2,1)S(1)}, bf16[2,1024,256]{2,1,0:T(8,128)(2,1)}, u32[]{:S(2)}) copy-start(bf16[2,1024,256]{2,1,0:T(8,128)(2,1)} %get-tuple-element.172) | copy-start | bytes 3145732
  152.1 17.1 %copy-start.10 = (bf16[2,1024,256]{2,1,0:T(8,128)(2,1)S(1)}, bf16[2,1024,256]{2,1,0:T(8,128)(2,1)}, u32[]{:S(2)}) copy-start(bf16[2,1024,256]{2,1,0:T(8,128)(2,1)} %get-tuple-element.167) | copy-start | bytes 3145732
  152.1 17.0 %collective-permute-start.25 = (bf16[2,512,256]{2,1,0:T(8,128)(2,1)S(1)}, bf16[2,512,256]{2,1,0:T(8,128)(2,1)S(1)}, u32[]{:S(2)}, u32[]{:S(2)}) collective-permute-start(bf16[2,512,256]{2,1,0:T(8,128)(2,1)S(1)} %pad_maximum_fusion.1), channel_id=1, source_target_pairs={{0,24},{2,26},{4,28},{6,30},{8,16},{10,18},{12,20},{14,22},{17,9},... | collective-permute-start | bytes 1572872 | tf_op jit(solution)/shard_map/ppermute | solution.py:120
  155.3 13.9 %collective-permute-start.26 = (bf16[2,512,256]{2,1,0:T(8,128)(2,1)S(1)}, bf16[2,512,256]{2,1,0:T(8,128)(2,1)S(1)}, u32[]{:S(2)}, u32[]{:S(2)}) collective-permute-start(bf16[2,512,256]{2,1,0:T(8,128)(2,1)S(1)} %pad_maximum_fusion.1), channel_id=1, source_target_pairs={{1,24},{3,26},{5,28},{7,30},{9,16},{11,18},{13,20},{15,22},{16,9},... | collective-permute-start | bytes 1572872 | tf_op jit(solution)/shard_map/ppermute | solution.py:120
  156.1 13.0 %collective-permute-start.27 = (bf16[1024,256]{1,0:T(8,128)(2,1)S(1)}, bf16[1024,256]{1,0:T(8,128)(2,1)S(1)}, u32[]{:S(2)}, u32[]{:S(2)}) collective-permute-start(bf16[1024,256]{1,0:T(8,128)(2,1)S(1)} %fusion.7), channel_id=1, source_target_pairs={{0,6},{1,3},{2,4},{3,1},{4,2},{5,7},{6,0},{7,5},{8,14},{9,11},{10,... | collective-permute-start | bytes 1572872 | tf_op jit(solution)/shard_map/ppermute | solution.py:120
  157.2 15.5 %copy-start.8 = (bf16[1024,256]{1,0:T(8,128)(2,1)}, bf16[1024,256]{1,0:T(8,128)(2,1)S(1)}, u32[]{:S(2)}) copy-start(bf16[1024,256]{1,0:T(8,128)(2,1)S(1)} %slice.80) | copy-start | bytes 1572868
  157.2 12.0 %collective-permute-start.24 = (bf16[2,512,256]{2,1,0:T(8,128)(2,1)S(1)}, bf16[2,512,256]{2,1,0:T(8,128)(2,1)S(1)}, u32[]{:S(2)}, u32[]{:S(2)}) collective-permute-start(bf16[2,512,256]{2,1,0:T(8,128)(2,1)S(1)} %bitcast.53), channel_id=1, source_target_pairs={{0,1},{1,0},{2,3},{3,2},{4,5},{5,4},{6,7},{7,6},{8,9},{9,8},{10,11... | collective-permute-start | bytes 1572872 | tf_op jit(solution)/shard_map/ppermute | solution.py:120
  169.2 3.5 %copy-start.12 = (bf16[2,512,256]{2,1,0:T(8,128)(2,1)}, bf16[2,512,256]{2,1,0:T(8,128)(2,1)S(1)}, u32[]{:S(2)}) copy-start(bf16[2,512,256]{2,1,0:T(8,128)(2,1)S(1)} %collective-permute-done.25.same0) | copy-start | bytes 1572868
  169.2 3.5 %copy-start.13 = (bf16[2,512,256]{2,1,0:T(8,128)(2,1)}, bf16[2,512,256]{2,1,0:T(8,128)(2,1)S(1)}, u32[]{:S(2)}) copy-start(bf16[2,512,256]{2,1,0:T(8,128)(2,1)S(1)} %collective-permute-done.26.other0) | copy-start | bytes 1572868
  169.2 3.5 %copy-start.14 = (bf16[2,512,256]{2,1,0:T(8,128)(2,1)}, bf16[2,512,256]{2,1,0:T(8,128)(2,1)S(1)}, u32[]{:S(2)}) copy-start(bf16[2,512,256]{2,1,0:T(8,128)(2,1)S(1)} %collective-permute-done.24.near_in) | copy-start | bytes 1572868
  169.4 10.5 %collective-permute-start.29 = (bf16[1024,256]{1,0:T(8,128)(2,1)S(1)}, bf16[1024,256]{1,0:T(8,128)(2,1)S(1)}, u32[]{:S(2)}, u32[]{:S(2)}) collective-permute-start(bf16[1024,256]{1,0:T(8,128)(2,1)S(1)} %fusion.8), channel_id=1, source_target_pairs={{0,6},{1,3},{2,4},{3,1},{4,2},{5,7},{6,0},{7,5},{8,14},{9,11},{10,... | collective-permute-start | bytes 1572872 | tf_op jit(solution)/shard_map/ppermute | solution.py:120
  172.7 8.2 %copy-start.19 = (f32[2,64,128]{2,1,0:T(8,128)S(1)}, f32[2,64,128]{2,1,0:T(8,128)}, u32[]{:S(2)}) copy-start(f32[2,64,128]{2,1,0:T(8,128)} %pre_ref.3) | copy-start | bytes 196612
  172.7 14.7 %collective-permute-start.31 = (bf16[2,512,256]{2,1,0:T(8,128)(2,1)S(1)}, bf16[2,512,256]{2,1,0:T(8,128)(2,1)S(1)}, u32[]{:S(2)}, u32[]{:S(2)}) collective-permute-start(bf16[2,512,256]{2,1,0:T(8,128)(2,1)S(1)} %bitcast.57), channel_id=1, source_target_pairs={{0,24},{2,26},{4,28},{6,30},{8,16},{10,18},{12,20},{14,22},{17,9},... | collective-permute-start | bytes 1572872 | tf_op jit(solution)/shard_map/ppermute | solution.py:120
  175.8 11.6 %collective-permute-start.32 = (bf16[2,512,256]{2,1,0:T(8,128)(2,1)S(1)}, bf16[2,512,256]{2,1,0:T(8,128)(2,1)S(1)}, u32[]{:S(2)}, u32[]{:S(2)}) collective-permute-start(bf16[2,512,256]{2,1,0:T(8,128)(2,1)S(1)} %bitcast.58), channel_id=1, source_target_pairs={{1,24},{3,26},{5,28},{7,30},{9,16},{11,18},{13,20},{15,22},{16,9},... | collective-permute-start | bytes 1572872 | tf_op jit(solution)/shard_map/ppermute | solution.py:120
  180.1 7.3 %copy-start.7 = (bf16[1024,256]{1,0:T(8,128)(2,1)}, bf16[1024,256]{1,0:T(8,128)(2,1)S(1)}, u32[]{:S(2)}) copy-start(bf16[1024,256]{1,0:T(8,128)(2,1)S(1)} %fusion.5) | copy-start | bytes 1572868
  180.1 7.3 %collective-permute-start.30 = (bf16[2,512,256]{2,1,0:T(8,128)(2,1)S(1)}, bf16[2,512,256]{2,1,0:T(8,128)(2,1)S(1)}, u32[]{:S(2)}, u32[]{:S(2)}) collective-permute-start(bf16[2,512,256]{2,1,0:T(8,128)(2,1)S(1)} %bitcast.51), channel_id=1, source_target_pairs={{0,1},{1,0},{2,3},{3,2},{4,5},{5,4},{6,7},{7,6},{8,9},{9,8},{10,11... | collective-permute-start | bytes 1572872 | tf_op jit(solution)/shard_map/ppermute | solution.py:120
  187.4 0.8 copy-start.15
  187.4 1.0 copy-start.16
  188.4 0.8 copy-start.17
